TPU v7x, 128 devices: a whole 4x4x4 slice. The times are simulated.
128 devices in a mesh: seq: 32 (over x, z, y_lo), head: 4 (over y_hi, core).
Axes of the slice: x: 4, y: 4 (y_hi: 2, y_lo: 2; y = y_hi * 2 + y_lo), z: 4, core: 2. Of those that a mesh axis runs over, the one named last changes fastest.
Arguments:
- tokens_in: bfloat16 [1024, 32, 6144], P('seq', None, 'head'), may hold values from -6 to 6
- gate_rows: bfloat16 [1024, 32, 6144], P('seq', None, 'head'), may hold values from -28 to 28
- gate_cols: bfloat16 [1024, 32, 6144], P(None, 'seq', 'head'), may hold values from -28 to 28
- write_rows: bfloat16 [64, 32768], P(None, 'seq'), may hold values from -6 to 6
- read_rows: bfloat16 [64, 32768], P(None, 'seq'), may hold values from -0.75 to 0.75
- step_rows: float32 [48, 32768], P('head', 'seq'), may hold values from 0 to 2, as said below
- decay_rows: float32 [48, 32768], P('head', 'seq'), may hold values from -1 to 0, as said below
- skip_rows: float32 [48], P('head'), may hold values from 0.5 to 2
- norm_rows: float32 [6144], P('head'), may hold values from 0.5 to 1.5
- write_cols: bfloat16 [64, 32768], P(None, 'seq'), may hold values from -6 to 6
- read_cols: bfloat16 [64, 32768], P(None, 'seq'), may hold values from -0.75 to 0.75
- step_cols: float32 [48, 32768], P('head', 'seq'), may hold values from 0 to 2, as said below
- decay_cols: float32 [48, 32768], P('head', 'seq'), may hold values from -1 to 0, as said below
- skip_cols: float32 [48], P('head'), may hold values from 0.5 to 2
- norm_cols: float32 [6144], P('head'), may hold values from 0.5 to 1.5
Outputs:
- mixed_cols: bfloat16 [1024, 32, 6144], P(None, 'seq', 'head')
Inputs may be any that keep to these rules, and one draw needn't show every extreme that they name: `step_rows`: positive. `step_cols`: positive. `decay_rows`: never positive. `decay_cols`: never positive.
All inputs are finite; a program needn't handle non-finite values.
Results may differ from a plain program's by a relative error of at most 0.0063.
Values may be sent and summed in bfloat16 or wider, within the bound.
No kernel may reach another device: no remote copies, remote signals or barrier semaphores. Data moves between devices by JAX's collectives and lax.ppermute only.
A program may use at most 128 MiB of HBM per device.

v0:
```python
import jax
import jax.numpy as jnp
from jax import lax
from jax.sharding import Mesh
from jax.sharding import PartitionSpec as P

BLOCK = 256
SEQ = ("seq_0", "seq_1", "seq_2")


EPSILON = 1e-05
HIGHEST = lax.Precision.HIGHEST


def neutral_like(array, identity):
    return jax.tree.map(
        lambda part, zero: jnp.zeros_like(part) + jnp.asarray(zero, part.dtype), array, identity
    )


def entering(array, axes, combine, identity):
    before = start = neutral_like(array, identity)
    subtotal = array
    for axis in reversed(axes):
        devices, here = (lax.axis_size(axis), lax.axis_index(axis))
        pieces = jax.tree.map(lambda part: lax.all_gather(part, axis), subtotal)
        inside, subtotal = (start, start)
        for k in range(devices):
            passed = k < here
            subtotal = combine(subtotal, jax.tree.map(lambda part: part[k], pieces))
            inside = jax.tree.map(lambda new, old: jnp.where(passed, new, old), subtotal, inside)
        before = combine(inside, before)
    return before


def from_everyone(array, axis):
    copies = jnp.broadcast_to(array, (lax.axis_size(axis), *array.shape))
    return lax.all_to_all(copies, axis, split_axis=0, concat_axis=0, tiled=True)


def of_everyone(array, axis):
    return from_everyone(array, axis).sum(axis=0)


def carried_state(device_total, end_state):

    def combine(earlier, latter):
        return (earlier[0] + latter[0], jnp.exp(latter[0])[:, None, None] * earlier[1] + latter[1])

    identity = (jnp.zeros_like(device_total), jnp.zeros_like(end_state))
    prefix = entering((device_total, end_state), SEQ, combine, identity)
    return prefix[1]


def ssd_layer(inputs, write_mat, read_mat, step_mat, decay_mat, skip_vec, gain_vec, gate_mat):
    length = inputs.shape[1]
    head_count = inputs.shape[3]
    head_width = inputs.shape[4]
    state_size = write_mat.shape[0]
    col_count = write_mat.shape[1]
    block_count = write_mat.shape[2]
    rows_iota = lax.broadcasted_iota(jnp.int32, (length, length), 0)
    cols_iota = lax.broadcasted_iota(jnp.int32, (length, length), 1)
    upper_ones = (rows_iota <= cols_iota).astype(jnp.float32)
    causal = rows_iota >= cols_iota
    cumulative = jnp.einsum("hcqs,st->hcqt", decay_mat, upper_ones, precision=HIGHEST)
    scores = jnp.einsum("ncqt,ncqs->cqts", read_mat, write_mat, preferred_element_type=jnp.float32)
    spread = cumulative[..., :, None] - cumulative[..., None, :]
    fading = jnp.where(causal, jnp.exp(jnp.where(causal, spread, 0.0)), 0.0)
    mixing = (fading * scores[None] * step_mat[..., None, :]).astype(jnp.bfloat16)
    inner_part = jnp.einsum(
        "hcqts,qschp->qtchp", mixing, inputs, preferred_element_type=jnp.float32
    )
    finals = cumulative[..., -1:]
    tail_weights = jnp.exp(finals - cumulative) * step_mat
    loaded = (write_mat[None] * tail_weights[:, None]).astype(jnp.bfloat16)
    block_states = jnp.einsum(
        "hncqs,qschp->cqhnp", loaded, inputs, preferred_element_type=jnp.float32
    )
    total_blocks = col_count * block_count
    flat_states = block_states.reshape(total_blocks, head_count, state_size, head_width)
    flat_totals = jnp.transpose(finals[..., 0], (1, 2, 0)).reshape(total_blocks, head_count)

    def advance(running, block_item):
        state_now, decay_sum = running
        block_total, block_state = block_item
        moved = (
            jnp.exp(block_total)[:, None, None] * state_now + block_state,
            decay_sum + block_total,
        )
        return (moved, (state_now, decay_sum))

    zero_state = jnp.zeros((head_count, state_size, head_width), jnp.float32)
    zero_total = jnp.zeros((head_count,), jnp.float32)
    scanned = lax.scan(advance, (zero_state, zero_total), (flat_totals, flat_states))
    end_state, device_total = scanned[0]
    incoming, before = scanned[1]
    prior_state = carried_state(device_total, end_state)
    incoming = incoming + jnp.exp(before)[:, :, None, None] * prior_state[None]
    incoming = incoming.reshape(col_count, block_count, head_count, state_size, head_width)
    from_state = jnp.einsum(
        "ncqt,cqhnp->qtchp", read_mat.astype(jnp.float32), incoming, precision=HIGHEST
    )
    lifting = jnp.transpose(jnp.exp(cumulative), (2, 3, 1, 0))[..., None]
    outputs = inner_part + from_state * lifting + skip_vec[:, None] * inputs
    features = gate_mat.shape[-1]
    gated = outputs.reshape(block_count, length, col_count, features) * jax.nn.silu(
        gate_mat.astype(jnp.float32)
    )
    squares = of_everyone(jnp.sum(gated * gated, axis=-1), "head")
    scaled = lax.rsqrt(squares / (features * lax.axis_size("head")) + EPSILON)
    return (gated * scaled[..., None] * gain_vec).astype(jnp.bfloat16)


def body(
    tokens_in,
    gate_rows,
    gate_cols,
    write_rows,
    read_rows,
    step_rows,
    decay_rows,
    skip_rows,
    norm_rows,
    write_cols,
    read_cols,
    step_cols,
    decay_cols,
    skip_cols,
    norm_cols,
):
    grid_rows = tokens_in.shape[0]
    grid_cols = tokens_in.shape[1]
    features = tokens_in.shape[2]
    head_count = step_rows.shape[0]
    head_width = features // head_count
    state_size = write_rows.shape[0]
    tokens = grid_rows * grid_cols
    first_blocks = tokens // BLOCK
    first_out = ssd_layer(
        tokens_in.reshape(first_blocks, BLOCK, 1, head_count, head_width),
        write_rows.reshape(state_size, 1, first_blocks, BLOCK),
        read_rows.reshape(state_size, 1, first_blocks, BLOCK),
        step_rows.reshape(head_count, 1, first_blocks, BLOCK),
        decay_rows.reshape(head_count, 1, first_blocks, BLOCK),
        skip_rows,
        norm_rows,
        gate_rows.reshape(first_blocks, BLOCK, 1, features),
    )
    hidden = lax.all_to_all(
        first_out.reshape(grid_rows, grid_cols, features),
        SEQ,
        split_axis=1,
        concat_axis=0,
        tiled=True,
    )
    column_len = hidden.shape[0]
    local_cols = hidden.shape[1]
    col_blocks = column_len // BLOCK
    second_out = ssd_layer(
        hidden.reshape(col_blocks, BLOCK, local_cols, head_count, head_width),
        write_cols.reshape(state_size, local_cols, col_blocks, BLOCK),
        read_cols.reshape(state_size, local_cols, col_blocks, BLOCK),
        step_cols.reshape(head_count, local_cols, col_blocks, BLOCK),
        decay_cols.reshape(head_count, local_cols, col_blocks, BLOCK),
        skip_cols,
        norm_cols,
        gate_cols.reshape(col_blocks, BLOCK, local_cols, features),
    )
    return second_out.reshape(column_len, local_cols, features)


def solution(mesh):
    torus = Mesh(
        mesh.devices.reshape(4, 4, 2, mesh.shape["head"]), ("seq_0", "seq_1", "seq_2", "head")
    )
    return jax.shard_map(
        body,
        mesh=torus,
        in_specs=(
            P(SEQ, None, "head"),
            P(SEQ, None, "head"),
            P(None, SEQ, "head"),
            P(None, SEQ),
            P(None, SEQ),
            P("head", SEQ),
            P("head", SEQ),
            P("head"),
            P("head"),
            P(None, SEQ),
            P(None, SEQ),
            P("head", SEQ),
            P("head", SEQ),
            P("head"),
            P("head"),
        ),
        out_specs=P(None, SEQ, "head"),
        check_vma=False,
    )
```

profile of v0, /device:TPU:1, one launch (start us, length us, event | category | flops | bytes accessed | tf_op | source)
XLA Modules:
  0.0 403.8 jit_solution(12692612234289655752)
XLA Ops:
  8.7 6.9 %reshape.656 = bf16[4,256,12,128]{3,2,1,0:T(8,128)(2,1)} reshape(bf16[32,32,1536]{2,1,0:T(8,128)(2,1)} %param.19) | data formatting | bytes 6291456 | tf_op jit(solution)/shard_map/reshape.13
  16.4 4.4 %fusion.30 = f32[4,12,64,128]{3,2,1,0:T(8,128)} fusion(bf16[4,256,12,128]{3,2,1,0:T(8,128)(2,1)} %reshape.656, f32[12,4,256]{2,0,1:T(8,128)S(1)} %get-tuple-element.183, f32[64,4,256]{2,0,1:T(8,128)S(1)} %copy.56), kind=kOutput, calls=%fused_computation.48 | convolution fusion | flops 202899456 | bytes 5029888 | tf_op jit(solution)/shard_map/hncqs,qschp->cqhnp/dot_general | solution.py:77
  20.8 1.3 broadcast.421.clone
  22.2 8.1 %while.34 = (s32[]{:T(128)}, f32[12,64,128]{2,1,0:T(8,128)S(1)}, f32[12]{0:T(128)S(1)}, f32[4,12,64,128]{3,2,1,0:T(8,128)}, f32[4,12]{1,0:T(4,128)S(1)}, /*index...) while((s32[]{:T(128)}, f32[12,64,128]{2,1,0:T(8,128)S(1)}, ...), condition=%wide.region_1.2_spmd.clone, body=%wide.region_0.1_spmd.clone.sunk | while | flops 393243 | bytes 1967093 | solution.py:95
  23.0 1.4 bitcast_add_fusion.4
  25.2 1.1 bitcast_add_fusion.4
  27.1 1.1 bitcast_add_fusion.4
  29.1 1.1 bitcast_add_fusion.4
  30.2 1.3 dynamic-slice
  32.5 4.4 %all-reduce = f32[24]{0:T(128)S(1)} all-reduce(f32[24]{0:T(128)S(1)} %dynamic-update-slice), channel_id=2, replica_groups=mesh['seq_0'=4,'seq_1'=4,'seq_2'=2,'head'=4] {'seq_2'}, use_global_device_ids=true, to_apply=%add | all-reduce | flops 24 | bytes 192
  36.9 1.3 dynamic-slice.1
  38.8 9.4 %all-gather.1 = f32[24,64,128]{2,1,0:T(8,128)S(1)} all-gather(f32[12,64,128]{2,1,0:T(8,128)S(1)} %get-tuple-element.88), channel_id=3, replica_groups=mesh['seq_0'=4,'seq_1'=4,'seq_2'=2,'head'=4] {'seq_2'}, dimensions={0}, use_global_device_ids=true | all-gather | bytes 1179648 | tf_op jit(solution)/shard_map/all_gather | solution.py:26
  50.2 10.0 %all-reduce.1 = f32[48]{0:T(128)S(1)} all-reduce(f32[48]{0:T(128)S(1)} %get-tuple-element.208), channel_id=6, replica_groups=mesh['seq_0'=4,'seq_1'=4,'seq_2'=2,'head'=4] {'seq_1'}, use_global_device_ids=true, to_apply=%add.1 | all-reduce | flops 48 | bytes 384
  61.4 20.3 %all-gather.13.cloned.1.call-done = f32[4,12,64,128]{3,2,1,0:T(8,128)} async-done(((f32[1,12,64,128]{3,2,1,0:T(8,128)}), f32[4,12,64,128]{3,2,1,0:T(8,128)}) %all-gather.13.cloned.1.call-update) | async-done | bytes 1572880 | tf_op jit(solution)/shard_map/all_gather | solution.py:26
  81.7 2.3 slice_add_fusion.12
  84.1 4.3 %reshape.667 = f32[4,256,1,12,128]{4,3,1,0,2:T(8,128)} reshape(bf16[32,32,1536]{2,1,0:T(8,128)(2,1)S(1)} %copy-done.1) | data formatting | bytes 9437184 | tf_op jit(solution)/shard_map/convert_element_type | solution.py:105
  89.5 9.3 %copy.60 = f32[4,256,1,12,128]{1,4,3,0,2:T(8,128)} copy(f32[4,256,1,12,128]{4,3,1,0,2:T(8,128)} %reshape.667) | data formatting | bytes 12582912 | tf_op jit(solution)/shard_map/convert_element_type | solution.py:105
  98.9 4.3 %reshape.668 = f32[4,256,1,12,128]{4,3,1,0,2:T(8,128)} reshape(bf16[32,32,1536]{2,1,0:T(8,128)(2,1)S(1)} %copy-done.2) | data formatting | bytes 9437184 | tf_op jit(solution)/shard_map/convert_element_type | solution.py:108
  103.2 9.3 %copy.63 = f32[4,256,1,12,128]{1,4,3,0,2:T(8,128)} copy(f32[4,256,1,12,128]{4,3,1,0,2:T(8,128)} %reshape.668) | data formatting | bytes 12582912 | tf_op jit(solution)/shard_map/convert_element_type | solution.py:108
  113.2 8.1 %all-gather.6 = f32[4,1,12]{2,1,0:T(1,128)S(1)} all-gather(f32[1,1,12]{2,1,0:T(1,128)S(1)} %copy-done.38), channel_id=1, replica_groups=mesh['seq_0'=4,'seq_1'=4,'seq_2'=2,'head'=4] {'seq_0'}, dimensions={0}, use_global_device_ids=true | all-gather | bytes 240 | tf_op jit(solution)/shard_map/all_gather | solution.py:26
  122.4 9.4 %fusion.8 = f32[4,12,256,128]{2,3,1,0:T(8,128)} fusion(f32[12,4,256]{2,0,1:T(8,128)S(1)} %copy-done.19, f32[4,256,256]{2,1,0:T(8,128)S(1)} %fusion.66, f32[12,4,256]{2,0,1:T(8,128)S(1)} %bitcast.213, pred[256,256]{1,0:T(8,128)(4,1)S(1)} %iota_compare_fusion.1, bf16[4,256,12,128]{3,2,1,0:T(8,128)(2,1)} %reshape.656), kind=kOutput, calls=%fused_computation.18 | convolution fusion | flops 824180736 | bytes 10649600 | tf_op jit(solution)/shard_map/hcqts,qschp->qtchp/dot_general | solution.py:71
  131.9 2.9 fusion.53
  134.9 12.7 %multiply_reduce_fusion.1 = (f32[4,256]{1,0:T(4,128)S(1)}, f32[4,256,1,12,128]{1,4,3,0,2:T(8,128)}) fusion(f32[4,256,1,12,128]{1,4,3,0,2:T(8,128)} %copy.63, f32[4,256,1,12,128]{1,4,3,0,2:T(8,128)} %copy.60, f32[12]{0:T(128)S(1)} %copy-done.41, f32[4,256,12]{1,2,0:T(8,128)S(1)} %copy-done.18, bf16[64,4,256,1]{2,1,0,3:T(4,128)(2,1)S(1)} %bitcast.217, ...), kind=kOutput, calls=%fused_computation.33 | convolution fusion | flops 1226046464 | bytes 27316464 | tf_op jit(solution)/shard_map/ncqt,cqhnp->qtchp/dot_general | solution.py:101
  148.2 7.0 %all-to-all-start = ((f32[4,4,256,1]{2,1,3,0:T(4,128)}), f32[4,4,256,1]{2,1,3,0:T(4,128)S(1)}, u32[]{:S(2)}, u32[]{:S(2)}) async-start(f32[4,4,256,1]{2,1,3,0:T(4,128)} %broadcast_in_dim.42), calls=%async_computation | async-start | bytes 32768 | tf_op jit(solution)/shard_map/all_to_all | solution.py:38
  155.2 9.4 %copy.61 = f32[4,256,1,12,128]{4,3,1,0,2:T(8,128)} copy(f32[4,256,1,12,128]{1,4,3,0,2:T(8,128)} %get-tuple-element.212) | data formatting | bytes 12582912 | tf_op jit(solution)/shard_map/add | solution.py:105
  164.6 8.7 %reshape.658 = f32[32,32,1536]{2,1,0:T(8,128)} reshape(f32[4,256,1,12,128]{4,3,1,0,2:T(8,128)} %copy.61) | data formatting | bytes 12582912 | tf_op jit(solution)/shard_map/reshape | solution.py:107
  173.4 4.5 %multiply_convert_fusion.5 = bf16[32,32,1536]{2,1,0:T(8,128)(2,1)S(1)} fusion(f32[32,32,1536]{2,1,0:T(8,128)} %reshape.658, f32[1536]{0:T(1024)S(1)} %copy-done.23, f32[32,32]{1,0:T(8,128)S(1)} %rsqrt.25, bf16[32,32,1536]{2,1,0:T(8,128)(2,1)S(1)} %copy-done.2), kind=kLoop, calls=%fused_computation.32 | loop fusion | flops 14155776 | bytes 12593152 | tf_op jit(solution)/shard_map/convert_element_type | solution.py:112
  177.8 3.4 copy.64
  181.2 4.2 %all-to-all-start.1 = ((bf16[32,32,1536]{2,0,1:T(8,128)(2,1)}), bf16[32,32,1536]{2,0,1:T(8,128)(2,1)S(1)}, u32[]{:S(2)}, u32[]{:S(2)}) async-start(bf16[32,32,1536]{2,0,1:T(8,128)(2,1)} %copy.64), calls=%async_computation.1 | async-start | bytes 6291456 | tf_op jit(solution)/shard_map/all_to_all | solution.py:150
  185.5 1.5 reshape.660
  187.0 1.5 mul.593
  188.5 1.6 reshape.662
  190.2 1.6 copy.70
  191.8 1.0 fusion.57
  193.4 1.5 exponential_multiply_fusion
  195.0 33.9 %all-to-all-done.1 = bf16[32,32,1536]{2,0,1:T(8,128)(2,1)S(1)} async-done(((bf16[32,32,1536]{2,0,1:T(8,128)(2,1)}), bf16[32,32,1536]{2,0,1:T(8,128)(2,1)S(1)}, u32[]{:S(2)}, u32[]{:S(2)}) %all-to-all-start.1) | async-done | bytes 3145760 | tf_op jit(solution)/shard_map/all_to_all | solution.py:150
  228.8 3.7 reshape.659
  232.5 4.5 %fusion.27 = f32[4,12,64,128]{3,2,1,0:T(8,128)} fusion(bf16[4,256,12,128]{3,2,1,0:T(8,128)(2,1)} %reshape.659, f32[12,4,256]{2,0,1:T(8,128)} %get-tuple-element.181, f32[64,4,256]{2,0,1:T(8,128)} %copy.70), kind=kOutput, calls=%fused_computation.45 | convolution fusion | flops 202899456 | bytes 5029888 | tf_op jit(solution)/shard_map/hncqs,qschp->cqhnp/dot_general | solution.py:77
  237.0 1.4 broadcast.421
  238.5 7.9 %while.35 = (s32[]{:T(128)}, f32[12,64,128]{2,1,0:T(8,128)S(1)}, f32[12]{0:T(128)S(1)}, f32[4,12,64,128]{3,2,1,0:T(8,128)}, f32[4,12]{1,0:T(4,128)S(1)}, /*index...) while((s32[]{:T(128)}, f32[12,64,128]{2,1,0:T(8,128)S(1)}, ...), condition=%wide.region_5.6_spmd.clone, body=%wide.region_4.5_spmd.clone.sunk | while | flops 393243 | bytes 1967093 | solution.py:95
  239.3 1.1 bitcast_add_fusion.5
  241.3 1.1 bitcast_add_fusion.5
  243.3 1.1 bitcast_add_fusion.5
  245.3 1.1 bitcast_add_fusion.5
  246.7 3.8 all-reduce.2
  250.4 9.0 %all-gather.3 = f32[24,64,128]{2,1,0:T(8,128)S(1)} all-gather(f32[12,64,128]{2,1,0:T(8,128)S(1)} %get-tuple-element.92), channel_id=5, replica_groups=mesh['seq_0'=4,'seq_1'=4,'seq_2'=2,'head'=4] {'seq_2'}, dimensions={0}, use_global_device_ids=true | all-gather | bytes 1179648 | tf_op jit(solution)/shard_map/all_gather | solution.py:26
  261.2 12.1 %all-reduce.3 = f32[48]{0:T(128)S(1)} all-reduce(f32[48]{0:T(128)S(1)} %get-tuple-element.200), channel_id=7, replica_groups=mesh['seq_0'=4,'seq_1'=4,'seq_2'=2,'head'=4] {'seq_1'}, use_global_device_ids=true, to_apply=%add.3 | all-reduce | flops 48 | bytes 384
  274.0 16.0 %all-gather.17.cloned.1.call-done = f32[4,12,64,128]{3,2,1,0:T(8,128)} async-done(((f32[1,12,64,128]{3,2,1,0:T(8,128)}), f32[4,12,64,128]{3,2,1,0:T(8,128)}) %all-gather.17.cloned.1.call-update) | async-done | bytes 1572880 | tf_op jit(solution)/shard_map/all_gather | solution.py:26
  289.9 2.3 slice_add_fusion.4
  292.3 4.6 %copy.76 = bf16[1024,1,1536]{0,2,1:T(8,128)(2,1)} copy(bf16[1024,1,1536]{2,0,1:T(8,128)(2,1)} %param.21) | data formatting | bytes 6291456 | tf_op args[2]
  296.9 7.0 %reshape.672 = f32[4,256,1,12,128]{1,0,4,3,2:T(4,128)} reshape(bf16[1024,1,1536]{0,2,1:T(8,128)(2,1)} %copy.76) | data formatting | bytes 9437184 | tf_op jit(solution)/shard_map/convert_element_type | solution.py:108
  304.6 1.3 fusion.61
  306.5 3.5 bitcast_convert_fusion
  310.0 8.4 %reshape.671 = f32[4,256,1,12,128]{4,3,1,0,2:T(8,128)} reshape(f32[32,32,1,1536]{3,1,0,2:T(8,128)} %bitcast_convert_fusion) | data formatting | bytes 12582912 | tf_op jit(solution)/shard_map/convert_element_type | solution.py:105
  318.4 9.3 %copy.74 = f32[4,256,1,12,128]{1,4,3,0,2:T(8,128)} copy(f32[4,256,1,12,128]{4,3,1,0,2:T(8,128)} %reshape.671) | data formatting | bytes 12582912 | tf_op jit(solution)/shard_map/convert_element_type | solution.py:105
  328.3 7.7 %all-gather.7 = f32[4,1,12]{2,1,0:T(1,128)S(1)} all-gather(f32[1,1,12]{2,1,0:T(1,128)S(1)} %get-tuple-element.195), channel_id=1, replica_groups=mesh['seq_0'=4,'seq_1'=4,'seq_2'=2,'head'=4] {'seq_0'}, dimensions={0}, use_global_device_ids=true | all-gather | bytes 240 | tf_op jit(solution)/shard_map/all_gather | solution.py:26
  336.7 9.3 %fusion.9 = f32[4,12,128,256]{3,2,1,0:T(8,128)} fusion(f32[12,4,256]{2,0,1:T(8,128)} %get-tuple-element.185, f32[4,256,256]{2,1,0:T(8,128)S(1)} %copy-done.7, f32[12,4,256]{2,0,1:T(8,128)S(1)} %bitcast.215, pred[256,256]{1,0:T(8,128)(4,1)} %copy-done.21, bf16[4,256,12,128]{3,2,1,0:T(8,128)(2,1)} %reshape.659), kind=kOutput, calls=%fused_computation.19 | convolution fusion | flops 824180736 | bytes 10649600 | tf_op jit(solution)/shard_map/hcqts,qschp->qtchp/dot_general | solution.py:71
  346.0 2.3 fusion.47
  348.3 12.6 %multiply_reduce_fusion = (f32[4,256]{1,0:T(4,128)S(1)}, f32[4,256,1,12,128]{1,4,3,0,2:T(8,128)}) fusion(f32[4,256,1,12,128]{1,0,4,3,2:T(4,128)} %reshape.672, f32[4,256,1,12,128]{1,4,3,0,2:T(8,128)} %copy.74, f32[12]{0:T(128)} %param.32, f32[4,256,12]{1,2,0:T(8,128)S(1)} %copy-done.20, bf16[64,4,256,1]{2,1,0,3:T(4,128)(2,1)} %bitcast.216, ...), kind=kOutput, calls=%fused_computation.27 | convolution fusion | flops 1226046464 | bytes 27316464 | tf_op jit(solution)/shard_map/ncqt,cqhnp->qtchp/dot_general | solution.py:101
  361.5 7.2 %all-to-all-start.2 = ((f32[4,4,256,1]{2,1,3,0:T(4,128)}), f32[4,4,256,1]{2,1,3,0:T(4,128)S(1)}, u32[]{:S(2)}, u32[]{:S(2)}) async-start(f32[4,4,256,1]{2,1,3,0:T(4,128)} %broadcast_in_dim.43), calls=%async_computation.2 | async-start | bytes 32768 | tf_op jit(solution)/shard_map/all_to_all | solution.py:38
  368.7 9.5 %copy.75 = f32[4,256,1,12,128]{1,0,4,3,2:T(4,128)} copy(f32[4,256,1,12,128]{1,4,3,0,2:T(8,128)} %get-tuple-element.214) | data formatting | bytes 12582912 | tf_op jit(solution)/shard_map/add | solution.py:105
  378.2 8.4 %reshape.664 = f32[1024,1,1536]{0,2,1:T(8,128)} reshape(f32[4,256,1,12,128]{1,0,4,3,2:T(4,128)} %copy.75) | data formatting | bytes 12582912 | tf_op jit(solution)/shard_map/reshape | solution.py:107
  386.7 5.6 %multiply_convert_fusion.4 = bf16[1024,1,1536]{0,2,1:T(8,128)(2,1)} fusion(f32[1024,1,1536]{0,2,1:T(8,128)} %reshape.664, f32[1536]{0:T(1024)S(1)} %copy-done.22, f32[1024]{0:T(1024)S(1)} %bitcast.220, bf16[1024,1,1536]{0,2,1:T(8,128)(2,1)S(1)} %copy-done), kind=kLoop, calls=%fused_computation.26 | loop fusion | flops 14155776 | bytes 12593152 | tf_op jit(solution)/shard_map/convert_element_type | solution.py:112
  392.3 4.6 %copy.79 = bf16[1024,1,1536]{2,0,1:T(8,128)(2,1)} copy(bf16[1024,1,1536]{0,2,1:T(8,128)(2,1)} %multiply_convert_fusion.4) | data formatting | bytes 6291456 | tf_op jit(solution)/shard_map/convert_element_type | solution.py:112
  (166 shorter events, 23.4 us)
Async XLA Ops:
  6.5 9.1 %copy-start.9 = (bf16[64,1024]{1,0:T(8,128)(2,1)S(1)}, bf16[64,1024]{1,0:T(8,128)(2,1)}, u32[]{:S(2)}) copy-start(bf16[64,1024]{1,0:T(8,128)(2,1)} %param.22) | copy-start | bytes 393220
  6.5 75.1 %all-gather.13.cloned.1.call-start = ((), (), s32[]{:S(2)}) async-start(), calls=%async_computation.3 | async-start | bytes 1966080 | tf_op jit(solution)/shard_map/all_gather | solution.py:26
  7.7 13.2 %copy-start.13 = (f32[256,12,4]{0,1,2:T(8,128)}, f32[256,12,4]{0,1,2:T(8,128)S(1)}, u32[]{:S(2)}) copy-start(f32[256,12,4]{0,1,2:T(8,128)S(1)} %fusion.59) | copy-start | bytes 147460
  22.2 61.9 %copy-start.1 = (bf16[32,32,1536]{2,1,0:T(8,128)(2,1)S(1)}, bf16[32,32,1536]{2,1,0:T(8,128)(2,1)}, u32[]{:S(2)}) copy-start(bf16[32,32,1536]{2,1,0:T(8,128)(2,1)} %param.19) | copy-start | bytes 9437188
  48.3 0.9 copy-start.3
  48.4 12.4 %copy-start.28 = (f32[12]{0:T(128)}, f32[12]{0:T(128)S(1)}, u32[]{:S(2)}) copy-start(f32[12]{0:T(128)S(1)} %get-tuple-element.209) | copy-start | bytes 148
  48.4 12.4 %copy-start.30 = (f32[12]{0:T(128)}, f32[12]{0:T(128)S(1)}, u32[]{:S(2)}) copy-start(f32[12]{0:T(128)S(1)} %get-tuple-element.210) | copy-start | bytes 148
  50.1 81.7 %all-gather.15.cloned.1.call-start = ((), (), s32[]{:S(2)}) async-start(), calls=%async_computation.4 | async-start | bytes 1966080 | tf_op jit(solution)/shard_map/all_gather | solution.py:26
  61.4 27.0 %copy-start.24 = (f32[12]{0:T(128)}, f32[12]{0:T(128)S(1)}, u32[]{:S(2)}) copy-start(f32[12]{0:T(128)S(1)} %get-tuple-element.207) | copy-start | bytes 148
  89.5 9.3 %copy-start.2 = (bf16[32,32,1536]{2,1,0:T(8,128)(2,1)S(1)}, bf16[32,32,1536]{2,1,0:T(8,128)(2,1)}, u32[]{:S(2)}) copy-start(bf16[32,32,1536]{2,1,0:T(8,128)(2,1)} %param.20) | copy-start | bytes 9437188
  103.2 9.3 %copy-start.8 = (bf16[64,1024]{1,0:T(8,128)(2,1)S(1)}, bf16[64,1024]{1,0:T(8,128)(2,1)}, u32[]{:S(2)}) copy-start(bf16[64,1024]{1,0:T(8,128)(2,1)} %param.23) | copy-start | bytes 393220
  103.2 10.0 %copy-start.38 = (f32[1,1,12]{2,1,0:T(1,128)S(1)}, f32[1,1,12]{2,1,0:T(1,128)}, u32[]{:S(2)}) copy-start(f32[1,1,12]{2,1,0:T(1,128)} %get-tuple-element.203) | copy-start | bytes 148
  103.2 18.7 %copy-start.10 = (bf16[64,1024]{1,0:T(8,128)(2,1)S(1)}, bf16[64,1024]{1,0:T(8,128)(2,1)}, u32[]{:S(2)}) copy-start(bf16[64,1024]{1,0:T(8,128)(2,1)} %param.22) | copy-start | bytes 393220
  103.2 19.1 %copy-start.14 = (f32[256,12,4]{0,1,2:T(8,128)S(1)}, f32[256,12,4]{0,1,2:T(8,128)}, u32[]{:S(2)}) copy-start(f32[256,12,4]{0,1,2:T(8,128)} %copy-done.13) | copy-start | bytes 147460
  103.2 19.1 %copy-start.19 = (f32[12,4,256]{2,0,1:T(8,128)S(1)}, f32[12,4,256]{2,0,1:T(8,128)}, u32[]{:S(2)}) copy-start(f32[12,4,256]{2,0,1:T(8,128)} %get-tuple-element.186) | copy-start | bytes 147460
  121.3 1.0 copy-start.21
  122.3 9.5 %copy-start.25 = (f32[12]{0:T(128)S(1)}, f32[12]{0:T(128)}, u32[]{:S(2)}) copy-start(f32[12]{0:T(128)} %copy-done.24) | copy-start | bytes 148
  122.3 9.5 %copy-start.29 = (f32[12]{0:T(128)S(1)}, f32[12]{0:T(128)}, u32[]{:S(2)}) copy-start(f32[12]{0:T(128)} %copy-done.28) | copy-start | bytes 148
  122.3 9.5 %copy-start.31 = (f32[12]{0:T(128)S(1)}, f32[12]{0:T(128)}, u32[]{:S(2)}) copy-start(f32[12]{0:T(128)} %copy-done.30) | copy-start | bytes 148
  122.3 9.5 %copy-start.34 = (f32[12]{0:T(128)S(1)}, f32[12]{0:T(128)}, u32[]{:S(2)}) copy-start(f32[12]{0:T(128)} %get-tuple-element.192) | copy-start | bytes 148
  122.3 9.5 %copy-start.35 = (f32[12]{0:T(128)S(1)}, f32[12]{0:T(128)}, u32[]{:S(2)}) copy-start(f32[12]{0:T(128)} %get-tuple-element.193) | copy-start | bytes 148
  122.4 9.5 %copy-start.36 = (f32[12]{0:T(128)S(1)}, f32[12]{0:T(128)}, u32[]{:S(2)}) copy-start(f32[12]{0:T(128)} %get-tuple-element.194) | copy-start | bytes 148
  122.4 9.5 %copy-start.37 = (f32[12]{0:T(128)S(1)}, f32[12]{0:T(128)}, u32[]{:S(2)}) copy-start(f32[12]{0:T(128)} %get-tuple-element.172) | copy-start | bytes 148
  122.4 9.5 %copy-start.40 = (f32[12]{0:T(128)S(1)}, f32[12]{0:T(128)}, u32[]{:S(2)}) copy-start(f32[12]{0:T(128)} %exp.377) | copy-start | bytes 148
  122.4 12.4 %copy-start.17 = (bf16[64,4,256]{2,1,0:T(4,128)(2,1)S(1)}, bf16[64,4,256]{2,1,0:T(4,128)(2,1)}, u32[]{:S(2)}) copy-start(bf16[64,4,256]{2,1,0:T(4,128)(2,1)} %reshape.654) | copy-start | bytes 393220
  122.4 12.4 %copy-start.18 = (f32[4,256,12]{1,2,0:T(8,128)S(1)}, f32[4,256,12]{1,2,0:T(8,128)}, u32[]{:S(2)}) copy-start(f32[4,256,12]{1,2,0:T(8,128)} %get-tuple-element.184) | copy-start | bytes 147460
  122.4 12.4 %copy-start.39 = (f32[4,12]{1,0:T(4,128)S(1)}, f32[4,12]{1,0:T(4,128)}, u32[]{:S(2)}) copy-start(f32[4,12]{1,0:T(4,128)} %exp.303) | copy-start | bytes 580
  122.4 12.4 %copy-start.41 = (f32[12]{0:T(128)S(1)}, f32[12]{0:T(128)}, u32[]{:S(2)}) copy-start(f32[12]{0:T(128)} %param.26) | copy-start | bytes 148
  148.2 25.1 %all-to-all-start = ((f32[4,4,256,1]{2,1,3,0:T(4,128)}), f32[4,4,256,1]{2,1,3,0:T(4,128)S(1)}, u32[]{:S(2)}, u32[]{:S(2)}) async-start(f32[4,4,256,1]{2,1,3,0:T(4,128)} %broadcast_in_dim.42), calls=%async_computation | async-start | bytes 32768 | tf_op jit(solution)/shard_map/all_to_all | solution.py:38
  164.6 8.8 %copy-start.23 = (f32[1536]{0:T(1024)S(1)}, f32[1536]{0:T(1024)}, u32[]{:S(2)}) copy-start(f32[1536]{0:T(1024)} %param.27) | copy-start | bytes 18436
  181.2 47.6 %all-to-all-start.1 = ((bf16[32,32,1536]{2,0,1:T(8,128)(2,1)}), bf16[32,32,1536]{2,0,1:T(8,128)(2,1)S(1)}, u32[]{:S(2)}, u32[]{:S(2)}) async-start(bf16[32,32,1536]{2,0,1:T(8,128)(2,1)} %copy.64), calls=%async_computation.1 | async-start | bytes 6291456 | tf_op jit(solution)/shard_map/all_to_all | solution.py:150
  185.5 104.5 %all-gather.17.cloned.1.call-start = ((), (), s32[]{:S(2)}) async-start(), calls=%async_computation.5 | async-start | bytes 1966080 | tf_op jit(solution)/shard_map/all_gather | solution.py:26
  192.8 0.6 copy-start.15
  259.4 0.9 copy-start.4
  259.5 14.4 %copy-start.32 = (f32[12]{0:T(128)}, f32[12]{0:T(128)S(1)}, u32[]{:S(2)}) copy-start(f32[12]{0:T(128)S(1)} %get-tuple-element.201) | copy-start | bytes 148
  259.5 14.4 %copy-start.33 = (f32[12]{0:T(128)}, f32[12]{0:T(128)S(1)}, u32[]{:S(2)}) copy-start(f32[12]{0:T(128)S(1)} %get-tuple-element.202) | copy-start | bytes 148
  261.2 84.8 %all-gather.19.cloned.1.call-start = ((), (), s32[]{:S(2)}) async-start(), calls=%async_computation.6 | async-start | bytes 1966080 | tf_op jit(solution)/shard_map/all_gather | solution.py:26
  274.0 18.3 %copy-start.26 = (f32[12]{0:T(128)}, f32[12]{0:T(128)S(1)}, u32[]{:S(2)}) copy-start(f32[12]{0:T(128)S(1)} %get-tuple-element.199) | copy-start | bytes 148
  296.9 7.0 %copy-start.11 = (bf16[64,1024]{1,0:T(8,128)(2,1)S(1)}, bf16[64,1024]{1,0:T(8,128)(2,1)}, u32[]{:S(2)}) copy-start(bf16[64,1024]{1,0:T(8,128)(2,1)} %param.29) | copy-start | bytes 393220
  296.9 7.7 %copy-start.12 = (bf16[64,1024]{1,0:T(8,128)(2,1)S(1)}, bf16[64,1024]{1,0:T(8,128)(2,1)}, u32[]{:S(2)}) copy-start(bf16[64,1024]{1,0:T(8,128)(2,1)} %param.28) | copy-start | bytes 393220
  318.4 18.2 %copy-start.7 = (f32[4,256,256]{2,1,0:T(8,128)S(1)}, f32[4,256,256]{2,1,0:T(8,128)}, u32[]{:S(2)}) copy-start(f32[4,256,256]{2,1,0:T(8,128)} %fusion.61) | copy-start | bytes 3145732
  318.4 18.2 %copy-start.16 = (f32[256,12,4]{0,1,2:T(8,128)S(1)}, f32[256,12,4]{0,1,2:T(8,128)}, u32[]{:S(2)}) copy-start(f32[256,12,4]{0,1,2:T(8,128)} %copy-done.15) | copy-start | bytes 147460
  336.7 9.3 %copy-start.5 = (f32[24,64,128]{2,1,0:T(8,128)S(1)}, f32[24,64,128]{2,1,0:T(8,128)}, u32[]{:S(2)}) copy-start(f32[24,64,128]{2,1,0:T(8,128)} %copy-done.4) | copy-start | bytes 2359300
  336.7 9.3 %copy-start.6 = (f32[4,12,64,128]{3,2,1,0:T(8,128)S(1)}, f32[4,12,64,128]{3,2,1,0:T(8,128)}, u32[]{:S(2)}) copy-start(f32[4,12,64,128]{3,2,1,0:T(8,128)} %all-gather.17.cloned.1.call-done) | copy-start | bytes 4718596
  336.7 9.3 %copy-start.27 = (f32[12]{0:T(128)S(1)}, f32[12]{0:T(128)}, u32[]{:S(2)}) copy-start(f32[12]{0:T(128)} %copy-done.26) | copy-start | bytes 148
  336.7 11.6 %copy-start.20 = (f32[4,256,12]{1,2,0:T(8,128)S(1)}, f32[4,256,12]{1,2,0:T(8,128)}, u32[]{:S(2)}) copy-start(f32[4,256,12]{1,2,0:T(8,128)} %get-tuple-element.182) | copy-start | bytes 147460
  361.5 25.2 %all-to-all-start.2 = ((f32[4,4,256,1]{2,1,3,0:T(4,128)}), f32[4,4,256,1]{2,1,3,0:T(4,128)S(1)}, u32[]{:S(2)}, u32[]{:S(2)}) async-start(f32[4,4,256,1]{2,1,3,0:T(4,128)} %broadcast_in_dim.43), calls=%async_computation.2 | async-start | bytes 32768 | tf_op jit(solution)/shard_map/all_to_all | solution.py:38
  378.2 8.5 %copy-start = (bf16[1024,1,1536]{0,2,1:T(8,128)(2,1)S(1)}, bf16[1024,1,1536]{0,2,1:T(8,128)(2,1)}, u32[]{:S(2)}) copy-start(bf16[1024,1,1536]{0,2,1:T(8,128)(2,1)} %copy.76) | copy-start | bytes 9437188
  378.2 8.5 %copy-start.22 = (f32[1536]{0:T(1024)S(1)}, f32[1536]{0:T(1024)}, u32[]{:S(2)}) copy-start(f32[1536]{0:T(1024)} %param.33) | copy-start | bytes 18436
Sparse Core Ops, SparseCore 0:
  50.2 31.4 all-gather.12
  84.2 26.3 all-gather.14
  261.3 28.5 all-gather.16
  292.4 26.3 all-gather.18
where the time goes:
time: 411 us; the launch traced here: 404 us
  local copies, waits for them, and re-layouts  133 us (32%)
  waiting for transfers between devices  70.2 us (17%)
  blocking collectives  64.4 us (16%)
  matrix products  55.8 us (14%)
  other arithmetic  46.5 us (11%)
  starting transfers between devices  18.6 us (5%)
  between operations  15.2 us (4%)
    all_gather x4, waiting for transfers between devices, entering(): pieces = jax.tree.map(lambda part: lax.all_gather(part, axis), subtotal)  36.2 us
    all_gather x4, blocking collectives, entering(): pieces = jax.tree.map(lambda part: lax.all_gather(part, axis), subtotal)  34.1 us
    all_to_all x1, waiting for transfers between devices, body(): lax.all_to_all(first_out.reshape(grid_rows, grid_cols, features), SEQ, sp...  33.9 us
    convert_element_type x4, local copies, waits for them, and re-layouts, ssd_layer(): outputs = inner_part + from_state * lifting + skip_vec[:, None] * inputs  31.4 us
    unnamed x4, blocking collectives  30.3 us
    dot_general x2, matrix products, ssd_layer(): jnp.einsum('ncqt,cqhnp->qtchp', read_mat.astype(jnp.float32), incoming, p...  25.3 us
    convert_element_type x3, local copies, waits for them, and re-layouts, ssd_layer(): gate_mat.astype(jnp.float32)  20.6 us
    add x2, local copies, waits for them, and re-layouts, ssd_layer(): outputs = inner_part + from_state * lifting + skip_vec[:, None] * inputs  18.9 us
  transfers between devices with their start and end apart: 7, of which 3 were waited for; matrix products, arithmetic and copies ran while one was open for 33% of the time, Pallas kernels for 0%

commit v1 on v0

v1 whole, which is shorter than its diff:
```python
import functools

import jax
import jax.numpy as jnp
from jax import lax
from jax.experimental import pallas as pl
from jax.experimental.pallas import tpu as pltpu
from jax.sharding import Mesh
from jax.sharding import PartitionSpec as P

BLOCK = 256
SEQ = ("seq_0", "seq_1", "seq_2")
EPSILON = 1e-05
LANES = 128
TILE = 8
HEADS_PER_STEP = 3
VMEM_LIMIT = 40 * 1024 * 1024
F32 = jnp.float32
BF16 = jnp.bfloat16


def params():
    return pltpu.CompilerParams(vmem_limit_bytes=VMEM_LIMIT)


def split_three(value):
    high = value.astype(BF16)
    rest = value - high.astype(F32)
    middle = rest.astype(BF16)
    low = (rest - middle.astype(F32)).astype(BF16)
    return high, middle, low


def running_sums(decay):
    length = decay.shape[1]
    earlier = lax.broadcasted_iota(jnp.int32, (length, length), 0)
    later = lax.broadcasted_iota(jnp.int32, (length, length), 1)
    upper = jnp.where(earlier <= later, 1.0, 0.0).astype(BF16)
    high, middle, low = split_three(decay)
    total = jnp.dot(low, upper, preferred_element_type=F32)
    total = total + jnp.dot(middle, upper, preferred_element_type=F32)
    return total + jnp.dot(high, upper, preferred_element_type=F32)


def norm_scale(squares, features):
    return lax.rsqrt(squares / features + EPSILON)


def head_inputs(x_ref, head, by_head):
    if by_head:
        rows = x_ref.shape[1] // 12
        return x_ref[:, head * rows : (head + 1) * rows, :].reshape(BLOCK, LANES)
    return x_ref[:, head * LANES : (head + 1) * LANES]


def states_kernel(by_head, features, *refs):
    if by_head:
        x_ref, write_ref, step_ref, decay_ref, squares_ref, payload_ref, before_ref, state, total = refs
    else:
        x_ref, write_ref, step_ref, decay_ref, payload_ref, before_ref, state, total = refs
    head_count = step_ref.shape[0]
    state_size = write_ref.shape[0]
    block = pl.program_id(0)

    @pl.when(block == 0)
    def _():
        state[...] = jnp.zeros_like(state)
        total[...] = jnp.zeros_like(total)

    before_ref[0] = state[...]
    cumulative = running_sums(decay_ref[...])
    final = cumulative[:, BLOCK - 1 :]
    weights = jnp.exp(final - cumulative) * step_ref[...]
    if by_head:
        weights = weights * norm_scale(squares_ref[...], features)
    fading = jnp.broadcast_to(jnp.exp(final), (head_count, LANES))
    write = write_ref[...].astype(F32)
    for head in range(head_count):
        loaded = (write * weights[head : head + 1, :]).astype(BF16)
        gained = jnp.dot(loaded, head_inputs(x_ref, head, by_head), preferred_element_type=F32)
        rows = slice(head * state_size, (head + 1) * state_size)
        state[rows, :] = fading[head : head + 1, :] * state[rows, :] + gained
    total[...] = total[...] + jnp.broadcast_to(final, (head_count, LANES))

    @pl.when(block == pl.num_programs(0) - 1)
    def _():
        devices, height = payload_ref.shape[0], payload_ref.shape[1] - TILE
        payload_ref[:, :height, :] = state[...].reshape(devices, height, LANES)
        for device in range(devices):
            for tile in range(height // TILE):
                head = (device * height + tile * TILE) // state_size
                payload_ref[device, height + tile : height + tile + 1, :] = total[head : head + 1, :]
            left = height + height // TILE
            payload_ref[device, left:, :] = jnp.zeros((height + TILE - left, LANES), F32)


def device_states(x, write, step, decay, squares, features, devices):
    head_count, length = step.shape
    state_size = write.shape[0]
    blocks = length // BLOCK
    height = head_count * state_size // devices
    by_head = squares is not None
    if by_head:
        x_spec = pl.BlockSpec((x.shape[0] // blocks, *x.shape[1:]), lambda k: (k, 0, 0))
    else:
        x_spec = pl.BlockSpec((BLOCK, x.shape[1]), lambda k: (k, 0))
    along = lambda rows: pl.BlockSpec((rows, BLOCK), lambda k: (0, k))
    specs = [x_spec, along(state_size), along(head_count), along(head_count)]
    operands = [x, write, step, decay]
    if by_head:
        specs.append(along(1))
        operands.append(squares)
    return pl.pallas_call(
        functools.partial(states_kernel, by_head, features),
        grid=(blocks,),
        in_specs=specs,
        out_specs=[
            pl.BlockSpec((devices, height + TILE, LANES), lambda k: (0, 0, 0)),
            pl.BlockSpec((1, head_count * state_size, LANES), lambda k: (k, 0, 0)),
        ],
        out_shape=[
            jax.ShapeDtypeStruct((devices, height + TILE, LANES), F32),
            jax.ShapeDtypeStruct((blocks, head_count * state_size, LANES), F32),
        ],
        scratch_shapes=[
            pltpu.VMEM((head_count * state_size, LANES), F32),
            pltpu.VMEM((head_count, LANES), F32),
        ],
        compiler_params=params(),
        cost_estimate=pl.CostEstimate(flops=500_000_000, bytes_accessed=6_000_000, transcendentals=20_000),
        name="states",
    )(*operands)


def prefix_kernel(ends_ref, prior_ref):
    devices, height, _ = prior_ref.shape
    running = [jnp.zeros((TILE, LANES), F32) for _ in range(height // TILE)]
    for device in range(devices):
        for tile in range(height // TILE):
            rows = slice(tile * TILE, (tile + 1) * TILE)
            prior_ref[device, rows, :] = running[tile]
            fade = jnp.exp(ends_ref[device, height + tile : height + tile + 1, :])
            running[tile] = fade * running[tile] + ends_ref[device, rows, :]


def prior_states(payload):
    devices, height, _ = payload.shape
    height = height - TILE
    ends = lax.all_to_all(payload, SEQ, split_axis=0, concat_axis=0, tiled=True)
    prior = pl.pallas_call(
        prefix_kernel,
        out_shape=jax.ShapeDtypeStruct((devices, height, LANES), F32),
        compiler_params=params(),
        name="prefix",
    )(ends)
    prior = lax.all_to_all(prior, SEQ, split_axis=0, concat_axis=0, tiled=True)
    return prior.reshape(devices * height, LANES)


def read_state(read, state):
    parts = jnp.concatenate(split_three(state), axis=0)
    wide = jnp.concatenate([read, read, read], axis=0)
    return lax.dot_general(wide, parts, (((0,), (0,)), ((), ())), preferred_element_type=F32)


def local_kernel(by_head, features, *refs):
    if by_head:
        x_ref, write_ref, read_ref, step_ref, decay_ref, squares_ref, before_ref, skip_ref, out_ref, lift_ref, total = refs
    else:
        x_ref, write_ref, read_ref, step_ref, decay_ref, before_ref, skip_ref, out_ref, lift_ref, total = refs
    head_count = step_ref.shape[0]
    state_size = write_ref.shape[0]
    block = pl.program_id(0)
    half = BLOCK // 2

    @pl.when(block == 0)
    def _():
        total[...] = jnp.zeros_like(total)

    cumulative = running_sums(decay_ref[...])
    step = step_ref[...]
    if by_head:
        scale = norm_scale(squares_ref[...], features)
        step = step * scale
        scale_column = jnp.transpose(jnp.broadcast_to(scale, (LANES, BLOCK)))
    padding = jnp.zeros((LANES - head_count, BLOCK), F32)
    columns = jnp.transpose(jnp.concatenate([cumulative, padding], axis=0))
    whole = jnp.concatenate([cumulative + total[:, :1], padding], axis=0)
    lift_ref[...] = jnp.exp(jnp.transpose(whole))
    total[...] = total[...] + jnp.broadcast_to(cumulative[:, BLOCK - 1 :], (head_count, LANES))
    read = read_ref[...]
    scores = lax.dot_general(read, write_ref[...], (((0,), (0,)), ((), ())), preferred_element_type=F32)
    first, last = slice(0, half), slice(half, BLOCK)
    causal = lax.broadcasted_iota(jnp.int32, (half, half), 0) >= lax.broadcasted_iota(
        jnp.int32, (half, half), 1
    )
    for head in range(head_count):
        row = cumulative[head : head + 1, :]
        column = jnp.broadcast_to(columns[:, head : head + 1], (BLOCK, LANES))
        weight = step[head : head + 1, :]

        def mixing(t, s):
            spread = column[t] - row[:, s]
            if t == s:
                spread = jnp.where(causal, spread, -jnp.inf)
            return (jnp.exp(spread) * scores[t, s] * weight[:, s]).astype(BF16)

        x = head_inputs(x_ref, head, by_head)
        upper = jnp.dot(mixing(first, first), x[first], preferred_element_type=F32)
        both = jnp.concatenate([mixing(last, first), mixing(last, last)], axis=1)
        lower = jnp.dot(both, x, preferred_element_type=F32)
        state = before_ref[0, head * state_size : (head + 1) * state_size, :]
        outputs = jnp.concatenate([upper, lower], axis=0) + jnp.exp(column) * read_state(read, state)
        skipped = skip_ref[head] * x.astype(F32)
        if by_head:
            skipped = skipped * scale_column
        out_ref[:, head * LANES : (head + 1) * LANES] = outputs + skipped


def local_outputs(x, write, read, step, decay, squares, before, skip, features):
    head_count, length = step.shape
    state_size = write.shape[0]
    blocks = length // BLOCK
    by_head = squares is not None
    if by_head:
        x_spec = pl.BlockSpec((x.shape[0] // blocks, *x.shape[1:]), lambda k: (k, 0, 0))
    else:
        x_spec = pl.BlockSpec((BLOCK, x.shape[1]), lambda k: (k, 0))
    along = lambda rows: pl.BlockSpec((rows, BLOCK), lambda k: (0, k))
    specs = [x_spec, along(state_size), along(state_size), along(head_count), along(head_count)]
    operands = [x, write, read, step, decay]
    if by_head:
        specs.append(along(1))
        operands.append(squares)
    specs.append(pl.BlockSpec((1, head_count * state_size, LANES), lambda k: (k, 0, 0)))
    specs.append(pl.BlockSpec(memory_space=pltpu.SMEM))
    operands += [before, skip]
    width = head_count * LANES
    return pl.pallas_call(
        functools.partial(local_kernel, by_head, features),
        grid=(blocks,),
        in_specs=specs,
        out_specs=[
            pl.BlockSpec((BLOCK, width), lambda k: (k, 0)),
            pl.BlockSpec((BLOCK, LANES), lambda k: (k, 0)),
        ],
        out_shape=[
            jax.ShapeDtypeStruct((length, width), F32),
            jax.ShapeDtypeStruct((length, LANES), F32),
        ],
        scratch_shapes=[pltpu.VMEM((head_count, LANES), F32)],
        compiler_params=params(),
        cost_estimate=pl.CostEstimate(
            flops=6_000_000_000, bytes_accessed=12_000_000, transcendentals=3_000_000
        ),
        name="local",
    )(*operands)


def gated_kernel(first_layer, local_ref, lift_ref, read_ref, prior_ref, gate_ref, gain_ref, *refs):
    if first_layer:
        out_ref, squares_ref, total, staged = refs
    else:
        out_ref, squares_ref, total = refs
    group = pl.program_id(0)
    length = local_ref.shape[0]
    heads = local_ref.shape[1] // LANES
    state_size = read_ref.shape[0]
    cols = out_ref.shape[0]
    rows = length // cols

    @pl.when(group == 0)
    def _():
        total[...] = jnp.zeros_like(total)

    read = read_ref[...]
    chosen = lax.broadcasted_iota(jnp.int32, (length, LANES), 1)
    for head in range(heads):
        place = slice(head * LANES, (head + 1) * LANES)
        state = prior_ref[head * state_size : (head + 1) * state_size, :]
        at = group * heads + head
        lift = jnp.sum(jnp.where(chosen == at, lift_ref[...], 0.0), axis=1, keepdims=True)
        outputs = local_ref[:, place] + lift * read_state(read, state)
        gate = gate_ref[:, place].astype(F32)
        gated = outputs * (gate / (1.0 + jnp.exp(-gate)))
        total[...] += gated * gated
        gated = gated * gain_ref[:, place]
        if first_layer:
            staged[...] = gated
            for col in range(cols):
                picked = staged[pl.ds(col, rows, stride=cols), :]
                out_ref[col, head * rows : (head + 1) * rows, :] = picked.astype(BF16)
        else:
            out_ref[:, place] = gated

    @pl.when(group == pl.num_programs(0) - 1)
    def _():
        if first_layer:
            ordered = jnp.concatenate(
                [total[pl.ds(col, rows, stride=cols), :] for col in range(cols)], axis=0
            )
        else:
            ordered = total[...]
        ones = jnp.ones((TILE, LANES), BF16)
        sums = jnp.zeros((TILE, length), F32)
        for part in split_three(ordered):
            sums = sums + lax.dot_general(
                ones, part, (((1,), (1,)), ((), ())), preferred_element_type=F32
            )
        squares_ref[...] = sums[:1]


def gated_outputs(first_layer, local, lift, read, prior, gate, gain, cols):
    length, width = local.shape
    state_size = read.shape[0]
    heads = HEADS_PER_STEP
    part = heads * LANES
    groups = width // part
    if first_layer:
        rows = length // cols
        out_spec = pl.BlockSpec((cols, heads * rows, LANES), lambda g: (0, g, 0))
        out_shape = jax.ShapeDtypeStruct((cols, width // LANES * rows, LANES), BF16)
        scratch = [pltpu.VMEM((length, LANES), F32), pltpu.VMEM((length, LANES), F32)]
    else:
        out_spec = pl.BlockSpec((length, part), lambda g: (0, g))
        out_shape = jax.ShapeDtypeStruct((length, width), F32)
        scratch = [pltpu.VMEM((length, LANES), F32)]
    return pl.pallas_call(
        functools.partial(gated_kernel, first_layer),
        grid=(groups,),
        in_specs=[
            pl.BlockSpec((length, part), lambda g: (0, g)),
            pl.BlockSpec((length, LANES), lambda g: (0, 0)),
            pl.BlockSpec((state_size, length), lambda g: (0, 0)),
            pl.BlockSpec((heads * state_size, LANES), lambda g: (g, 0)),
            pl.BlockSpec((length, part), lambda g: (0, g)),
            pl.BlockSpec((1, part), lambda g: (0, g)),
        ],
        out_specs=[out_spec, pl.BlockSpec((1, length), lambda g: (0, 0))],
        out_shape=[out_shape, jax.ShapeDtypeStruct((1, length), F32)],
        scratch_shapes=scratch,
        compiler_params=params(),
        cost_estimate=pl.CostEstimate(
            flops=1_200_000_000, bytes_accessed=13_000_000, transcendentals=2_000_000
        ),
        name="gated",
    )(local, lift, read, prior, gate, gain)


def scaled_kernel(features, gated_ref, squares_ref, out_ref):
    scale = norm_scale(squares_ref[...], features)
    column = jnp.transpose(jnp.broadcast_to(scale, (LANES, scale.shape[1])))
    for head in range(gated_ref.shape[1] // LANES):
        place = slice(head * LANES, (head + 1) * LANES)
        out_ref[:, place] = (gated_ref[:, place] * column).astype(BF16)


def scaled_outputs(gated, squares, features):
    length, width = gated.shape
    return pl.pallas_call(
        functools.partial(scaled_kernel, features),
        grid=(length // BLOCK,),
        in_specs=[
            pl.BlockSpec((BLOCK, width), lambda k: (k, 0)),
            pl.BlockSpec((1, BLOCK), lambda k: (0, k)),
        ],
        out_specs=pl.BlockSpec((BLOCK, width), lambda k: (k, 0)),
        out_shape=jax.ShapeDtypeStruct((length, width), BF16),
        compiler_params=params(),
        name="scaled",
    )(gated, squares)


def column_squares(squares, devices):
    whole = lax.psum(squares, "head")[0]
    for axis in reversed(SEQ):
        whole = lax.all_gather(whole, axis)
    whole = whole.reshape(devices, devices, -1)
    mine = lax.dynamic_index_in_dim(whole, lax.axis_index(SEQ), axis=1, keepdims=False)
    return mine.reshape(1, -1)


def body(
    tokens_in,
    gate_rows,
    gate_cols,
    write_rows,
    read_rows,
    step_rows,
    decay_rows,
    skip_rows,
    norm_rows,
    write_cols,
    read_cols,
    step_cols,
    decay_cols,
    skip_cols,
    norm_cols,
):
    grid_rows, grid_cols, width = tokens_in.shape
    devices = lax.axis_size(SEQ)
    features = float(width * lax.axis_size("head"))
    tokens = grid_rows * grid_cols
    column_len = gate_cols.shape[0]

    x = tokens_in.reshape(tokens, width)
    payload, before = device_states(x, write_rows, step_rows, decay_rows, None, features, devices)
    prior = prior_states(payload)
    local, lift = local_outputs(
        x, write_rows, read_rows, step_rows, decay_rows, None, before, skip_rows, features
    )
    hidden, squares = gated_outputs(
        True, local, lift, read_rows, prior, gate_rows.reshape(tokens, width), norm_rows[None], grid_cols
    )
    hidden = lax.all_to_all(hidden, SEQ, split_axis=0, concat_axis=0, tiled=True)
    squares = column_squares(squares, devices)

    payload, before = device_states(
        hidden, write_cols, step_cols, decay_cols, squares, features, devices
    )
    prior = prior_states(payload)
    local, lift = local_outputs(
        hidden, write_cols, read_cols, step_cols, decay_cols, squares, before, skip_cols, features
    )
    gated, squares = gated_outputs(
        False, local, lift, read_cols, prior, gate_cols.reshape(column_len, width), norm_cols[None], 1
    )
    squares = lax.psum(squares, "head")
    out = scaled_outputs(gated, squares, features)
    return out.reshape(column_len, 1, width)


def solution(mesh):
    torus = Mesh(
        mesh.devices.reshape(4, 4, 2, mesh.shape["head"]), ("seq_0", "seq_1", "seq_2", "head")
    )
    return jax.shard_map(
        body,
        mesh=torus,
        in_specs=(
            P(SEQ, None, "head"),
            P(SEQ, None, "head"),
            P(None, SEQ, "head"),
            P(None, SEQ),
            P(None, SEQ),
            P("head", SEQ),
            P("head", SEQ),
            P("head"),
            P("head"),
            P(None, SEQ),
            P(None, SEQ),
            P("head", SEQ),
            P("head", SEQ),
            P("head"),
            P("head"),
        ),
        out_specs=P(None, SEQ, "head"),
        check_vma=False,
    )
```

time: 411 us -> 222 us (0.54); the launches traced: 404 us -> 221 us
  local copies, waits for them, and re-layouts: 133 us -> 45.5 us
  matrix products: 55.8 us -> 0 us
  waiting for transfers between devices: 70.2 us -> 19.4 us
  other arithmetic: 46.5 us -> 0 us
  Pallas kernels: 0 us -> 42.1 us
  blocking collectives: 64.4 us -> 82.7 us
  between operations: 15.2 us -> 0.26 us
  starting transfers between devices: 18.6 us -> 30.8 us
    convert_element_type x11 -> x0, local copies, waits for them, and re-layouts: 61.7 us -> none  [the longest x4 31.4 us: ssd_layer(): outputs = inner_part + from_state * lifting + skip_vec[:, None] * inputs]
    dot_general x10 -> x0, matrix products: 55.8 us -> none  [the longest x2 25.3 us: ssd_layer(): jnp.einsum('ncqt,cqhnp->qtchp', read_mat.astype(jnp.float32), incoming, p...]
    psum x0 -> x2, blocking collectives: none -> 53.3 us  [the longest x1 37.2 us: column_squares(): whole = lax.psum(squares, 'head')[0]]
    pallas_call x0 -> x9, Pallas kernels: none -> 42.1 us  [the longest x2 16.1 us: gated_outputs(): pl.pallas_call(functools.partial(gated_kernel, first_layer), grid=(groups...]
    all_gather x4 -> x0, waiting for transfers between devices: 36.2 us -> none  [entering(): pieces = jax.tree.map(lambda part: lax.all_gather(part, axis), subtotal)]
    unnamed x94 -> x79, local copies, waits for them, and re-layouts: 9.85 us -> 42.7 us
    unnamed x4 -> x0, blocking collectives: 30.3 us -> none
    add x2 -> x0, local copies, waits for them, and re-layouts: 18.9 us -> none  [ssd_layer(): outputs = inner_part + from_state * lifting + skip_vec[:, None] * inputs]
  transfers between devices with their start and end apart: 7 -> 5, of which waited for: 3 -> 2; matrix products, arithmetic and copies ran while one was open for 33% -> 1% of each run, Pallas kernels for 0% -> 7%
where the time goes in v1:
time: 222 us; the launch traced here: 221 us
  blocking collectives  82.7 us (37%)
  local copies, waits for them, and re-layouts  45.5 us (20%)
  Pallas kernels  42.1 us (19%)
  starting transfers between devices  30.8 us (14%)
  waiting for transfers between devices  19.4 us (9%)
    unnamed x79, local copies, waits for them, and re-layouts  42.7 us
    psum x1, blocking collectives, column_squares(): whole = lax.psum(squares, 'head')[0]  37.2 us
    all_gather x3, blocking collectives, column_squares(): whole = lax.all_gather(whole, axis)  29.4 us
    all_to_all x2, waiting for transfers between devices, prior_states(): ends = lax.all_to_all(payload, SEQ, split_axis=0, concat_axis=0, tiled=True)  19.4 us
    pallas_call x2, Pallas kernels, gated_outputs(): pl.pallas_call(functools.partial(gated_kernel, first_layer), grid=(groups...  16.1 us
    psum x1, blocking collectives, body(): squares = lax.psum(squares, 'head')  16 us
    all_to_all x2, starting transfers between devices, prior_states(): ends = lax.all_to_all(payload, SEQ, split_axis=0, concat_axis=0, tiled=True)  15.2 us
    pallas_call x2, Pallas kernels, local_outputs(): pl.pallas_call(functools.partial(local_kernel, by_head, features), grid=(...  14.7 us
  transfers between devices with their start and end apart: 5, of which 2 were waited for; matrix products, arithmetic and copies ran while one was open for 1% of the time, Pallas kernels for 7%

profile of v1, /device:TPU:1, one launch (start us, length us, event | category | flops | bytes accessed | tf_op | source)
XLA Modules:
  0.0 220.8 jit_solution(16067526231636403560)
XLA Ops:
  0.0 1.9 copy-done.6
  1.9 0.9 copy-done.20
  2.8 0.8 copy-done.24
  3.7 0.8 copy-done.26
  4.5 2.5 %states.2 = (f32[32,32,128]{2,1,0:T(8,128)S(1)}, f32[4,768,128]{2,1,0:T(8,128)S(1)}) custom-call(bf16[1024,1536]{1,0:T(8,128)(2,1)S(1)} %bitcast.8, bf16[64,1024]{1,0:T(8,128)(2,1)S(1)} %copy-done.20, f32[12,1024]{1,0:T(8,128)S(1)} %copy-done.24, f32[12,1024]{1,0:T(8,128)S(1)} %copy-done.26), custom_call_target="tpu_custom_call" | custom-call | flops 500000000 | bytes 6000000 | tf_op jit(solution)/shard_map/states/pallas_call | solution.py:113
  7.1 0.0 copy-start.10
  7.1 0.8 copy-done.10
  7.9 1.1 copy-done.34
  9.0 9.9 %all-to-all-start = ((f32[32,32,128]{2,1,0:T(8,128)}), f32[32,32,128]{2,1,0:T(8,128)}, u32[]{:S(2)}, u32[]{:S(2)}) async-start(f32[32,32,128]{2,1,0:T(8,128)} %copy-done.10), calls=%async_computation | async-start | bytes 1048576 | tf_op jit(solution)/shard_map/all_to_all | solution.py:149
  18.9 10.7 %all-to-all-done.ends_ref = f32[32,32,128]{2,1,0:T(8,128)} async-done(((f32[32,32,128]{2,1,0:T(8,128)}), f32[32,32,128]{2,1,0:T(8,128)}, u32[]{:S(2)}, u32[]{:S(2)}) %all-to-all-start) | async-done | bytes 524320 | tf_op jit(solution)/shard_map/all_to_all | solution.py:149
  29.6 1.9 prefix.2
  31.5 3.9 %all-to-all-start.1 = ((f32[32,24,128]{2,1,0:T(8,128)}), f32[32,24,128]{2,1,0:T(8,128)S(1)}, u32[]{:S(2)}, u32[]{:S(2)}) async-start(f32[32,24,128]{2,1,0:T(8,128)} %prefix.2), calls=%async_computation.1 | async-start | bytes 786432 | tf_op jit(solution)/shard_map/all_to_all | solution.py:156
  35.4 0.0 copy-start.16
  35.4 0.9 copy-done.16
  36.3 0.9 copy-done.21
  37.2 0.8 copy-done.25
  38.0 0.8 copy-done.27
  38.9 1.4 copy-done.35
  40.3 7.4 %local.2 = (f32[1024,1536]{1,0:T(8,128)S(1)}, f32[1024,128]{1,0:T(8,128)S(1)}) custom-call(bf16[1024,1536]{1,0:T(8,128)(2,1)S(1)} %bitcast.9, bf16[64,1024]{1,0:T(8,128)(2,1)S(1)} %copy-done.21, bf16[64,1024]{1,0:T(8,128)(2,1)S(1)} %copy-done.16, f32[12,1024]{1,0:T(8,128)S(1)} %copy-done.25, f32[12,1024]{1,0:T(8,128)S(1)} %copy-done.27, ...), custom_call_target="tpu_custom_call" | custom-call | flops 6000000000 | bytes 12000000 | tf_op jit(solution)/shard_map/local/pallas_call | solution.py:239
  47.7 2.7 %copy-done.3 = f32[1024,1536]{1,0:T(8,128)} copy-done((f32[1024,1536]{1,0:T(8,128)}, f32[1024,1536]{1,0:T(8,128)S(1)}, u32[]{:S(2)}) %copy-start.3) | copy-done | bytes 6291480
  50.3 0.8 copy-done.14
  51.1 0.0 all-to-all-done.1
  51.1 2.8 %copy-done.4 = f32[1024,1536]{1,0:T(8,128)S(1)} copy-done((f32[1024,1536]{1,0:T(8,128)S(1)}, f32[1024,1536]{1,0:T(8,128)}, u32[]{:S(2)}) %copy-start.4) | copy-done | bytes 6291480
  53.9 1.9 copy-done.8
  55.8 1.0 copy-done.15
  56.9 0.9 copy-done.17
  57.8 9.5 %gated.2 = (bf16[32,384,128]{2,1,0:T(8,128)(2,1)S(1)}, f32[1,1024]{1,0:T(1,128)S(1)}) custom-call(f32[1024,1536]{1,0:T(8,128)S(1)} %copy-done.4, f32[1024,128]{1,0:T(8,128)S(1)} %copy-done.15, bf16[64,1024]{1,0:T(8,128)(2,1)S(1)} %copy-done.17, f32[768,128]{1,0:T(8,128)S(1)} %bitcast.13, bf16[1024,1536]{1,0:T(8,128)(2,1)S(1)} %bitcast.10, ...), custom_call_target="tpu_custom_call" | custom-call | flops 1200000000 | bytes 13000000 | tf_op jit(solution)/shard_map/gated/pallas_call | solution.py:328
  67.2 0.0 copy-start.5
  67.2 1.7 copy-done.5
  68.9 7.9 %all-to-all-start.2 = ((bf16[32,384,128]{2,1,0:T(8,128)(2,1)}), bf16[32,384,128]{2,1,0:T(8,128)(2,1)S(1)}, u32[]{:S(2)}, u32[]{:S(2)}) async-start(bf16[32,384,128]{2,1,0:T(8,128)(2,1)} %copy-done.5), calls=%async_computation.2 | async-start | bytes 6291456 | tf_op jit(solution)/shard_map/all_to_all | solution.py:415
  76.8 37.2 %psum.14 = f32[1,1024]{1,0:T(1,128)S(1)} all-reduce(f32[1,1024]{1,0:T(1,128)S(1)} %get-tuple-element.22), channel_id=1, replica_groups=mesh['seq_0'=4,'seq_1'=4,'seq_2'=2,'head'=4] {'head'}, use_global_device_ids=true, to_apply=%region_0.0 | all-reduce | flops 1024 | bytes 8192 | tf_op jit(solution)/shard_map/psum | solution.py:375
  114.0 3.4 %all-gather.2 = f32[2,1,1024]{2,1,0:T(1,128)S(1)} all-gather(f32[1,1,1024]{2,1,0:T(1,128)S(1)} %bitcast.15), channel_id=1, replica_groups=mesh['seq_0'=4,'seq_1'=4,'seq_2'=2,'head'=4] {'seq_2'}, dimensions={0}, use_global_device_ids=true | all-gather | bytes 12288 | tf_op jit(solution)/shard_map/all_gather | solution.py:377
  117.4 13.0 %all-gather.3 = f32[4,2,1024]{2,1,0:T(2,128)S(1)} all-gather(f32[1,2,1024]{2,1,0:T(2,128)S(1)} %copy.16), channel_id=2, replica_groups=mesh['seq_0'=4,'seq_1'=4,'seq_2'=2,'head'=4] {'seq_1'}, dimensions={0}, use_global_device_ids=true | all-gather | bytes 40960 | tf_op jit(solution)/shard_map/all_gather | solution.py:377
  130.4 13.1 %all-gather.1 = f32[16,2,1024]{2,1,0:T(2,128)S(1)} all-gather(f32[4,2,1024]{2,1,0:T(2,128)S(1)} %all-gather.3), channel_id=3, replica_groups=mesh['seq_0'=4,'seq_1'=4,'seq_2'=2,'head'=4] {'seq_0'}, dimensions={0}, use_global_device_ids=true | all-gather | bytes 163840 | tf_op jit(solution)/shard_map/all_gather | solution.py:377
  143.5 1.0 reshape.28
  144.5 1.0 dynamic-slice_reduce_fusion
  145.5 0.1 reshape.29.refs_4_.refs_5_
  145.6 0.0 all-to-all-done.2.refs_0_
  145.6 2.6 %states.3 = (f32[32,32,128]{2,1,0:T(8,128)S(1)}, f32[4,768,128]{2,1,0:T(8,128)S(1)}) custom-call(bf16[32,384,128]{2,1,0:T(8,128)(2,1)S(1)} %all-to-all-done.2.refs_0_, bf16[64,1024]{1,0:T(8,128)(2,1)S(1)} %copy-done.22, f32[12,1024]{1,0:T(8,128)S(1)} %copy-done.28, f32[12,1024]{1,0:T(8,128)S(1)} %copy-done.30, f32[1,1024]{1,0:T(1,128)S(1)} %reshape.29.refs_4_.refs_5_), custom_call_target="tpu_custom_call" | custom-call | flops 500000000 | bytes 6000000 | tf_op jit(solution)/shard_map/states/pallas_call | solution.py:113
  148.2 0.8 copy-done.11
  149.0 1.1 copy-done.32
  150.1 5.3 %all-to-all-start.3 = ((f32[32,32,128]{2,1,0:T(8,128)}), f32[32,32,128]{2,1,0:T(8,128)}, u32[]{:S(2)}, u32[]{:S(2)}) async-start(f32[32,32,128]{2,1,0:T(8,128)} %copy-done.11), calls=%async_computation.3 | async-start | bytes 1048576 | tf_op jit(solution)/shard_map/all_to_all | solution.py:149
  155.5 0.7 broadcast_in_dim.7.gain_ref
  156.2 8.8 %all-to-all-done.3.ends_ref = f32[32,32,128]{2,1,0:T(8,128)} async-done(((f32[32,32,128]{2,1,0:T(8,128)}), f32[32,32,128]{2,1,0:T(8,128)}, u32[]{:S(2)}, u32[]{:S(2)}) %all-to-all-start.3) | async-done | bytes 524320 | tf_op jit(solution)/shard_map/all_to_all | solution.py:149
  164.9 1.9 prefix.3
  166.8 3.9 %all-to-all-start.4 = ((f32[32,24,128]{2,1,0:T(8,128)}), f32[32,24,128]{2,1,0:T(8,128)S(1)}, u32[]{:S(2)}, u32[]{:S(2)}) async-start(f32[32,24,128]{2,1,0:T(8,128)} %prefix.3), calls=%async_computation.4 | async-start | bytes 786432 | tf_op jit(solution)/shard_map/all_to_all | solution.py:156
  170.7 0.0 copy-start.18
  170.7 0.9 copy-done.18
  171.6 0.9 copy-done.23
  172.5 0.8 copy-done.29
  173.4 0.8 copy-done.31
  174.2 1.4 copy-done.33
  175.6 7.4 %local.3 = (f32[1024,1536]{1,0:T(8,128)S(1)}, f32[1024,128]{1,0:T(8,128)S(1)}) custom-call(bf16[32,384,128]{2,1,0:T(8,128)(2,1)S(1)} %all-to-all-done.2.refs_0_, bf16[64,1024]{1,0:T(8,128)(2,1)S(1)} %copy-done.23, bf16[64,1024]{1,0:T(8,128)(2,1)S(1)} %copy-done.18, f32[12,1024]{1,0:T(8,128)S(1)} %copy-done.29, f32[12,1024]{1,0:T(8,128)S(1)} %copy-done.31, ...), custom_call_target="tpu_custom_call" | custom-call | flops 6000000000 | bytes 12000000 | tf_op jit(solution)/shard_map/local/pallas_call | solution.py:239
  183.0 2.7 %copy-done.2 = f32[1024,1536]{1,0:T(8,128)} copy-done((f32[1024,1536]{1,0:T(8,128)}, f32[1024,1536]{1,0:T(8,128)S(1)}, u32[]{:S(2)}) %copy-start.2) | copy-done | bytes 6291480
  185.7 0.8 copy-done.12
  186.4 0.0 all-to-all-done.4
  186.5 1.9 copy-done.9
  188.3 1.0 copy-done.13
  189.4 0.9 copy-done.19
  190.3 6.6 %gated.3 = (f32[1024,1536]{1,0:T(8,128)S(1)}, f32[1,1024]{1,0:T(1,128)S(1)}) custom-call(f32[1024,1536]{1,0:T(8,128)} %copy-done.2, f32[1024,128]{1,0:T(8,128)S(1)} %copy-done.13, bf16[64,1024]{1,0:T(8,128)(2,1)S(1)} %copy-done.19, f32[768,128]{1,0:T(8,128)S(1)} %bitcast.12, bf16[1024,1536]{1,0:T(8,128)(2,1)S(1)} %bitcast.11, ...), custom_call_target="tpu_custom_call" | custom-call | flops 1200000000 | bytes 13000000 | tf_op jit(solution)/shard_map/gated/pallas_call | solution.py:328
  196.9 2.7 %copy-done = f32[1024,1536]{1,0:T(8,128)} copy-done((f32[1024,1536]{1,0:T(8,128)}, f32[1024,1536]{1,0:T(8,128)S(1)}, u32[]{:S(2)}) %copy-start) | copy-done | bytes 6291480
  199.6 16.0 %psum.15.squares_ref = f32[1,1024]{1,0:T(1,128)S(1)} all-reduce(f32[1,1024]{1,0:T(1,128)S(1)} %get-tuple-element.28), channel_id=1, replica_groups=mesh['seq_0'=4,'seq_1'=4,'seq_2'=2,'head'=4] {'head'}, use_global_device_ids=true, to_apply=%region_1.2 | all-reduce | flops 1024 | bytes 8192 | tf_op jit(solution)/shard_map/psum | solution.py:428
  215.6 2.8 %copy-done.1 = f32[1024,1536]{1,0:T(8,128)S(1)} copy-done((f32[1024,1536]{1,0:T(8,128)S(1)}, f32[1024,1536]{1,0:T(8,128)}, u32[]{:S(2)}) %copy-start.1) | copy-done | bytes 6291480
  218.4 2.4 %scaled.1 = bf16[1024,1536]{1,0:T(8,128)(2,1)} custom-call(f32[1024,1536]{1,0:T(8,128)S(1)} %copy-done.1, f32[1,1024]{1,0:T(1,128)S(1)} %psum.15.squares_ref), custom_call_target="tpu_custom_call" | custom-call | tf_op jit(solution)/shard_map/scaled/pallas_call | solution.py:360
  (44 shorter events, 0.1 us)
Async XLA Ops:
  0.0 35.3 %copy-start.36 = (f32[12]{0:T(128)S(1)}, f32[12]{0:T(128)}, u32[]{:S(2)}) copy-start(f32[12]{0:T(128)} %refs_6_.1) | copy-start | bytes 148
  0.0 1.9 copy-start.6
  1.9 0.9 copy-start.20
  2.8 0.8 copy-start.24
  3.7 0.8 copy-start.26
  4.5 14.4 %copy-start.38 = (f32[1536]{0:T(1024)S(1)}, f32[1536]{0:T(1024)}, u32[]{:S(2)}) copy-start(f32[1536]{0:T(1024)} %param.23) | copy-start | bytes 18436
  4.5 30.9 %copy-start.7 = (bf16[32,32,1536]{2,1,0:T(8,128)(2,1)S(1)}, bf16[32,32,1536]{2,1,0:T(8,128)(2,1)}, u32[]{:S(2)}) copy-start(bf16[32,32,1536]{2,1,0:T(8,128)(2,1)} %param.15) | copy-start | bytes 9437188
  7.1 0.8 copy-start.10
  7.9 1.1 copy-start.34
  9.0 20.5 %all-to-all-start = ((f32[32,32,128]{2,1,0:T(8,128)}), f32[32,32,128]{2,1,0:T(8,128)}, u32[]{:S(2)}, u32[]{:S(2)}) async-start(f32[32,32,128]{2,1,0:T(8,128)} %copy-done.10), calls=%async_computation | async-start | bytes 1048576 | tf_op jit(solution)/shard_map/all_to_all | solution.py:149
  31.5 19.7 %all-to-all-start.1 = ((f32[32,24,128]{2,1,0:T(8,128)}), f32[32,24,128]{2,1,0:T(8,128)S(1)}, u32[]{:S(2)}, u32[]{:S(2)}) async-start(f32[32,24,128]{2,1,0:T(8,128)} %prefix.2), calls=%async_computation.1 | async-start | bytes 786432 | tf_op jit(solution)/shard_map/all_to_all | solution.py:156
  35.4 0.9 copy-start.16
  36.3 0.9 copy-start.21
  37.2 0.8 copy-start.25
  38.0 0.8 copy-start.27
  38.9 1.4 copy-start.35
  47.7 2.7 %copy-start.3 = (f32[1024,1536]{1,0:T(8,128)}, f32[1024,1536]{1,0:T(8,128)S(1)}, u32[]{:S(2)}) copy-start(f32[1024,1536]{1,0:T(8,128)S(1)} %get-tuple-element.18.local_ref) | copy-start | bytes 18874372
  50.3 0.8 copy-start.14
  51.1 2.8 %copy-start.4 = (f32[1024,1536]{1,0:T(8,128)S(1)}, f32[1024,1536]{1,0:T(8,128)}, u32[]{:S(2)}) copy-start(f32[1024,1536]{1,0:T(8,128)} %copy-done.3) | copy-start | bytes 18874372
  53.9 1.9 copy-start.8
  55.8 1.0 copy-start.15
  56.9 0.9 copy-start.17
  67.2 1.7 copy-start.5
  68.9 76.7 %copy-start.22 = (bf16[64,1024]{1,0:T(8,128)(2,1)S(1)}, bf16[64,1024]{1,0:T(8,128)(2,1)}, u32[]{:S(2)}) copy-start(bf16[64,1024]{1,0:T(8,128)(2,1)} %refs_1_.7) | copy-start | bytes 393220
  68.9 76.7 %copy-start.28 = (f32[12,1024]{1,0:T(8,128)S(1)}, f32[12,1024]{1,0:T(8,128)}, u32[]{:S(2)}) copy-start(f32[12,1024]{1,0:T(8,128)} %refs_3_.7) | copy-start | bytes 147460
  68.9 76.7 %copy-start.30 = (f32[12,1024]{1,0:T(8,128)S(1)}, f32[12,1024]{1,0:T(8,128)}, u32[]{:S(2)}) copy-start(f32[12,1024]{1,0:T(8,128)} %refs_4_.3) | copy-start | bytes 147460
  68.9 76.7 %all-to-all-start.2 = ((bf16[32,384,128]{2,1,0:T(8,128)(2,1)}), bf16[32,384,128]{2,1,0:T(8,128)(2,1)S(1)}, u32[]{:S(2)}, u32[]{:S(2)}) async-start(bf16[32,384,128]{2,1,0:T(8,128)(2,1)} %copy-done.5), calls=%async_computation.2 | async-start | bytes 6291456 | tf_op jit(solution)/shard_map/all_to_all | solution.py:415
  144.5 26.2 %copy-start.37 = (f32[12]{0:T(128)S(1)}, f32[12]{0:T(128)}, u32[]{:S(2)}) copy-start(f32[12]{0:T(128)} %refs_7_.1) | copy-start | bytes 148
  148.2 0.8 copy-start.11
  149.0 1.1 copy-start.32
  150.1 14.8 %all-to-all-start.3 = ((f32[32,32,128]{2,1,0:T(8,128)}), f32[32,32,128]{2,1,0:T(8,128)}, u32[]{:S(2)}, u32[]{:S(2)}) async-start(f32[32,32,128]{2,1,0:T(8,128)} %copy-done.11), calls=%async_computation.3 | async-start | bytes 1048576 | tf_op jit(solution)/shard_map/all_to_all | solution.py:149
  166.8 19.6 %all-to-all-start.4 = ((f32[32,24,128]{2,1,0:T(8,128)}), f32[32,24,128]{2,1,0:T(8,128)S(1)}, u32[]{:S(2)}, u32[]{:S(2)}) async-start(f32[32,24,128]{2,1,0:T(8,128)} %prefix.3), calls=%async_computation.4 | async-start | bytes 786432 | tf_op jit(solution)/shard_map/all_to_all | solution.py:156
  170.7 0.9 copy-start.18
  171.6 0.9 copy-start.23
  172.5 0.8 copy-start.29
  173.4 0.8 copy-start.31
  174.2 1.4 copy-start.33
  183.0 2.7 %copy-start.2 = (f32[1024,1536]{1,0:T(8,128)}, f32[1024,1536]{1,0:T(8,128)S(1)}, u32[]{:S(2)}) copy-start(f32[1024,1536]{1,0:T(8,128)S(1)} %get-tuple-element.24.local_ref) | copy-start | bytes 18874372
  185.7 0.8 copy-start.12
  186.5 1.9 copy-start.9
  188.3 1.0 copy-start.13
  189.4 0.9 copy-start.19
  196.9 2.7 %copy-start = (f32[1024,1536]{1,0:T(8,128)}, f32[1024,1536]{1,0:T(8,128)S(1)}, u32[]{:S(2)}) copy-start(f32[1024,1536]{1,0:T(8,128)S(1)} %get-tuple-element.27.gated_ref) | copy-start | bytes 18874372
  215.6 2.8 %copy-start.1 = (f32[1024,1536]{1,0:T(8,128)S(1)}, f32[1024,1536]{1,0:T(8,128)}, u32[]{:S(2)}) copy-start(f32[1024,1536]{1,0:T(8,128)} %copy-done) | copy-start | bytes 18874372

commit v2 on v1

--- a/solution.py
+++ b/solution.py
@@ -13,14 +13,15 @@
 EPSILON = 1e-05
 LANES = 128
 TILE = 8
-HEADS_PER_STEP = 3
-VMEM_LIMIT = 40 * 1024 * 1024
+HEADS_PER_STEP = 2
+EXTRA = 16
+MEGABYTE = 1024 * 1024
 F32 = jnp.float32
 BF16 = jnp.bfloat16
 
 
-def params():
-    return pltpu.CompilerParams(vmem_limit_bytes=VMEM_LIMIT)
+def params(megabytes=56):
+    return pltpu.CompilerParams(vmem_limit_bytes=megabytes * MEGABYTE)
 
 
 def split_three(value):
@@ -48,9 +49,14 @@
 
 def head_inputs(x_ref, head, by_head):
     if by_head:
-        rows = x_ref.shape[1] // 12
+        rows = BLOCK // x_ref.shape[0]
         return x_ref[:, head * rows : (head + 1) * rows, :].reshape(BLOCK, LANES)
     return x_ref[:, head * LANES : (head + 1) * LANES]
+
+
+def block_scale(squares_ref, features):
+    pieces = [squares_ref[device : device + 1, :] for device in range(squares_ref.shape[0])]
+    return norm_scale(jnp.concatenate(pieces, axis=1), features)
 
 
 def states_kernel(by_head, features, *refs):
@@ -72,7 +78,7 @@
     final = cumulative[:, BLOCK - 1 :]
     weights = jnp.exp(final - cumulative) * step_ref[...]
     if by_head:
-        weights = weights * norm_scale(squares_ref[...], features)
+        weights = weights * block_scale(squares_ref, features)
     fading = jnp.broadcast_to(jnp.exp(final), (head_count, LANES))
     write = write_ref[...].astype(F32)
     for head in range(head_count):
@@ -108,7 +114,7 @@
     specs = [x_spec, along(state_size), along(head_count), along(head_count)]
     operands = [x, write, step, decay]
     if by_head:
-        specs.append(along(1))
+        specs.append(pl.BlockSpec((squares.shape[0] // blocks, squares.shape[1]), lambda k: (k, 0)))
         operands.append(squares)
     return pl.pallas_call(
         functools.partial(states_kernel, by_head, features),
@@ -143,31 +149,36 @@
             running[tile] = fade * running[tile] + ends_ref[device, rows, :]
 
 
-def prior_states(payload):
+def prior_states(payload, beside):
     devices, height, _ = payload.shape
     height = height - TILE
     ends = lax.all_to_all(payload, SEQ, split_axis=0, concat_axis=0, tiled=True)
+    ends, beside = lax.optimization_barrier((ends, beside))
     prior = pl.pallas_call(
         prefix_kernel,
         out_shape=jax.ShapeDtypeStruct((devices, height, LANES), F32),
-        compiler_params=params(),
+        compiler_params=params(8),
         name="prefix",
     )(ends)
     prior = lax.all_to_all(prior, SEQ, split_axis=0, concat_axis=0, tiled=True)
-    return prior.reshape(devices * height, LANES)
-
-
-def read_state(read, state):
+    return prior.reshape(devices * height, LANES), beside
+
+
+def three_reads(read):
+    turned = jnp.transpose(read.astype(F32)).astype(BF16)
+    return jnp.concatenate([turned, turned, turned], axis=1)
+
+
+def read_state(reads, state):
     parts = jnp.concatenate(split_three(state), axis=0)
-    wide = jnp.concatenate([read, read, read], axis=0)
-    return lax.dot_general(wide, parts, (((0,), (0,)), ((), ())), preferred_element_type=F32)
+    return jnp.dot(reads, parts, preferred_element_type=F32)
 
 
 def local_kernel(by_head, features, *refs):
     if by_head:
-        x_ref, write_ref, read_ref, step_ref, decay_ref, squares_ref, before_ref, skip_ref, out_ref, lift_ref, total = refs
-    else:
-        x_ref, write_ref, read_ref, step_ref, decay_ref, before_ref, skip_ref, out_ref, lift_ref, total = refs
+        x_ref, write_ref, read_ref, step_ref, decay_ref, squares_ref, before_ref, skip_ref, out_ref, lift_ref, reads_ref, total = refs
+    else:
+        x_ref, write_ref, read_ref, step_ref, decay_ref, before_ref, skip_ref, out_ref, lift_ref, reads_ref, total = refs
     head_count = step_ref.shape[0]
     state_size = write_ref.shape[0]
     block = pl.program_id(0)
@@ -180,7 +191,7 @@
     cumulative = running_sums(decay_ref[...])
     step = step_ref[...]
     if by_head:
-        scale = norm_scale(squares_ref[...], features)
+        scale = block_scale(squares_ref, features)
         step = step * scale
         scale_column = jnp.transpose(jnp.broadcast_to(scale, (LANES, BLOCK)))
     padding = jnp.zeros((LANES - head_count, BLOCK), F32)
@@ -189,6 +200,8 @@
     lift_ref[...] = jnp.exp(jnp.transpose(whole))
     total[...] = total[...] + jnp.broadcast_to(cumulative[:, BLOCK - 1 :], (head_count, LANES))
     read = read_ref[...]
+    reads = three_reads(read)
+    reads_ref[...] = reads
     scores = lax.dot_general(read, write_ref[...], (((0,), (0,)), ((), ())), preferred_element_type=F32)
     first, last = slice(0, half), slice(half, BLOCK)
     causal = lax.broadcasted_iota(jnp.int32, (half, half), 0) >= lax.broadcasted_iota(
@@ -210,7 +223,7 @@
         both = jnp.concatenate([mixing(last, first), mixing(last, last)], axis=1)
         lower = jnp.dot(both, x, preferred_element_type=F32)
         state = before_ref[0, head * state_size : (head + 1) * state_size, :]
-        outputs = jnp.concatenate([upper, lower], axis=0) + jnp.exp(column) * read_state(read, state)
+        outputs = jnp.concatenate([upper, lower], axis=0) + jnp.exp(column) * read_state(reads, state)
         skipped = skip_ref[head] * x.astype(F32)
         if by_head:
             skipped = skipped * scale_column
@@ -230,7 +243,7 @@
     specs = [x_spec, along(state_size), along(state_size), along(head_count), along(head_count)]
     operands = [x, write, read, step, decay]
     if by_head:
-        specs.append(along(1))
+        specs.append(pl.BlockSpec((squares.shape[0] // blocks, squares.shape[1]), lambda k: (k, 0)))
         operands.append(squares)
     specs.append(pl.BlockSpec((1, head_count * state_size, LANES), lambda k: (k, 0, 0)))
     specs.append(pl.BlockSpec(memory_space=pltpu.SMEM))
@@ -243,10 +256,12 @@
         out_specs=[
             pl.BlockSpec((BLOCK, width), lambda k: (k, 0)),
             pl.BlockSpec((BLOCK, LANES), lambda k: (k, 0)),
+            pl.BlockSpec((BLOCK, 3 * state_size), lambda k: (k, 0)),
         ],
         out_shape=[
             jax.ShapeDtypeStruct((length, width), F32),
             jax.ShapeDtypeStruct((length, LANES), F32),
+            jax.ShapeDtypeStruct((length, 3 * state_size), BF16),
         ],
         scratch_shapes=[pltpu.VMEM((head_count, LANES), F32)],
         compiler_params=params(),
@@ -257,94 +272,117 @@
     )(*operands)
 
 
-def gated_kernel(first_layer, local_ref, lift_ref, read_ref, prior_ref, gate_ref, gain_ref, *refs):
+def gated_kernel(first_layer, groups, local_ref, lift_ref, reads_ref, prior_ref, gate_ref, gain_ref, *refs):
     if first_layer:
-        out_ref, squares_ref, total, staged = refs
+        out_ref, total, staged = refs
+        cols = out_ref.shape[0]
     else:
         out_ref, squares_ref, total = refs
     group = pl.program_id(0)
     length = local_ref.shape[0]
     heads = local_ref.shape[1] // LANES
-    state_size = read_ref.shape[0]
-    cols = out_ref.shape[0]
-    rows = length // cols
+    state_size = reads_ref.shape[1] // 3
 
     @pl.when(group == 0)
     def _():
         total[...] = jnp.zeros_like(total)
 
-    read = read_ref[...]
-    chosen = lax.broadcasted_iota(jnp.int32, (length, LANES), 1)
-    for head in range(heads):
-        place = slice(head * LANES, (head + 1) * LANES)
-        state = prior_ref[head * state_size : (head + 1) * state_size, :]
-        at = group * heads + head
-        lift = jnp.sum(jnp.where(chosen == at, lift_ref[...], 0.0), axis=1, keepdims=True)
-        outputs = local_ref[:, place] + lift * read_state(read, state)
-        gate = gate_ref[:, place].astype(F32)
-        gated = outputs * (gate / (1.0 + jnp.exp(-gate)))
-        total[...] += gated * gated
-        gated = gated * gain_ref[:, place]
+    @pl.when(group < groups)
+    def _():
+        reads = reads_ref[...]
+        lifts = pltpu.roll(lift_ref[...], lax.rem(LANES - group * heads, LANES), 1)
+        state = prior_ref[...]
+        states = [state[head * state_size : (head + 1) * state_size, :] for head in range(heads)]
+        from_state = read_state(reads, jnp.concatenate(states, axis=1))
+        for head in range(heads):
+            place = slice(head * LANES, (head + 1) * LANES)
+            outputs = local_ref[:, place] + lifts[:, head : head + 1] * from_state[:, place]
+            gate = gate_ref[:, place].astype(F32)
+            gated = outputs * (gate / (1.0 + jnp.exp(-gate)))
+            total[...] += gated * gated
+            gated = gated * gain_ref[:, place]
+            if first_layer:
+                rows = length // cols
+                staged[...] = gated
+                for col in range(cols):
+                    picked = staged[pl.ds(col, rows, stride=cols), :]
+                    out_ref[col, head * rows : (head + 1) * rows, :] = picked.astype(BF16)
+            else:
+                out_ref[:, place] = gated
+
+    @pl.when(group == pl.num_programs(0) - 1)
+    def _():
+        ordered = total[...]
         if first_layer:
-            staged[...] = gated
-            for col in range(cols):
-                picked = staged[pl.ds(col, rows, stride=cols), :]
-                out_ref[col, head * rows : (head + 1) * rows, :] = picked.astype(BF16)
-        else:
-            out_ref[:, place] = gated
-
-    @pl.when(group == pl.num_programs(0) - 1)
-    def _():
-        if first_layer:
+            rows = length // cols
             ordered = jnp.concatenate(
                 [total[pl.ds(col, rows, stride=cols), :] for col in range(cols)], axis=0
             )
-        else:
-            ordered = total[...]
         ones = jnp.ones((TILE, LANES), BF16)
         sums = jnp.zeros((TILE, length), F32)
         for part in split_three(ordered):
             sums = sums + lax.dot_general(
                 ones, part, (((1,), (1,)), ((), ())), preferred_element_type=F32
             )
-        squares_ref[...] = sums[:1]
-
-
-def gated_outputs(first_layer, local, lift, read, prior, gate, gain, cols):
+        if first_layer:
+            high, middle, low = [part.astype(F32) for part in split_three(sums)]
+            row = lax.broadcasted_iota(jnp.int32, (TILE, length), 0)
+            parts = jnp.where(row == 0, high, jnp.where(row == 1, middle, low))
+            parts = jnp.where(row < 3, parts, 0.0)
+            empty = jnp.zeros((EXTRA - TILE, LANES), F32)
+            for col in range(cols):
+                start = col * rows
+                inside = start % LANES
+                tile = parts[:, start - inside : start - inside + LANES]
+                if inside:
+                    tile = pltpu.roll(tile, LANES - inside, 1)
+                out_ref[col, :EXTRA, :] = jnp.concatenate([tile, empty], axis=0).astype(BF16)
+        else:
+            squares_ref[...] = sums[:1]
+
+
+def gated_outputs(first_layer, local, lift, reads, prior, gate, gain, cols):
     length, width = local.shape
-    state_size = read.shape[0]
     heads = HEADS_PER_STEP
     part = heads * LANES
     groups = width // part
+    state_size = reads.shape[1] // 3
+    at = lambda g: jnp.minimum(g, groups - 1)
     if first_layer:
         rows = length // cols
-        out_spec = pl.BlockSpec((cols, heads * rows, LANES), lambda g: (0, g, 0))
-        out_shape = jax.ShapeDtypeStruct((cols, width // LANES * rows, LANES), BF16)
+        out_specs = pl.BlockSpec((cols, heads * rows, LANES), lambda g: (0, g, 0))
+        out_shape = jax.ShapeDtypeStruct((cols, width // LANES * rows + EXTRA, LANES), BF16)
         scratch = [pltpu.VMEM((length, LANES), F32), pltpu.VMEM((length, LANES), F32)]
     else:
-        out_spec = pl.BlockSpec((length, part), lambda g: (0, g))
-        out_shape = jax.ShapeDtypeStruct((length, width), F32)
+        out_specs = [
+            pl.BlockSpec((length, part), lambda g: (0, g)),
+            pl.BlockSpec((1, length), lambda g: (0, 0)),
+        ]
+        out_shape = [
+            jax.ShapeDtypeStruct((length, width), F32),
+            jax.ShapeDtypeStruct((1, length), F32),
+        ]
         scratch = [pltpu.VMEM((length, LANES), F32)]
     return pl.pallas_call(
-        functools.partial(gated_kernel, first_layer),
-        grid=(groups,),
+        functools.partial(gated_kernel, first_layer, groups),
+        grid=(groups + 1 if first_layer else groups,),
         in_specs=[
-            pl.BlockSpec((length, part), lambda g: (0, g)),
+            pl.BlockSpec((length, part), lambda g: (0, at(g))),
             pl.BlockSpec((length, LANES), lambda g: (0, 0)),
-            pl.BlockSpec((state_size, length), lambda g: (0, 0)),
-            pl.BlockSpec((heads * state_size, LANES), lambda g: (g, 0)),
-            pl.BlockSpec((length, part), lambda g: (0, g)),
-            pl.BlockSpec((1, part), lambda g: (0, g)),
-        ],
-        out_specs=[out_spec, pl.BlockSpec((1, length), lambda g: (0, 0))],
-        out_shape=[out_shape, jax.ShapeDtypeStruct((1, length), F32)],
+            pl.BlockSpec((length, 3 * state_size), lambda g: (0, 0)),
+            pl.BlockSpec((heads * state_size, LANES), lambda g: (at(g), 0)),
+            pl.BlockSpec((length, part), lambda g: (0, at(g))),
+            pl.BlockSpec((1, part), lambda g: (0, at(g))),
+        ],
+        out_specs=out_specs,
+        out_shape=out_shape,
         scratch_shapes=scratch,
-        compiler_params=params(),
+        compiler_params=params(52),
         cost_estimate=pl.CostEstimate(
             flops=1_200_000_000, bytes_accessed=13_000_000, transcendentals=2_000_000
         ),
         name="gated",
-    )(local, lift, read, prior, gate, gain)
+    )(local, lift, reads, prior, gate, gain)
 
 
 def scaled_kernel(features, gated_ref, squares_ref, out_ref):
@@ -369,15 +407,6 @@
         compiler_params=params(),
         name="scaled",
     )(gated, squares)
-
-
-def column_squares(squares, devices):
-    whole = lax.psum(squares, "head")[0]
-    for axis in reversed(SEQ):
-        whole = lax.all_gather(whole, axis)
-    whole = whole.reshape(devices, devices, -1)
-    mine = lax.dynamic_index_in_dim(whole, lax.axis_index(SEQ), axis=1, keepdims=False)
-    return mine.reshape(1, -1)
 
 
 def body(
@@ -405,25 +434,26 @@
 
     x = tokens_in.reshape(tokens, width)
     payload, before = device_states(x, write_rows, step_rows, decay_rows, None, features, devices)
-    prior = prior_states(payload)
-    local, lift = local_outputs(
+    local = local_outputs(
         x, write_rows, read_rows, step_rows, decay_rows, None, before, skip_rows, features
     )
-    hidden, squares = gated_outputs(
-        True, local, lift, read_rows, prior, gate_rows.reshape(tokens, width), norm_rows[None], grid_cols
+    prior, local = prior_states(payload, local)
+    hidden = gated_outputs(
+        True, *local, prior, gate_rows.reshape(tokens, width), norm_rows[None], grid_cols
     )
     hidden = lax.all_to_all(hidden, SEQ, split_axis=0, concat_axis=0, tiled=True)
-    squares = column_squares(squares, devices)
+    squares = hidden[:, -EXTRA : 3 - EXTRA, :grid_rows].astype(F32)
+    squares = lax.psum(squares[:, 0] + squares[:, 1] + squares[:, 2], "head")
 
     payload, before = device_states(
         hidden, write_cols, step_cols, decay_cols, squares, features, devices
     )
-    prior = prior_states(payload)
-    local, lift = local_outputs(
+    local = local_outputs(
         hidden, write_cols, read_cols, step_cols, decay_cols, squares, before, skip_cols, features
     )
+    prior, local = prior_states(payload, local)
     gated, squares = gated_outputs(
-        False, local, lift, read_cols, prior, gate_cols.reshape(column_len, width), norm_cols[None], 1
+        False, *local, prior, gate_cols.reshape(column_len, width), norm_cols[None], 1
     )
     squares = lax.psum(squares, "head")
     out = scaled_outputs(gated, squares, features)

time: 222 us -> 180 us (0.81)
  local copies, waits for them, and re-layouts: 45.5 us -> 4.21 us
  Pallas kernels: 42.1 us -> 57.8 us
  blocking collectives: 82.7 us -> 69.6 us
  starting transfers between devices: 30.8 us -> 27.5 us
    all_to_all x0 -> x1, blocking collectives: none -> 43.1 us  [body(): lax.all_to_all(hidden, SEQ, split_axis=0, concat_axis=0, tiled=True)]
    unnamed x79 -> x14, local copies, waits for them, and re-layouts: 42.7 us -> 4.18 us
    all_gather x3 -> x0, blocking collectives: 29.4 us -> none  [column_squares(): whole = lax.all_gather(whole, axis)]
    psum x1, blocking collectives: 37.2 us -> 16 us  [body(): squares = lax.psum(squares[:, 0] + squares[:, 1] + squares[:, 2], 'head')]
    all_to_all x2, waiting for transfers between devices: 0.01 us -> 17.9 us  [prior_states(): prior = lax.all_to_all(prior, SEQ, split_axis=0, concat_axis=0, tiled=True)]
    all_to_all x2, waiting for transfers between devices: 19.4 us -> 1.63 us  [prior_states(): ends = lax.all_to_all(payload, SEQ, split_axis=0, concat_axis=0, tiled=True)]
    all_to_all x1 -> x0, starting transfers between devices: 7.85 us -> none  [body(): lax.all_to_all(hidden, SEQ, split_axis=0, concat_axis=0, tiled=True)]
    all_to_all x2, starting transfers between devices: 7.75 us -> 13.8 us  [prior_states(): prior = lax.all_to_all(prior, SEQ, split_axis=0, concat_axis=0, tiled=True)]
  transfers between devices with their start and end apart: 5 -> 4, of which waited for: 2 -> 4; matrix products, arithmetic and copies ran while one was open for 1% -> 0% of each run, Pallas kernels for 7% -> 11%
where the time goes in v2:
time: 180 us; the launch traced here: 179 us
  blocking collectives  69.6 us (39%)
  Pallas kernels  57.8 us (32%)
  starting transfers between devices  27.5 us (15%)
  waiting for transfers between devices  19.5 us (11%)
  local copies, waits for them, and re-layouts  4.21 us (2%)
    all_to_all x1, blocking collectives, body(): lax.all_to_all(hidden, SEQ, split_axis=0, concat_axis=0, tiled=True)  43.1 us
    pallas_call x2, Pallas kernels, gated_outputs(): pl.pallas_call(functools.partial(gated_kernel, first_layer, groups), grid...  21.1 us
    pallas_call x2, Pallas kernels, local_outputs(): pl.pallas_call(functools.partial(local_kernel, by_head, features), grid=(...  19.1 us
    all_to_all x2, waiting for transfers between devices, prior_states(): prior = lax.all_to_all(prior, SEQ, split_axis=0, concat_axis=0, tiled=True)  17.9 us
    psum x1, blocking collectives, body(): squares = lax.psum(squares[:, 0] + squares[:, 1] + squares[:, 2], 'head')  16 us
    all_to_all x2, starting transfers between devices, prior_states(): prior = lax.all_to_all(prior, SEQ, split_axis=0, concat_axis=0, tiled=True)  13.8 us
    all_to_all x2, starting transfers between devices, prior_states(): ends = lax.all_to_all(payload, SEQ, split_axis=0, concat_axis=0, tiled=True)  13.6 us
    pallas_call x2, Pallas kernels, device_states(): pl.pallas_call(functools.partial(states_kernel, by_head, features), grid=...  10.7 us
  transfers between devices with their start and end apart: 4, of which 4 were waited for; matrix products, arithmetic and copies ran while one was open for 0% of the time, Pallas kernels for 11%

profile of v2, /device:TPU:1, one launch (start us, length us, event | category | flops | bytes accessed | tf_op | source)
XLA Modules:
  0.0 178.7 jit_solution(7293219673688096006)
XLA Ops:
  0.0 5.3 %states.2 = (f32[32,32,128]{2,1,0:T(8,128)}, f32[4,768,128]{2,1,0:T(8,128)}) custom-call(bf16[1024,1536]{1,0:T(8,128)(2,1)} %bitcast.10, bf16[64,1024]{1,0:T(8,128)(2,1)} %refs_1_.5, f32[12,1024]{1,0:T(8,128)} %refs_3_.5, f32[12,1024]{1,0:T(8,128)} %refs_4_.2), custom_call_target="tpu_custom_call" | custom-call | flops 500000000 | bytes 6000000 | tf_op jit(solution)/shard_map/states/pallas_call | solution.py:119
  5.3 9.7 %all-to-all-start = ((f32[32,32,128]{2,1,0:T(8,128)}), f32[32,32,128]{2,1,0:T(8,128)S(1)}, u32[]{:S(2)}, u32[]{:S(2)}) async-start(f32[32,32,128]{2,1,0:T(8,128)} %get-tuple-element.25), calls=%async_computation | async-start | bytes 1048576 | tf_op jit(solution)/shard_map/all_to_all | solution.py:155
  15.1 0.0 copy-start.5
  15.1 9.6 %local.2 = (f32[1024,1536]{1,0:T(8,128)}, f32[1024,128]{1,0:T(8,128)}, bf16[1024,192]{1,0:T(8,128)(2,1)}) custom-call(bf16[1024,1536]{1,0:T(8,128)(2,1)} %bitcast.11, bf16[64,1024]{1,0:T(8,128)(2,1)} %refs_1_.5, bf16[64,1024]{1,0:T(8,128)(2,1)} %refs_2_.5, f32[12,1024]{1,0:T(8,128)} %refs_3_.5, f32[12,1024]{1,0:T(8,128)} %refs_4_.2, ...), custom_call_target="tpu_custom_call" | custom-call | flops 6000000000 | bytes 12000000 | tf_op jit(solution)/shard_map/local/pallas_call | solution.py:252
  24.7 1.1 all-to-all-done.ends_ref
  25.8 0.8 prefix.2
  26.6 6.7 %all-to-all-start.1 = ((f32[32,24,128]{2,1,0:T(8,128)}), f32[32,24,128]{2,1,0:T(8,128)S(1)}, u32[]{:S(2)}, u32[]{:S(2)}) async-start(f32[32,24,128]{2,1,0:T(8,128)} %prefix.2), calls=%async_computation.1 | async-start | bytes 786432 | tf_op jit(solution)/shard_map/all_to_all | solution.py:163
  33.3 0.0 copy-done.5
  33.3 8.9 %all-to-all-done.1 = f32[32,24,128]{2,1,0:T(8,128)S(1)} async-done(((f32[32,24,128]{2,1,0:T(8,128)}), f32[32,24,128]{2,1,0:T(8,128)S(1)}, u32[]{:S(2)}, u32[]{:S(2)}) %all-to-all-start.1) | async-done | bytes 393248 | tf_op jit(solution)/shard_map/all_to_all | solution.py:163
  42.2 0.0 copy-start.2
  42.2 1.0 copy-done.2
  43.2 0.0 copy-start.3
  43.2 1.0 copy-done.3
  44.3 11.4 %gated.2 = bf16[32,400,128]{2,1,0:T(8,128)(2,1)} custom-call(f32[1024,1536]{1,0:T(8,128)} %get-tuple-element.30.local_ref, f32[1024,128]{1,0:T(8,128)S(1)} %copy-done.2, bf16[1024,192]{1,0:T(8,128)(2,1)S(1)} %copy-done.3, f32[768,128]{1,0:T(8,128)S(1)} %bitcast.9, bf16[1024,1536]{1,0:T(8,128)(2,1)} %bitcast.12, f32[1,1536]{1,0:T(1,128)S(1)} %broadcast_in_dim.6.gain_ref), custom_call_target="tpu_custom_call" | custom-call | flops 1200000000 | bytes 13000000 | tf_op jit(solution)/shard_map/gated/pallas_call | solution.py:366
  55.7 43.1 %all_to_all.25.refs_0_ = bf16[32,400,128]{2,1,0:T(8,128)(2,1)S(1)} all-to-all(bf16[32,400,128]{2,1,0:T(8,128)(2,1)} %gated.2), channel_id=1, replica_groups=mesh['seq_0'=4,'seq_1'=4,'seq_2'=2,'head'=4] {'seq_0','seq_1','seq_2'}, dimensions={0} | all-to-all | bytes 6553600 | tf_op jit(solution)/shard_map/all_to_all | solution.py:444
  98.8 0.0 copy-start.4
  98.9 16.0 %psum.14.refs_4_.refs_5_ = f32[32,32]{1,0:T(8,128)} all-reduce(f32[32,32]{1,0:T(8,128)S(1)} %fusion), channel_id=1, replica_groups=mesh['seq_0'=4,'seq_1'=4,'seq_2'=2,'head'=4] {'head'}, use_global_device_ids=true, to_apply=%region_0.0 | all-reduce | flops 1024 | bytes 8192 | tf_op jit(solution)/shard_map/psum | solution.py:446
  114.9 0.0 copy-done.4
  114.9 5.4 %states.3 = (f32[32,32,128]{2,1,0:T(8,128)}, f32[4,768,128]{2,1,0:T(8,128)}) custom-call(bf16[32,400,128]{2,1,0:T(8,128)(2,1)} %copy-done.4, bf16[64,1024]{1,0:T(8,128)(2,1)} %refs_1_.7, f32[12,1024]{1,0:T(8,128)} %refs_3_.7, f32[12,1024]{1,0:T(8,128)} %refs_4_.3, f32[32,32]{1,0:T(8,128)} %psum.14.refs_4_.refs_5_), custom_call_target="tpu_custom_call" | custom-call | flops 500000000 | bytes 6000000 | tf_op jit(solution)/shard_map/states/pallas_call | solution.py:119
  120.2 3.9 %all-to-all-start.3 = ((f32[32,32,128]{2,1,0:T(8,128)}), f32[32,32,128]{2,1,0:T(8,128)S(1)}, u32[]{:S(2)}, u32[]{:S(2)}) async-start(f32[32,32,128]{2,1,0:T(8,128)} %get-tuple-element.34), calls=%async_computation.3 | async-start | bytes 1048576 | tf_op jit(solution)/shard_map/all_to_all | solution.py:155
  124.1 0.0 copy-start.6
  124.1 9.4 %local.3 = (f32[1024,1536]{1,0:T(8,128)}, f32[1024,128]{1,0:T(8,128)}, bf16[1024,192]{1,0:T(8,128)(2,1)}) custom-call(bf16[32,400,128]{2,1,0:T(8,128)(2,1)} %copy-done.4, bf16[64,1024]{1,0:T(8,128)(2,1)} %refs_1_.7, bf16[64,1024]{1,0:T(8,128)(2,1)} %refs_2_.7, f32[12,1024]{1,0:T(8,128)} %refs_3_.7, f32[12,1024]{1,0:T(8,128)} %refs_4_.3, ...), custom_call_target="tpu_custom_call" | custom-call | flops 6000000000 | bytes 12000000 | tf_op jit(solution)/shard_map/local/pallas_call | solution.py:252
  133.6 0.6 all-to-all-done.3.ends_ref
  134.1 0.8 prefix.3
  135.0 7.2 %all-to-all-start.4 = ((f32[32,24,128]{2,1,0:T(8,128)}), f32[32,24,128]{2,1,0:T(8,128)S(1)}, u32[]{:S(2)}, u32[]{:S(2)}) async-start(f32[32,24,128]{2,1,0:T(8,128)} %prefix.3), calls=%async_computation.4 | async-start | bytes 786432 | tf_op jit(solution)/shard_map/all_to_all | solution.py:163
  142.2 0.0 copy-done.6
  142.2 9.0 %all-to-all-done.4 = f32[32,24,128]{2,1,0:T(8,128)S(1)} async-done(((f32[32,24,128]{2,1,0:T(8,128)}), f32[32,24,128]{2,1,0:T(8,128)S(1)}, u32[]{:S(2)}, u32[]{:S(2)}) %all-to-all-start.4) | async-done | bytes 393248 | tf_op jit(solution)/shard_map/all_to_all | solution.py:163
  151.2 0.0 copy-start
  151.2 1.0 copy-done
  152.2 0.0 copy-start.1
  152.2 1.0 copy-done.1
  153.2 9.7 %gated.3 = (f32[1024,1536]{1,0:T(8,128)}, f32[1,1024]{1,0:T(1,128)S(1)}) custom-call(f32[1024,1536]{1,0:T(8,128)} %get-tuple-element.39.local_ref, f32[1024,128]{1,0:T(8,128)S(1)} %copy-done, bf16[1024,192]{1,0:T(8,128)(2,1)S(1)} %copy-done.1, f32[768,128]{1,0:T(8,128)S(1)} %bitcast.8, bf16[1024,1536]{1,0:T(8,128)(2,1)} %bitcast.13, ...), custom_call_target="tpu_custom_call" | custom-call | flops 1200000000 | bytes 13000000 | tf_op jit(solution)/shard_map/gated/pallas_call | solution.py:366
  163.0 10.5 %psum.15.squares_ref = f32[1,1024]{1,0:T(1,128)} all-reduce(f32[1,1024]{1,0:T(1,128)S(1)} %get-tuple-element.44), channel_id=1, replica_groups=mesh['seq_0'=4,'seq_1'=4,'seq_2'=2,'head'=4] {'head'}, use_global_device_ids=true, to_apply=%region_1.0 | all-reduce | flops 1024 | bytes 8192 | tf_op jit(solution)/shard_map/psum | solution.py:458
  173.4 5.2 %scaled.1 = bf16[1024,1536]{1,0:T(8,128)(2,1)} custom-call(f32[1024,1536]{1,0:T(8,128)} %get-tuple-element.43.gated_ref, f32[1,1024]{1,0:T(1,128)} %psum.15.squares_ref), custom_call_target="tpu_custom_call" | custom-call | tf_op jit(solution)/shard_map/scaled/pallas_call | solution.py:398
  (5 shorter events, 0.0 us)
Async XLA Ops:
  5.3 20.4 %all-to-all-start = ((f32[32,32,128]{2,1,0:T(8,128)}), f32[32,32,128]{2,1,0:T(8,128)S(1)}, u32[]{:S(2)}, u32[]{:S(2)}) async-start(f32[32,32,128]{2,1,0:T(8,128)} %get-tuple-element.25), calls=%async_computation | async-start | bytes 1048576 | tf_op jit(solution)/shard_map/all_to_all | solution.py:155
  15.1 18.2 %copy-start.5 = (f32[1536]{0:T(1024)S(1)}, f32[1536]{0:T(1024)}, u32[]{:S(2)}) copy-start(f32[1536]{0:T(1024)} %param.23) | copy-start | bytes 18436
  26.6 15.6 %all-to-all-start.1 = ((f32[32,24,128]{2,1,0:T(8,128)}), f32[32,24,128]{2,1,0:T(8,128)S(1)}, u32[]{:S(2)}, u32[]{:S(2)}) async-start(f32[32,24,128]{2,1,0:T(8,128)} %prefix.2), calls=%async_computation.1 | async-start | bytes 786432 | tf_op jit(solution)/shard_map/all_to_all | solution.py:163
  42.2 1.0 copy-start.2
  43.2 1.0 copy-start.3
  98.8 16.0 %copy-start.4 = (bf16[32,400,128]{2,1,0:T(8,128)(2,1)}, bf16[32,400,128]{2,1,0:T(8,128)(2,1)S(1)}, u32[]{:S(2)}) copy-start(bf16[32,400,128]{2,1,0:T(8,128)(2,1)S(1)} %all_to_all.25.refs_0_) | copy-start | bytes 9830404
  120.2 13.9 %all-to-all-start.3 = ((f32[32,32,128]{2,1,0:T(8,128)}), f32[32,32,128]{2,1,0:T(8,128)S(1)}, u32[]{:S(2)}, u32[]{:S(2)}) async-start(f32[32,32,128]{2,1,0:T(8,128)} %get-tuple-element.34), calls=%async_computation.3 | async-start | bytes 1048576 | tf_op jit(solution)/shard_map/all_to_all | solution.py:155
  124.1 18.0 %copy-start.6 = (f32[1536]{0:T(1024)S(1)}, f32[1536]{0:T(1024)}, u32[]{:S(2)}) copy-start(f32[1536]{0:T(1024)} %param.29) | copy-start | bytes 18436
  135.0 16.2 %all-to-all-start.4 = ((f32[32,24,128]{2,1,0:T(8,128)}), f32[32,24,128]{2,1,0:T(8,128)S(1)}, u32[]{:S(2)}, u32[]{:S(2)}) async-start(f32[32,24,128]{2,1,0:T(8,128)} %prefix.3), calls=%async_computation.4 | async-start | bytes 786432 | tf_op jit(solution)/shard_map/all_to_all | solution.py:163
  151.2 1.0 copy-start
  152.2 1.0 copy-start.1

commit v3 on v2

v3 whole, which is shorter than its diff:
```python
import functools

import jax
import jax.numpy as jnp
from jax import lax
from jax.experimental import pallas as pl
from jax.experimental.pallas import tpu as pltpu
from jax.sharding import Mesh
from jax.sharding import PartitionSpec as P

BLOCK = 256
SEQ = ("seq_0", "seq_1", "seq_2")
EPSILON = 1e-05
LANES = 128
TILE = 8
HEADS_PER_STEP = 2
EXTRA = 16
CHUNK = 128
PITCH = 40
OWN_TYPE = jnp.float32
FACTOR_TYPE = jnp.bfloat16
LAST_TYPE = jnp.float32
SCALED_ROWS = 128
STATES_MB = (56, 48)
MEGABYTE = 1024 * 1024
F32 = jnp.float32
BF16 = jnp.bfloat16


def params(megabytes=56):
    return pltpu.CompilerParams(vmem_limit_bytes=megabytes * MEGABYTE)


def split_three(value):
    high = value.astype(BF16)
    rest = value - high.astype(F32)
    middle = rest.astype(BF16)
    low = (rest - middle.astype(F32)).astype(BF16)
    return high, middle, low


def split_two(value):
    high = value.astype(BF16)
    return high, (value - high.astype(F32)).astype(BF16)


def running_sums(decay):
    length = decay.shape[1]
    earlier = lax.broadcasted_iota(jnp.int32, (length, length), 0)
    later = lax.broadcasted_iota(jnp.int32, (length, length), 1)
    upper = jnp.where(earlier <= later, 1.0, 0.0).astype(BF16)
    high, middle, low = split_three(decay)
    total = jnp.dot(low, upper, preferred_element_type=F32)
    total = total + jnp.dot(middle, upper, preferred_element_type=F32)
    return total + jnp.dot(high, upper, preferred_element_type=F32)


def norm_scale(squares, features):
    return lax.rsqrt(squares / features + EPSILON)


def head_inputs(x_ref, head, by_head):
    if by_head:
        rows = BLOCK // x_ref.shape[0]
        return x_ref[:, head * rows : (head + 1) * rows, :].reshape(BLOCK, LANES)
    return x_ref[:, head * LANES : (head + 1) * LANES]


def block_scale(squares_ref, features):
    squares = squares_ref[...]
    pieces = [squares[device : device + 1, :] for device in range(squares.shape[0])]
    return norm_scale(jnp.concatenate(pieces, axis=1), features)


HBM = pl.BlockSpec(memory_space=pltpu.HBM)
VMEM = pl.BlockSpec(memory_space=pltpu.VMEM)


def silu(value):
    below = 1.0 + jnp.exp(-value)
    inverse = pl.reciprocal(below, approx=True)
    return value * (inverse * (2.0 - below * inverse))


def states_kernel(by_head, features, x_ref, write_hbm, step_hbm, decay_hbm, *refs):
    if by_head:
        squares_ref, gain_ref, payload_hbm, before_hbm, write_ref, step_ref, decay_ref, before, payload, total, sent, got = refs
    else:
        payload_hbm, before_hbm, x_in, write_ref, step_ref, decay_ref, before, payload, total, sent, got = refs
    head_count = step_ref.shape[0]
    state_size = write_ref.shape[0]
    blocks = before.shape[0] - 1
    pairs = ((decay_hbm, decay_ref), (step_hbm, step_ref), (write_hbm, write_ref))
    small = [pltpu.make_async_copy(*pair, got.at[at]) for at, pair in enumerate(pairs)]

    def x_copy(block):
        rows = pl.ds(pl.multiple_of(block * BLOCK, BLOCK), BLOCK)
        return pltpu.make_async_copy(x_ref.at[rows], x_in.at[block], got.at[3 + block])

    def before_copy(block):
        return pltpu.make_async_copy(before.at[block], before_hbm.at[block], sent.at[block])

    for copy in small:
        copy.start()
    if not by_head:
        for block in range(blocks):
            x_copy(block).start()
    before[0] = jnp.zeros(before.shape[1:], F32)
    total[...] = jnp.zeros_like(total)
    for copy in small:
        copy.wait()

    def advance(block, carry):
        positions = pl.ds(pl.multiple_of(block * BLOCK, BLOCK), BLOCK)
        before_copy(block).start()
        cumulative = running_sums(decay_ref[:, positions])
        final = cumulative[:, BLOCK - 1 :]
        weights = jnp.exp(final - cumulative) * step_ref[:, positions]
        if by_head:
            devices = BLOCK // squares_ref.shape[1]
            at = pl.ds(pl.multiple_of(block * devices, devices), devices)
            weights = weights * block_scale(squares_ref[at, :], features)
            x_block = x_ref.at[at]
        else:
            x_copy(block).wait()
            x_block = x_in.at[block]
        fading = jnp.broadcast_to(jnp.exp(final), (head_count, LANES))
        write = write_ref[:, positions].astype(F32)
        for head in range(head_count):
            loaded = (write * weights[head : head + 1, :]).astype(BF16)
            gained = jnp.dot(loaded, head_inputs(x_block, head, by_head), preferred_element_type=F32)
            if by_head:
                gained = gained * gain_ref[:, head * LANES : (head + 1) * LANES]
            rows = slice(head * state_size, (head + 1) * state_size)
            before[block + 1, rows, :] = fading[head : head + 1, :] * before[block, rows, :] + gained
        total[...] = total[...] + jnp.broadcast_to(final, (head_count, LANES))
        return carry

    lax.fori_loop(0, blocks, advance, 0)
    devices, height = payload.shape[0], payload.shape[1] - TILE
    payload[:, :height, :] = before[blocks].reshape(devices, height, LANES)
    for device in range(devices):
        for tile in range(height // TILE):
            head = (device * height + tile * TILE) // state_size
            payload[device, height + tile : height + tile + 1, :] = total[head : head + 1, :]
        left = height + height // TILE
        payload[device, left:, :] = jnp.zeros((height + TILE - left, LANES), F32)
    out = pltpu.make_async_copy(payload, payload_hbm, sent.at[blocks])
    out.start()
    for block in range(blocks):
        before_copy(block).wait()
    out.wait()


def device_states(x, write, step, decay, squares, gain, features, devices):
    head_count, length = step.shape
    state_size = write.shape[0]
    blocks = length // BLOCK
    height = head_count * state_size // devices
    by_head = squares is not None
    specs = [VMEM if by_head else HBM, HBM, HBM, HBM]
    operands = [x, write, step, decay]
    scratch = []
    if by_head:
        specs += [VMEM, VMEM]
        operands += [squares, gain]
    else:
        scratch.append(pltpu.VMEM((blocks, BLOCK, x.shape[1]), BF16))
    return pl.pallas_call(
        functools.partial(states_kernel, by_head, features),
        in_specs=specs,
        out_specs=[HBM, HBM],
        out_shape=[
            jax.ShapeDtypeStruct((devices, height + TILE, LANES), F32),
            jax.ShapeDtypeStruct((blocks, head_count * state_size, LANES), F32),
        ],
        scratch_shapes=scratch
        + [
            pltpu.VMEM(write.shape, BF16),
            pltpu.VMEM(step.shape, F32),
            pltpu.VMEM(decay.shape, F32),
            pltpu.VMEM((blocks + 1, head_count * state_size, LANES), F32),
            pltpu.VMEM((devices, height + TILE, LANES), F32),
            pltpu.VMEM((head_count, LANES), F32),
            pltpu.SemaphoreType.DMA((blocks + 1,)),
            pltpu.SemaphoreType.DMA((3 + blocks,)),
        ],
        compiler_params=params(STATES_MB[by_head]),
        cost_estimate=pl.CostEstimate(flops=500_000_000, bytes_accessed=6_000_000, transcendentals=20_000),
        name="states",
    )(*operands)


def prefix_kernel(ends_ref, prior_ref):
    devices, height, _ = prior_ref.shape
    running = [jnp.zeros((TILE, LANES), F32) for _ in range(height // TILE)]
    for device in range(devices):
        for tile in range(height // TILE):
            rows = slice(tile * TILE, (tile + 1) * TILE)
            prior_ref[device, rows, :] = running[tile]
            fade = jnp.exp(ends_ref[device, height + tile : height + tile + 1, :])
            running[tile] = fade * running[tile] + ends_ref[device, rows, :]


def prior_states(payload, beside):
    devices, height, _ = payload.shape
    height = height - TILE
    ends = lax.all_to_all(payload, SEQ, split_axis=0, concat_axis=0, tiled=True)
    ends, beside = lax.optimization_barrier((ends, beside))
    prior = pl.pallas_call(
        prefix_kernel,
        out_shape=jax.ShapeDtypeStruct((devices, height, LANES), F32),
        compiler_params=params(8),
        name="prefix",
    )(ends)
    prior = lax.all_to_all(prior, SEQ, split_axis=0, concat_axis=0, tiled=True)
    return prior.reshape(devices * height, LANES), beside


def read_state(reads, state):
    parts = jnp.concatenate(split_two(state), axis=0)
    return jnp.dot(reads, parts, preferred_element_type=F32)


def local_kernel(by_head, features, *refs):
    if by_head:
        x_ref, write_ref, read_ref, step_ref, decay_ref, squares_ref, gain_ref, before_ref, skip_ref, out_ref, total = refs
    else:
        x_ref, write_ref, read_ref, step_ref, decay_ref, before_ref, skip_ref, out_ref, total = refs
    head_count = step_ref.shape[0]
    state_size = write_ref.shape[0]
    block = pl.program_id(0)
    half = BLOCK // 2

    @pl.when(block == 0)
    def _():
        total[...] = jnp.zeros_like(total)

    cumulative = running_sums(decay_ref[...])
    step = step_ref[...]
    if by_head:
        scale = block_scale(squares_ref, features)
        step = step * scale
        scale_column = jnp.transpose(jnp.broadcast_to(scale, (LANES, BLOCK)))
    padding = jnp.zeros((LANES - head_count, BLOCK), F32)
    columns = jnp.transpose(jnp.concatenate([cumulative, padding], axis=0))
    whole = jnp.concatenate([cumulative + total[:, :1], padding], axis=0)
    lift = jnp.exp(jnp.transpose(whole))
    total[...] = total[...] + jnp.broadcast_to(cumulative[:, BLOCK - 1 :], (head_count, LANES))
    read = read_ref[...]
    turned = jnp.transpose(read.astype(F32))
    reads = jnp.concatenate([turned, turned], axis=1).astype(BF16)
    out_ref[:, head_count * LANES :] = jnp.concatenate([lift[:, : LANES - state_size], turned], axis=1)
    scores = lax.dot_general(read, write_ref[...], (((0,), (0,)), ((), ())), preferred_element_type=F32)
    first, last = slice(0, half), slice(half, BLOCK)
    causal = lax.broadcasted_iota(jnp.int32, (half, half), 0) >= lax.broadcasted_iota(
        jnp.int32, (half, half), 1
    )
    for head in range(head_count):
        row = cumulative[head : head + 1, :]
        column = jnp.broadcast_to(columns[:, head : head + 1], (BLOCK, LANES))
        weight = step[head : head + 1, :]

        def mixing(t, s):
            spread = column[t] - row[:, s]
            if t == s:
                spread = jnp.where(causal, spread, -jnp.inf)
            return (jnp.exp(spread) * scores[t, s] * weight[:, s]).astype(BF16)

        x = head_inputs(x_ref, head, by_head)
        upper = jnp.dot(mixing(first, first), x[first], preferred_element_type=F32)
        both = jnp.concatenate([mixing(last, first), mixing(last, last)], axis=1)
        lower = jnp.dot(both, x, preferred_element_type=F32)
        state = before_ref[0, head * state_size : (head + 1) * state_size, :]
        place = slice(head * LANES, (head + 1) * LANES)
        skipped = skip_ref[head] * x.astype(F32)
        outputs = jnp.concatenate([upper, lower], axis=0)
        if by_head:
            outputs = (outputs + skipped * scale_column) * gain_ref[:, place]
        else:
            outputs = outputs + skipped
        out_ref[:, place] = outputs + jnp.exp(column) * read_state(reads, state)


def local_outputs(x, write, read, step, decay, squares, gain, before, skip, features):
    head_count, length = step.shape
    state_size = write.shape[0]
    blocks = length // BLOCK
    by_head = squares is not None
    if by_head:
        x_spec = pl.BlockSpec((x.shape[0] // blocks, *x.shape[1:]), lambda k: (k, 0, 0))
    else:
        x_spec = pl.BlockSpec((BLOCK, x.shape[1]), lambda k: (k, 0))
    along = lambda rows: pl.BlockSpec((rows, BLOCK), lambda k: (0, k))
    specs = [x_spec, along(state_size), along(state_size), along(head_count), along(head_count)]
    operands = [x, write, read, step, decay]
    if by_head:
        specs.append(pl.BlockSpec((squares.shape[0] // blocks, squares.shape[1]), lambda k: (k, 0)))
        specs.append(pl.BlockSpec((1, gain.shape[1]), lambda k: (0, 0)))
        operands += [squares, gain]
    specs.append(pl.BlockSpec((1, head_count * state_size, LANES), lambda k: (k, 0, 0)))
    specs.append(pl.BlockSpec(memory_space=pltpu.SMEM))
    operands += [before, skip]
    width = (head_count + 1) * LANES
    return pl.pallas_call(
        functools.partial(local_kernel, by_head, features),
        grid=(blocks,),
        in_specs=specs,
        out_specs=pl.BlockSpec((BLOCK, width), lambda k: (k, 0)),
        out_shape=jax.ShapeDtypeStruct((length, width), F32),
        scratch_shapes=[pltpu.VMEM((head_count, LANES), F32)],
        compiler_params=params(),
        cost_estimate=pl.CostEstimate(
            flops=6_000_000_000, bytes_accessed=12_000_000, transcendentals=3_000_000
        ),
        name="local",
    )(*operands)


def factors_kernel(local_hbm, gate_hbm, own_hbm, factor_hbm, local_in, side, gate_in, own, own_side, factor, sent, got):
    groups, length, width = local_in.shape
    heads = width // LANES

    def lanes(group):
        return pl.ds(pl.multiple_of(group * width, width), width)

    def local_copy(group):
        return pltpu.make_async_copy(local_hbm.at[:, lanes(group)], local_in.at[group], got.at[group])

    def gate_copy(group):
        return pltpu.make_async_copy(gate_hbm.at[:, lanes(group)], gate_in.at[group], got.at[groups + group])

    def own_copy(group):
        return pltpu.make_async_copy(own.at[group], own_hbm.at[:, lanes(group)], sent.at[group])

    def factor_copy(group):
        return pltpu.make_async_copy(factor.at[group], factor_hbm.at[:, lanes(group)], sent.at[groups + group])

    beside = pl.ds(groups * width, LANES)
    side_copy = pltpu.make_async_copy(local_hbm.at[:, beside], side, got.at[2 * groups])
    own_side_copy = pltpu.make_async_copy(own_side, own_hbm.at[:, beside], sent.at[2 * groups])
    side_copy.start()
    for group in range(groups):
        local_copy(group).start()
        gate_copy(group).start()
    side_copy.wait()
    lane = lax.broadcasted_iota(jnp.int32, (length, LANES), 1)
    reads = jnp.where(lane < LANES // 2, pltpu.roll(side[...], LANES // 2, 1), side[...])
    own_side[...] = reads.astype(own_side.dtype)
    own_side_copy.start()

    def advance(group, carry):
        lifts = pltpu.roll(side[...], lax.rem(LANES - group * heads, LANES), 1)
        local_copy(group).wait()
        gate_copy(group).wait()
        for start in range(0, length, CHUNK):
            chunk = slice(start, start + CHUNK)
            for head in range(heads):
                place = slice(head * LANES, (head + 1) * LANES)
                gate = silu(gate_in[group, chunk, place].astype(F32))
                own[group, chunk, place] = (local_in[group, chunk, place] * gate).astype(own.dtype)
                factor[group, chunk, place] = (lifts[chunk, head : head + 1] * gate).astype(factor.dtype)
        own_copy(group).start()
        factor_copy(group).start()
        return carry

    lax.fori_loop(0, groups, advance, 0)
    own_side_copy.wait()
    for group in range(groups):
        own_copy(group).wait()
        factor_copy(group).wait()


def output_factors(local, gate):
    length, width = gate.shape
    part = HEADS_PER_STEP * LANES
    groups = width // part
    return pl.pallas_call(
        factors_kernel,
        in_specs=[HBM, HBM],
        out_specs=[HBM, HBM],
        out_shape=[
            jax.ShapeDtypeStruct((length, width + LANES), OWN_TYPE),
            jax.ShapeDtypeStruct((length, width), FACTOR_TYPE),
        ],
        scratch_shapes=[
            pltpu.VMEM((groups, length, part), F32),
            pltpu.VMEM((length, LANES), F32),
            pltpu.VMEM((groups, length, part), BF16),
            pltpu.VMEM((groups, length, part), OWN_TYPE),
            pltpu.VMEM((length, LANES), OWN_TYPE),
            pltpu.VMEM((groups, length, part), FACTOR_TYPE),
            pltpu.SemaphoreType.DMA((2 * groups + 1,)),
            pltpu.SemaphoreType.DMA((2 * groups + 1,)),
        ],
        compiler_params=params(),
        cost_estimate=pl.CostEstimate(
            flops=100_000_000, bytes_accessed=20_000_000, transcendentals=3_000_000
        ),
        name="factors",
    )(local, gate)


def gated_kernel(first_layer, own_hbm, factor_hbm, prior_ref, *refs):
    if first_layer:
        out_hbm, own, factor, side, out_in, total, sent, got, staged, extra = refs
        cols = out_hbm.shape[0]
    else:
        out_hbm, squares_ref, own, factor, side, out_in, total, sent, got = refs
    groups, length, width = own.shape
    heads = width // LANES
    state_size = LANES // 2

    def lanes(group):
        return pl.ds(pl.multiple_of(group * width, width), width)

    def own_copy(group):
        return pltpu.make_async_copy(own_hbm.at[:, lanes(group)], own.at[group], got.at[group])

    def factor_copy(group):
        return pltpu.make_async_copy(factor_hbm.at[:, lanes(group)], factor.at[group], got.at[groups + group])

    def out_copy(group):
        if first_layer:
            rows = out_in.shape[2]
            place = out_hbm.at[:, pl.ds(pl.multiple_of(group * rows, rows), rows), :]
        else:
            place = out_hbm.at[:, lanes(group)]
        return pltpu.make_async_copy(out_in.at[group], place, sent.at[group])

    side_copy = pltpu.make_async_copy(own_hbm.at[:, pl.ds(groups * width, LANES)], side, got.at[2 * groups])
    side_copy.start()
    for group in range(groups):
        own_copy(group).start()
        factor_copy(group).start()
    total[...] = jnp.zeros_like(total)
    side_copy.wait()

    def advance(group, carry):
        depth = heads * state_size
        state = prior_ref[pl.ds(pl.multiple_of(group * depth, depth), depth), :]
        states = [state[head * state_size : (head + 1) * state_size, :] for head in range(heads)]
        parts = jnp.concatenate(split_two(jnp.concatenate(states, axis=1)), axis=0)
        own_copy(group).wait()
        factor_copy(group).wait()
        for start in range(0, length, CHUNK):
            chunk = slice(start, start + CHUNK)
            from_state = jnp.dot(side[chunk, :].astype(BF16), parts, preferred_element_type=F32)
            squares = total[chunk, :]
            for head in range(heads):
                place = slice(head * LANES, (head + 1) * LANES)
                gated = own[group, chunk, place].astype(F32)
                gated = gated + factor[group, chunk, place].astype(F32) * from_state[:, place]
                squares = squares + gated * gated
                if first_layer:
                    for row in range(CHUNK // cols):
                        pitched = pl.ds((start // cols + row) * PITCH, cols)
                        staged[head, pitched, :] = gated[row * cols : (row + 1) * cols, :]
                else:
                    out_in[group, chunk, place] = gated.astype(out_in.dtype)
            total[chunk, :] = squares
        if first_layer:
            rows = length // cols
            for head in range(heads):
                for col in range(cols):
                    picked = staged[head, pl.ds(col, rows, stride=PITCH), :]
                    out_in[group, col, head * rows : (head + 1) * rows, :] = picked.astype(BF16)
        out_copy(group).start()
        return carry

    lax.fori_loop(0, groups, advance, 0)
    ordered = total[...]
    if first_layer:
        rows = length // cols
        ordered = jnp.concatenate([total[pl.ds(col, rows, stride=cols), :] for col in range(cols)], axis=0)
    ones = jnp.ones((TILE, LANES), BF16)
    sums = jnp.zeros((TILE, length), F32)
    for part in split_three(ordered):
        sums = sums + lax.dot_general(ones, part, (((1,), (1,)), ((), ())), preferred_element_type=F32)
    if first_layer:
        high, middle, low = [part.astype(F32) for part in split_three(sums)]
        row = lax.broadcasted_iota(jnp.int32, (TILE, length), 0)
        parts = jnp.where(row == 0, high, jnp.where(row == 1, middle, low))
        parts = jnp.where(row < 3, parts, 0.0)
        empty = jnp.zeros((EXTRA - TILE, LANES), F32)
        for col in range(cols):
            start = col * rows
            inside = start % LANES
            tile = parts[:, start - inside : start - inside + LANES]
            if inside:
                tile = pltpu.roll(tile, LANES - inside, 1)
            extra[col, :, :] = jnp.concatenate([tile, empty], axis=0).astype(BF16)
        last = out_hbm.at[:, pl.ds(out_hbm.shape[1] - EXTRA, EXTRA), :]
        extra_copy = pltpu.make_async_copy(extra, last, sent.at[groups])
        extra_copy.start()
        extra_copy.wait()
    else:
        squares_ref[...] = sums[:1]
    for group in range(groups):
        out_copy(group).wait()


def gated_outputs(first_layer, own, factor, prior, cols):
    length, width = factor.shape
    heads = HEADS_PER_STEP
    part = heads * LANES
    groups = width // part
    scratch = [
        pltpu.VMEM((groups, length, part), own.dtype),
        pltpu.VMEM((groups, length, part), factor.dtype),
        pltpu.VMEM((length, LANES), own.dtype),
    ]
    last = [
        pltpu.VMEM((length, LANES), F32),
        pltpu.SemaphoreType.DMA((groups + 1,)),
        pltpu.SemaphoreType.DMA((2 * groups + 1,)),
    ]
    if first_layer:
        rows = length // cols
        out_specs = HBM
        out_shape = jax.ShapeDtypeStruct((cols, width // LANES * rows + EXTRA, LANES), BF16)
        scratch.append(pltpu.VMEM((groups, cols, heads * rows, LANES), BF16))
        last += [pltpu.VMEM((heads, rows * PITCH, LANES), F32), pltpu.VMEM((cols, EXTRA, LANES), BF16)]
    else:
        out_specs = [HBM, VMEM]
        out_shape = [
            jax.ShapeDtypeStruct((length, width), LAST_TYPE),
            jax.ShapeDtypeStruct((1, length), F32),
        ]
        scratch.append(pltpu.VMEM((groups, length, part), LAST_TYPE))
    return pl.pallas_call(
        functools.partial(gated_kernel, first_layer),
        in_specs=[HBM, HBM, VMEM],
        out_specs=out_specs,
        out_shape=out_shape,
        scratch_shapes=scratch + last,
        compiler_params=params(52),
        cost_estimate=pl.CostEstimate(
            flops=1_200_000_000, bytes_accessed=13_000_000, transcendentals=2_000_000
        ),
        name="gated",
    )(own, factor, prior)


def scaled_kernel(features, gated_hbm, squares_ref, gain_ref, out_hbm, gated_in, out_in, sent, got):
    parts, rows, width = gated_in.shape

    def gated_copy(part):
        place = pl.ds(pl.multiple_of(part * rows, rows), rows)
        return pltpu.make_async_copy(gated_hbm.at[place], gated_in.at[part], got.at[part])

    def out_copy(part):
        place = pl.ds(pl.multiple_of(part * rows, rows), rows)
        return pltpu.make_async_copy(out_in.at[part], out_hbm.at[place], sent.at[part])

    for part in range(parts):
        gated_copy(part).start()

    def advance(part, carry):
        squares = squares_ref[:, pl.ds(pl.multiple_of(part * rows, rows), rows)]
        scale = norm_scale(squares, features)
        column = jnp.transpose(jnp.broadcast_to(scale, (LANES, rows)))
        gated_copy(part).wait()
        for head in range(width // LANES):
            place = slice(head * LANES, (head + 1) * LANES)
            gated = gated_in[part, :, place].astype(F32) * column
            out_in[part, :, place] = (gated * gain_ref[:, place]).astype(BF16)
        out_copy(part).start()
        return carry

    lax.fori_loop(0, parts, advance, 0)
    for part in range(parts):
        out_copy(part).wait()


def scaled_outputs(gated, squares, gain, features):
    length, width = gated.shape
    parts = length // SCALED_ROWS
    return pl.pallas_call(
        functools.partial(scaled_kernel, features),
        in_specs=[HBM, VMEM, VMEM],
        out_specs=HBM,
        out_shape=jax.ShapeDtypeStruct((length, width), BF16),
        scratch_shapes=[
            pltpu.VMEM((parts, SCALED_ROWS, width), gated.dtype),
            pltpu.VMEM((parts, SCALED_ROWS, width), BF16),
            pltpu.SemaphoreType.DMA((parts,)),
            pltpu.SemaphoreType.DMA((parts,)),
        ],
        compiler_params=params(),
        name="scaled",
    )(gated, squares, gain)


def body(
    tokens_in,
    gate_rows,
    gate_cols,
    write_rows,
    read_rows,
    step_rows,
    decay_rows,
    skip_rows,
    norm_rows,
    write_cols,
    read_cols,
    step_cols,
    decay_cols,
    skip_cols,
    norm_cols,
):
    grid_rows, grid_cols, width = tokens_in.shape
    devices = lax.axis_size(SEQ)
    features = float(width * lax.axis_size("head"))
    tokens = grid_rows * grid_cols
    column_len = gate_cols.shape[0]

    x = tokens_in.reshape(tokens, width)
    payload, before = device_states(x, write_rows, step_rows, decay_rows, None, None, features, devices)
    local = local_outputs(
        x, write_rows, read_rows, step_rows, decay_rows, None, None, before, skip_rows, features
    )
    prior, local = prior_states(payload, local)
    hidden = gated_outputs(
        True, *output_factors(local, gate_rows.reshape(tokens, width)), prior, grid_cols
    )
    hidden = lax.all_to_all(hidden, SEQ, split_axis=0, concat_axis=0, tiled=True)
    squares = hidden[:, -EXTRA : 3 - EXTRA, :grid_rows].astype(F32)
    squares = lax.psum(squares[:, 0] + squares[:, 1] + squares[:, 2], "head")

    payload, before = device_states(
        hidden, write_cols, step_cols, decay_cols, squares, norm_rows[None], features, devices
    )
    local = local_outputs(
        hidden, write_cols, read_cols, step_cols, decay_cols, squares, norm_rows[None], before, skip_cols, features
    )
    prior, local = prior_states(payload, local)
    gated, squares = gated_outputs(
        False, *output_factors(local, gate_cols.reshape(column_len, width)), prior, 1
    )
    squares = lax.psum(squares, "head")
    out = scaled_outputs(gated, squares, norm_cols[None], features)
    return out.reshape(column_len, 1, width)


def solution(mesh):
    torus = Mesh(
        mesh.devices.reshape(4, 4, 2, mesh.shape["head"]), ("seq_0", "seq_1", "seq_2", "head")
    )
    return jax.shard_map(
        body,
        mesh=torus,
        in_specs=(
            P(SEQ, None, "head"),
            P(SEQ, None, "head"),
            P(None, SEQ, "head"),
            P(None, SEQ),
            P(None, SEQ),
            P("head", SEQ),
            P("head", SEQ),
            P("head"),
            P("head"),
            P(None, SEQ),
            P(None, SEQ),
            P("head", SEQ),
            P("head", SEQ),
            P("head"),
            P("head"),
        ),
        out_specs=P(None, SEQ, "head"),
        check_vma=False,
    )
```

time: 180 us -> 178 us (0.989)
  blocking collectives: 69.6 us -> 27.6 us
  waiting for transfers between devices: 19.5 us -> 43 us
  starting transfers between devices: 27.5 us -> 37.2 us
  Pallas kernels: 57.8 us -> 64.4 us
    all_to_all x1 -> x0, blocking collectives: 43.1 us -> none  [body(): lax.all_to_all(hidden, SEQ, split_axis=0, concat_axis=0, tiled=True)]
    all_to_all x0 -> x1, waiting for transfers between devices: none -> 40.7 us  [body(): lax.all_to_all(hidden, SEQ, split_axis=0, concat_axis=0, tiled=True)]
    all_to_all x2, waiting for transfers between devices: 17.9 us -> 0.86 us  [prior_states(): prior = lax.all_to_all(prior, SEQ, split_axis=0, concat_axis=0, tiled=True)]
    all_to_all x0 -> x1, starting transfers between devices: none -> 7.1 us  [body(): lax.all_to_all(hidden, SEQ, split_axis=0, concat_axis=0, tiled=True)]
    pallas_call x5 -> x7, Pallas kernels: 37.1 us -> 42.9 us  [the longest x2 16.3 us: output_factors(): pl.pallas_call(factors_kernel, in_specs=[HBM, HBM], out_specs=[HBM, HBM],...]
    all_to_all x2, starting transfers between devices: 13.6 us -> 16.1 us  [prior_states(): ends = lax.all_to_all(payload, SEQ, split_axis=0, concat_axis=0, tiled=True)]
    unnamed x14 -> x20, local copies, waits for them, and re-layouts: 4.18 us -> 2.67 us
  transfers between devices with their start and end apart: 4 -> 5, of which waited for: 4 -> 4; matrix products, arithmetic and copies ran while one was open for 0% -> 1% of each run, Pallas kernels for 11% -> 20%
where the time goes in v3:
time: 178 us; the launch traced here: 177 us
  Pallas kernels  64.4 us (36%)
  waiting for transfers between devices  43 us (24%)
  starting transfers between devices  37.2 us (21%)
  blocking collectives  27.6 us (16%)
  local copies, waits for them, and re-layouts  3.88 us (2%)
    all_to_all x1, waiting for transfers between devices, body(): lax.all_to_all(hidden, SEQ, split_axis=0, concat_axis=0, tiled=True)  40.7 us
    pallas_call x2, Pallas kernels, local_outputs(): pl.pallas_call(functools.partial(local_kernel, by_head, features), grid=(...  18.8 us
    pallas_call x2, Pallas kernels, output_factors(): pl.pallas_call(factors_kernel, in_specs=[HBM, HBM], out_specs=[HBM, HBM],...  16.3 us
    all_to_all x2, starting transfers between devices, prior_states(): ends = lax.all_to_all(payload, SEQ, split_axis=0, concat_axis=0, tiled=True)  16.1 us
    psum x1, blocking collectives, body(): squares = lax.psum(squares[:, 0] + squares[:, 1] + squares[:, 2], 'head')  15.5 us
    all_to_all x2, starting transfers between devices, prior_states(): prior = lax.all_to_all(prior, SEQ, split_axis=0, concat_axis=0, tiled=True)  13.9 us
    pallas_call x2, Pallas kernels, gated_outputs(): pl.pallas_call(functools.partial(gated_kernel, first_layer), in_specs=[HB...  13.5 us
    psum x1, blocking collectives, body(): squares = lax.psum(squares, 'head')  12 us
  transfers between devices with their start and end apart: 5, of which 4 were waited for; matrix products, arithmetic and copies ran while one was open for 1% of the time, Pallas kernels for 20%

profile of v3, /device:TPU:1, one launch (start us, length us, event | category | flops | bytes accessed | tf_op | source)
XLA Modules:
  0.0 176.9 jit_solution(10731332013345282738)
XLA Ops:
  0.0 4.4 %states.2 = (f32[32,32,128]{2,1,0:T(8,128)}, f32[4,768,128]{2,1,0:T(8,128)}) custom-call(bf16[1024,1536]{1,0:T(8,128)(2,1)} %bitcast.12, bf16[64,1024]{1,0:T(8,128)(2,1)} %refs_1_.2, f32[12,1024]{1,0:T(8,128)} %refs_3_.2, f32[12,1024]{1,0:T(8,128)} %refs_4_.2), custom_call_target="tpu_custom_call" | custom-call | flops 500000000 | bytes 6000000 | tf_op jit(solution)/shard_map/states/pallas_call | solution.py:169
  4.4 9.7 %all-to-all-start = ((f32[32,32,128]{2,1,0:T(8,128)}), f32[32,32,128]{2,1,0:T(8,128)S(1)}, u32[]{:S(2)}, u32[]{:S(2)}) async-start(f32[32,32,128]{2,1,0:T(8,128)} %get-tuple-element.19), calls=%async_computation | async-start | bytes 1048576 | tf_op jit(solution)/shard_map/all_to_all | solution.py:208
  14.1 9.3 %local.2.local_hbm = f32[1024,1664]{1,0:T(8,128)} custom-call(bf16[1024,1536]{1,0:T(8,128)(2,1)} %bitcast.13, bf16[64,1024]{1,0:T(8,128)(2,1)} %refs_1_.2, bf16[64,1024]{1,0:T(8,128)(2,1)} %refs_2_.2, f32[12,1024]{1,0:T(8,128)} %refs_3_.2, f32[12,1024]{1,0:T(8,128)} %refs_4_.2, f32[4,768,128]{2,1,0:T(8,128)} %get-tuple-element.20.refs_5_, f32[12]{0:T(128)} %refs_6_.1), custom_call_target="tpu_custom_call" | custom-call | flops 6000000000 | bytes 12000000 | tf_op jit(solution)/shard_map/local/pallas_call | solution.py:305
  23.4 1.4 all-to-all-done.ends_ref
  24.8 0.8 prefix.2
  25.7 6.3 %all-to-all-start.1 = ((f32[32,24,128]{2,1,0:T(8,128)}), f32[32,24,128]{2,1,0:T(8,128)S(1)}, u32[]{:S(2)}, u32[]{:S(2)}) async-start(f32[32,24,128]{2,1,0:T(8,128)} %prefix.2), calls=%async_computation.1 | async-start | bytes 786432 | tf_op jit(solution)/shard_map/all_to_all | solution.py:216
  32.0 8.2 %factors.2 = (f32[1024,1664]{1,0:T(8,128)}, bf16[1024,1536]{1,0:T(8,128)(2,1)}) custom-call(f32[1024,1664]{1,0:T(8,128)} %local.2.local_hbm, bf16[1024,1536]{1,0:T(8,128)(2,1)} %bitcast.10), custom_call_target="tpu_custom_call" | custom-call | flops 100000000 | bytes 20000000 | tf_op jit(solution)/shard_map/factors/pallas_call | solution.py:378
  40.1 0.8 all-to-all-done.1
  40.9 6.5 %gated.2 = bf16[32,400,128]{2,1,0:T(8,128)(2,1)} custom-call(f32[1024,1664]{1,0:T(8,128)} %get-tuple-element.22.own_hbm, bf16[1024,1536]{1,0:T(8,128)(2,1)} %get-tuple-element.23.factor_hbm, f32[768,128]{1,0:T(8,128)S(1)} %bitcast.9), custom_call_target="tpu_custom_call" | custom-call | flops 1200000000 | bytes 13000000 | tf_op jit(solution)/shard_map/gated/pallas_call | solution.py:531
  47.4 0.0 copy-start.8
  47.4 0.0 copy-start.2
  47.4 0.0 copy-start.4
  47.4 0.0 copy-start.5
  47.4 7.1 %all-to-all-start.2 = ((bf16[32,400,128]{2,1,0:T(8,128)(2,1)}), bf16[32,400,128]{2,1,0:T(8,128)(2,1)S(1)}, u32[]{:S(2)}, u32[]{:S(2)}) async-start(bf16[32,400,128]{2,1,0:T(8,128)(2,1)} %gated.2), calls=%async_computation.2 | async-start | bytes 6553600 | tf_op jit(solution)/shard_map/all_to_all | solution.py:627
  54.6 0.0 copy-done.8
  54.6 0.6 broadcast_in_dim.7.refs_1_.refs_6_
  55.2 40.7 %all-to-all-done.2.x_ref.refs_0_ = bf16[32,400,128]{2,1,0:T(8,128)(2,1)S(1)} async-done(((bf16[32,400,128]{2,1,0:T(8,128)(2,1)}), bf16[32,400,128]{2,1,0:T(8,128)(2,1)S(1)}, u32[]{:S(2)}, u32[]{:S(2)}) %all-to-all-start.2) | async-done | bytes 3276832 | tf_op jit(solution)/shard_map/all_to_all | solution.py:627
  95.9 0.0 copy-start
  95.9 0.7 fusion
  96.6 15.5 %psum.14.refs_0_.refs_5_ = f32[32,32]{1,0:T(8,128)S(1)} all-reduce(f32[32,32]{1,0:T(8,128)} %fusion), channel_id=1, replica_groups=mesh['seq_0'=4,'seq_1'=4,'seq_2'=2,'head'=4] {'head'}, use_global_device_ids=true, to_apply=%region_0.0 | all-reduce | flops 1024 | bytes 8192 | tf_op jit(solution)/shard_map/psum | solution.py:629
  112.1 0.0 copy-done.2
  112.1 0.0 copy-done.4
  112.1 0.0 copy-done.5
  112.2 0.0 copy-start.6
  112.2 0.7 copy-done.6
  112.8 0.0 copy-start.3
  112.9 3.6 %states.3 = (f32[32,32,128]{2,1,0:T(8,128)S(1)}, f32[4,768,128]{2,1,0:T(8,128)S(1)}) custom-call(bf16[32,400,128]{2,1,0:T(8,128)(2,1)S(1)} %all-to-all-done.2.x_ref.refs_0_, bf16[64,1024]{1,0:T(8,128)(2,1)S(1)} %copy-done.2, f32[12,1024]{1,0:T(8,128)S(1)} %copy-done.4, f32[12,1024]{1,0:T(8,128)S(1)} %copy-done.5, f32[32,32]{1,0:T(8,128)S(1)} %psum.14.refs_0_.refs_5_, ...), custom_call_target="tpu_custom_call" | custom-call | flops 500000000 | bytes 6000000 | tf_op jit(solution)/shard_map/states/pallas_call | solution.py:169
  116.5 0.0 copy-start.1
  116.5 0.8 copy-done.1
  117.3 0.0 copy-start.7
  117.3 1.1 copy-done.7
  118.4 6.4 %all-to-all-start.3 = ((f32[32,32,128]{2,1,0:T(8,128)}), f32[32,32,128]{2,1,0:T(8,128)}, u32[]{:S(2)}, u32[]{:S(2)}) async-start(f32[32,32,128]{2,1,0:T(8,128)} %copy-done.1), calls=%async_computation.3 | async-start | bytes 1048576 | tf_op jit(solution)/shard_map/all_to_all | solution.py:208
  124.8 0.0 copy-done
  124.9 0.0 copy-done.3
  124.9 0.0 copy-start.9
  124.9 9.5 %local.3.local_hbm = f32[1024,1664]{1,0:T(8,128)} custom-call(bf16[32,400,128]{2,1,0:T(8,128)(2,1)} %copy-done, bf16[64,1024]{1,0:T(8,128)(2,1)} %refs_1_.3, bf16[64,1024]{1,0:T(8,128)(2,1)} %refs_2_.3, f32[12,1024]{1,0:T(8,128)} %refs_3_.3, f32[12,1024]{1,0:T(8,128)} %refs_4_.3, f32[32,32]{1,0:T(8,128)} %copy-done.3, ...), custom_call_target="tpu_custom_call" | custom-call | flops 6000000000 | bytes 12000000 | tf_op jit(solution)/shard_map/local/pallas_call | solution.py:305
  134.4 0.0 all-to-all-done.3.ends_ref
  134.4 1.9 %prefix.3 = f32[32,24,128]{2,1,0:T(8,128)} custom-call(f32[32,32,128]{2,1,0:T(8,128)} %all-to-all-done.3.ends_ref), custom_call_target="tpu_custom_call" | custom-call | tf_op jit(solution)/shard_map/prefix/pallas_call | solution.py:210
  136.3 7.7 %all-to-all-start.4 = ((f32[32,24,128]{2,1,0:T(8,128)}), f32[32,24,128]{2,1,0:T(8,128)S(1)}, u32[]{:S(2)}, u32[]{:S(2)}) async-start(f32[32,24,128]{2,1,0:T(8,128)} %prefix.3), calls=%async_computation.4 | async-start | bytes 786432 | tf_op jit(solution)/shard_map/all_to_all | solution.py:216
  143.9 0.0 copy-done.9
  143.9 0.6 broadcast_in_dim.8.gain_ref
  144.5 8.1 %factors.3 = (f32[1024,1664]{1,0:T(8,128)}, bf16[1024,1536]{1,0:T(8,128)(2,1)}) custom-call(f32[1024,1664]{1,0:T(8,128)} %local.3.local_hbm, bf16[1024,1536]{1,0:T(8,128)(2,1)} %bitcast.11), custom_call_target="tpu_custom_call" | custom-call | flops 100000000 | bytes 20000000 | tf_op jit(solution)/shard_map/factors/pallas_call | solution.py:378
  152.7 0.1 all-to-all-done.4
  152.8 7.0 %gated.3 = (f32[1024,1536]{1,0:T(8,128)}, f32[1,1024]{1,0:T(1,128)S(1)}) custom-call(f32[1024,1664]{1,0:T(8,128)} %get-tuple-element.28.own_hbm, bf16[1024,1536]{1,0:T(8,128)(2,1)} %get-tuple-element.29.factor_hbm, f32[768,128]{1,0:T(8,128)S(1)} %bitcast.8), custom_call_target="tpu_custom_call" | custom-call | flops 1200000000 | bytes 13000000 | tf_op jit(solution)/shard_map/gated/pallas_call | solution.py:531
  159.7 12.0 %psum.15.squares_ref = f32[1,1024]{1,0:T(1,128)} all-reduce(f32[1,1024]{1,0:T(1,128)S(1)} %get-tuple-element.32), channel_id=1, replica_groups=mesh['seq_0'=4,'seq_1'=4,'seq_2'=2,'head'=4] {'head'}, use_global_device_ids=true, to_apply=%region_1.0 | all-reduce | flops 1024 | bytes 8192 | tf_op jit(solution)/shard_map/psum | solution.py:641
  171.8 5.2 %scaled.1 = bf16[1024,1536]{1,0:T(8,128)(2,1)} custom-call(f32[1024,1536]{1,0:T(8,128)} %get-tuple-element.31.gated_hbm, f32[1,1024]{1,0:T(1,128)} %psum.15.squares_ref, f32[1,1536]{1,0:T(1,128)} %broadcast_in_dim.8.gain_ref), custom_call_target="tpu_custom_call" | custom-call | tf_op jit(solution)/shard_map/scaled/pallas_call | solution.py:579
  (2 shorter events, 0.0 us)
Async XLA Ops:
  4.4 20.5 %all-to-all-start = ((f32[32,32,128]{2,1,0:T(8,128)}), f32[32,32,128]{2,1,0:T(8,128)S(1)}, u32[]{:S(2)}, u32[]{:S(2)}) async-start(f32[32,32,128]{2,1,0:T(8,128)} %get-tuple-element.19), calls=%async_computation | async-start | bytes 1048576 | tf_op jit(solution)/shard_map/all_to_all | solution.py:208
  25.7 15.2 %all-to-all-start.1 = ((f32[32,24,128]{2,1,0:T(8,128)}), f32[32,24,128]{2,1,0:T(8,128)S(1)}, u32[]{:S(2)}, u32[]{:S(2)}) async-start(f32[32,24,128]{2,1,0:T(8,128)} %prefix.2), calls=%async_computation.1 | async-start | bytes 786432 | tf_op jit(solution)/shard_map/all_to_all | solution.py:216
  47.4 7.2 %copy-start.8 = (f32[1536]{0:T(1024)S(1)}, f32[1536]{0:T(1024)}, u32[]{:S(2)}) copy-start(f32[1536]{0:T(1024)} %param.23) | copy-start | bytes 18436
  47.4 64.7 %copy-start.2 = (bf16[64,1024]{1,0:T(8,128)(2,1)S(1)}, bf16[64,1024]{1,0:T(8,128)(2,1)}, u32[]{:S(2)}) copy-start(bf16[64,1024]{1,0:T(8,128)(2,1)} %refs_1_.3) | copy-start | bytes 393220
  47.4 64.7 %copy-start.4 = (f32[12,1024]{1,0:T(8,128)S(1)}, f32[12,1024]{1,0:T(8,128)}, u32[]{:S(2)}) copy-start(f32[12,1024]{1,0:T(8,128)} %refs_3_.3) | copy-start | bytes 147460
  47.4 64.7 %copy-start.5 = (f32[12,1024]{1,0:T(8,128)S(1)}, f32[12,1024]{1,0:T(8,128)}, u32[]{:S(2)}) copy-start(f32[12,1024]{1,0:T(8,128)} %refs_4_.3) | copy-start | bytes 147460
  47.4 48.5 %all-to-all-start.2 = ((bf16[32,400,128]{2,1,0:T(8,128)(2,1)}), bf16[32,400,128]{2,1,0:T(8,128)(2,1)S(1)}, u32[]{:S(2)}, u32[]{:S(2)}) async-start(bf16[32,400,128]{2,1,0:T(8,128)(2,1)} %gated.2), calls=%async_computation.2 | async-start | bytes 6553600 | tf_op jit(solution)/shard_map/all_to_all | solution.py:627
  95.9 28.9 %copy-start = (bf16[32,400,128]{2,1,0:T(8,128)(2,1)}, bf16[32,400,128]{2,1,0:T(8,128)(2,1)S(1)}, u32[]{:S(2)}) copy-start(bf16[32,400,128]{2,1,0:T(8,128)(2,1)S(1)} %all-to-all-done.2.x_ref.refs_0_) | copy-start | bytes 9830404
  112.2 0.7 copy-start.6
  112.8 12.0 %copy-start.3 = (f32[32,32]{1,0:T(8,128)}, f32[32,32]{1,0:T(8,128)S(1)}, u32[]{:S(2)}) copy-start(f32[32,32]{1,0:T(8,128)S(1)} %psum.14.refs_0_.refs_5_) | copy-start | bytes 12292
  116.5 0.8 copy-start.1
  117.3 1.1 copy-start.7
  118.4 15.9 %all-to-all-start.3 = ((f32[32,32,128]{2,1,0:T(8,128)}), f32[32,32,128]{2,1,0:T(8,128)}, u32[]{:S(2)}, u32[]{:S(2)}) async-start(f32[32,32,128]{2,1,0:T(8,128)} %copy-done.1), calls=%async_computation.3 | async-start | bytes 1048576 | tf_op jit(solution)/shard_map/all_to_all | solution.py:208
  124.9 19.1 %copy-start.9 = (f32[1536]{0:T(1024)S(1)}, f32[1536]{0:T(1024)}, u32[]{:S(2)}) copy-start(f32[1536]{0:T(1024)} %param.29) | copy-start | bytes 18436
  136.3 16.5 %all-to-all-start.4 = ((f32[32,24,128]{2,1,0:T(8,128)}), f32[32,24,128]{2,1,0:T(8,128)S(1)}, u32[]{:S(2)}, u32[]{:S(2)}) async-start(f32[32,24,128]{2,1,0:T(8,128)} %prefix.3), calls=%async_computation.4 | async-start | bytes 786432 | tf_op jit(solution)/shard_map/all_to_all | solution.py:216

commit v4 on v3

v4 whole, which is shorter than its diff:
```python
import functools

import jax
import jax.numpy as jnp
from jax import lax
from jax.experimental import pallas as pl
from jax.experimental.pallas import tpu as pltpu
from jax.sharding import Mesh
from jax.sharding import PartitionSpec as P

BLOCK = 256
SEQ = ("seq_0", "seq_1", "seq_2")
EPSILON = 1e-05
LANES = 128
TILE = 8
HEADS_PER_STEP = 2
EXTRA = 16
CHUNK = 128
PITCH = 40
LOG2E = 1.4426950408889634
OWN_TYPE = jnp.float32
FACTOR_TYPE = jnp.bfloat16
LAST_TYPE = jnp.bfloat16
SCALED_ROWS = 128
GATED_MB = (49, 52)
MEGABYTE = 1024 * 1024
F32 = jnp.float32
BF16 = jnp.bfloat16


def params(megabytes=56):
    return pltpu.CompilerParams(vmem_limit_bytes=megabytes * MEGABYTE)


def split_three(value):
    high = value.astype(BF16)
    rest = value - high.astype(F32)
    middle = rest.astype(BF16)
    low = (rest - middle.astype(F32)).astype(BF16)
    return high, middle, low


def split_two(value):
    high = value.astype(BF16)
    return high, (value - high.astype(F32)).astype(BF16)


def running_sums(decay):
    length = decay.shape[1]
    earlier = lax.broadcasted_iota(jnp.int32, (length, length), 0)
    later = lax.broadcasted_iota(jnp.int32, (length, length), 1)
    upper = jnp.where(earlier <= later, 1.0, 0.0).astype(BF16)
    high, middle, low = split_three(decay)
    total = jnp.dot(low, upper, preferred_element_type=F32)
    total = total + jnp.dot(middle, upper, preferred_element_type=F32)
    return total + jnp.dot(high, upper, preferred_element_type=F32)


def norm_scale(squares, features):
    return lax.rsqrt(squares / features + EPSILON)


def head_inputs(x_ref, head, by_head):
    if by_head:
        rows = BLOCK // x_ref.shape[0]
        return x_ref[:, head * rows : (head + 1) * rows, :].reshape(BLOCK, LANES)
    return x_ref[:, head * LANES : (head + 1) * LANES]


def block_scale(squares_ref, block, features):
    rows = BLOCK // LANES
    squares = squares_ref[pl.ds(block * rows, rows), :]
    pieces = [squares[row : row + 1, :] for row in range(rows)]
    return norm_scale(jnp.concatenate(pieces, axis=1), features)


HBM = pl.BlockSpec(memory_space=pltpu.HBM)
VMEM = pl.BlockSpec(memory_space=pltpu.VMEM)


def silu(value):
    return value * pl.reciprocal(1.0 + jnp.exp(-value), approx=True)


def states_kernel(by_head, features, x_ref, write_hbm, step_hbm, decay_hbm, *refs):
    if by_head:
        squares_ref, gain_hbm, payload_hbm, before_hbm, gain_ref, x_in, write_ref, step_ref, decay_ref, before, payload, total, sent, got = refs
    else:
        payload_hbm, before_hbm, x_in, write_ref, step_ref, decay_ref, before, payload, total, sent, got = refs
    head_count = step_ref.shape[0]
    state_size = write_ref.shape[0]
    blocks = before.shape[0] - 1
    pairs = ((decay_hbm, decay_ref), (step_hbm, step_ref), (write_hbm, write_ref))
    if by_head:
        pairs += ((gain_hbm, gain_ref),)
    small = [pltpu.make_async_copy(*pair, got.at[at]) for at, pair in enumerate(pairs)]

    def x_copy(block):
        rows = x_in.shape[1]
        place = pl.ds(pl.multiple_of(block * rows, rows), rows)
        return pltpu.make_async_copy(x_ref.at[place], x_in.at[block], got.at[len(pairs) + block])

    def before_copy(block):
        return pltpu.make_async_copy(before.at[block], before_hbm.at[block], sent.at[block])

    for copy in small:
        copy.start()
    for block in range(blocks):
        x_copy(block).start()
    before[0] = jnp.zeros(before.shape[1:], F32)
    total[...] = jnp.zeros_like(total)
    for copy in small:
        copy.wait()

    def advance(block, carry):
        positions = pl.ds(pl.multiple_of(block * BLOCK, BLOCK), BLOCK)
        before_copy(block).start()
        cumulative = running_sums(decay_ref[:, positions])
        final = cumulative[:, BLOCK - 1 :]
        weights = jnp.exp(final - cumulative) * step_ref[:, positions]
        if by_head:
            weights = weights * block_scale(squares_ref, block, features)
        x_copy(block).wait()
        x_block = x_in.at[block]
        fading = jnp.broadcast_to(jnp.exp(final), (head_count, LANES))
        write = write_ref[:, positions].astype(F32)
        for head in range(head_count):
            loaded = (write * weights[head : head + 1, :]).astype(BF16)
            gained = jnp.dot(loaded, head_inputs(x_block, head, by_head), preferred_element_type=F32)
            if by_head:
                gained = gained * gain_ref[:, head * LANES : (head + 1) * LANES]
            rows = slice(head * state_size, (head + 1) * state_size)
            before[block + 1, rows, :] = fading[head : head + 1, :] * before[block, rows, :] + gained
        total[...] = total[...] + jnp.broadcast_to(final, (head_count, LANES))
        return carry

    lax.fori_loop(0, blocks, advance, 0)
    devices, height = payload.shape[0], payload.shape[1] - TILE
    payload[:, :height, :] = before[blocks].reshape(devices, height, LANES)
    for device in range(devices):
        for tile in range(height // TILE):
            head = (device * height + tile * TILE) // state_size
            payload[device, height + tile : height + tile + 1, :] = total[head : head + 1, :]
        left = height + height // TILE
        payload[device, left:, :] = jnp.zeros((height + TILE - left, LANES), F32)
    out = pltpu.make_async_copy(payload, payload_hbm, sent.at[blocks])
    out.start()
    for block in range(blocks):
        before_copy(block).wait()
    out.wait()


def device_states(x, write, step, decay, squares, gain, features, devices):
    head_count, length = step.shape
    state_size = write.shape[0]
    blocks = length // BLOCK
    height = head_count * state_size // devices
    by_head = squares is not None
    specs = [HBM] * 4
    operands = [x, write, step, decay]
    scratch = []
    if by_head:
        specs += [VMEM, HBM]
        operands += [squares, gain]
        scratch.append(pltpu.VMEM(gain.shape, F32))
    scratch.append(pltpu.VMEM((blocks, x.shape[0] // blocks, *x.shape[1:]), BF16))
    return pl.pallas_call(
        functools.partial(states_kernel, by_head, features),
        in_specs=specs,
        out_specs=[HBM, HBM],
        out_shape=[
            jax.ShapeDtypeStruct((devices, height + TILE, LANES), F32),
            jax.ShapeDtypeStruct((blocks, head_count * state_size, LANES), F32),
        ],
        scratch_shapes=scratch
        + [
            pltpu.VMEM(write.shape, BF16),
            pltpu.VMEM(step.shape, F32),
            pltpu.VMEM(decay.shape, F32),
            pltpu.VMEM((blocks + 1, head_count * state_size, LANES), F32),
            pltpu.VMEM((devices, height + TILE, LANES), F32),
            pltpu.VMEM((head_count, LANES), F32),
            pltpu.SemaphoreType.DMA((blocks + 1,)),
            pltpu.SemaphoreType.DMA((4 + blocks,)),
        ],
        compiler_params=params(),
        cost_estimate=pl.CostEstimate(flops=500_000_000, bytes_accessed=6_000_000, transcendentals=20_000),
        name="states",
    )(*operands)


def prefix_kernel(ends_ref, prior_ref):
    devices, height, _ = prior_ref.shape
    running = [jnp.zeros((TILE, LANES), F32) for _ in range(height // TILE)]
    for device in range(devices):
        for tile in range(height // TILE):
            rows = slice(tile * TILE, (tile + 1) * TILE)
            prior_ref[device, rows, :] = running[tile]
            fade = jnp.exp(ends_ref[device, height + tile : height + tile + 1, :])
            running[tile] = fade * running[tile] + ends_ref[device, rows, :]


def prior_states(payload, beside, later):
    devices, height, _ = payload.shape
    height = height - TILE
    ends = lax.all_to_all(payload, SEQ, split_axis=0, concat_axis=0, tiled=True)
    ends, beside, later = lax.optimization_barrier((ends, beside, later))
    prior = pl.pallas_call(
        prefix_kernel,
        out_shape=jax.ShapeDtypeStruct((devices, height, LANES), F32),
        compiler_params=params(8),
        name="prefix",
    )(ends)
    prior = lax.all_to_all(prior, SEQ, split_axis=0, concat_axis=0, tiled=True)
    return prior.reshape(devices * height, LANES), beside, later


def read_state(reads, state):
    parts = jnp.concatenate(split_two(state), axis=0)
    return jnp.dot(reads, parts, preferred_element_type=F32)


def local_kernel(by_head, features, first, *refs):
    x_ref, write_ref, read_ref, step_ref, decay_ref, gate_ref, before_ref, skip_ref = refs[:8]
    if by_head:
        squares_ref, gain_ref = refs[8:10]
    own_ref, factor_ref, total = refs[-3:]
    head_count = step_ref.shape[0]
    state_size = write_ref.shape[0]
    half = BLOCK // 2
    block = first + pl.program_id(0)

    @pl.when(pl.program_id(0) == 0)
    def _():
        total[...] = jnp.zeros_like(total)
        if first:
            earlier = jnp.sum(decay_ref[:, : first * BLOCK], axis=1, keepdims=True)
            total[...] = jnp.broadcast_to(earlier, total.shape)

    cumulative = running_sums(decay_ref[:, pl.ds(pl.multiple_of(block * BLOCK, BLOCK), BLOCK)])
    step = step_ref[...]
    if by_head:
        scale = block_scale(squares_ref, block, features)
        step = step * scale
        scale_column = jnp.transpose(jnp.broadcast_to(scale, (LANES, BLOCK)))
    padding = jnp.zeros((LANES - head_count, BLOCK), F32)
    columns = jnp.transpose(jnp.concatenate([cumulative, padding], axis=0))
    lifts = jnp.exp(columns)
    columns = columns * LOG2E
    lowered = (cumulative - jnp.log(step)) * LOG2E
    kept = jnp.exp(total[...])
    total[...] = total[...] + jnp.broadcast_to(cumulative[:, BLOCK - 1 :], (head_count, LANES))
    read = read_ref[...]
    turned = jnp.transpose(read.astype(F32))
    reads = jnp.concatenate([turned, turned], axis=1)
    own_ref[:, head_count * LANES :] = reads.astype(own_ref.dtype)
    reads = reads.astype(BF16)
    scores = lax.dot_general(read, write_ref[...], (((0,), (0,)), ((), ())), preferred_element_type=F32)
    first_half, last_half = slice(0, half), slice(half, BLOCK)
    causal = lax.broadcasted_iota(jnp.int32, (half, half), 0) >= lax.broadcasted_iota(
        jnp.int32, (half, half), 1
    )
    for head in range(head_count):
        row = lowered[head : head + 1, :]
        column = jnp.broadcast_to(columns[:, head : head + 1], (BLOCK, LANES))

        def mixing(t, s):
            spread = column[t] - row[:, s]
            if t == s:
                spread = jnp.where(causal, spread, -jnp.inf)
            return (jnp.exp2(spread) * scores[t, s]).astype(BF16)

        x = head_inputs(x_ref, head, by_head)
        upper = jnp.dot(mixing(first_half, first_half), x[first_half], preferred_element_type=F32)
        both = jnp.concatenate([mixing(last_half, first_half), mixing(last_half, last_half)], axis=1)
        lower = jnp.dot(both, x, preferred_element_type=F32)
        state = before_ref[0, head * state_size : (head + 1) * state_size, :]
        place = slice(head * LANES, (head + 1) * LANES)
        skipped = skip_ref[head] * x.astype(F32)
        outputs = jnp.concatenate([upper, lower], axis=0)
        if by_head:
            outputs = (outputs + skipped * scale_column) * gain_ref[:, place]
        else:
            outputs = outputs + skipped
        lift = jnp.broadcast_to(lifts[:, head : head + 1], (BLOCK, LANES))
        outputs = outputs + lift * read_state(reads, state)
        gate = silu(gate_ref[:, place].astype(F32))
        own_ref[:, place] = (outputs * gate).astype(own_ref.dtype)
        factor_ref[:, place] = (lift * kept[head : head + 1, :] * gate).astype(factor_ref.dtype)


def local_factors(first, count, x, write, read, step, decay, gate, squares, gain, before, skip, features, done):
    head_count, length = step.shape
    state_size = write.shape[0]
    blocks = length // BLOCK
    width = head_count * LANES
    by_head = squares is not None
    if by_head:
        x_spec = pl.BlockSpec((x.shape[0] // blocks, *x.shape[1:]), lambda k: (first + k, 0, 0))
    else:
        x_spec = pl.BlockSpec((BLOCK, width), lambda k: (first + k, 0))
    along = lambda rows: pl.BlockSpec((rows, BLOCK), lambda k: (0, first + k))
    specs = [
        x_spec,
        along(state_size),
        along(state_size),
        along(head_count),
        pl.BlockSpec((head_count, length), lambda k: (0, 0)),
        pl.BlockSpec((BLOCK, width), lambda k: (first + k, 0)),
        pl.BlockSpec((1, head_count * state_size, LANES), lambda k: (first + k, 0, 0)),
        pl.BlockSpec(memory_space=pltpu.SMEM),
    ]
    operands = [x, write, read, step, decay, gate, before, skip]
    if by_head:
        specs.append(pl.BlockSpec(squares.shape, lambda k: (0, 0)))
        specs.append(pl.BlockSpec((1, width), lambda k: (0, 0)))
        operands += [squares, gain]
    aliases = {len(operands) + at: at for at in range(len(done))}
    return pl.pallas_call(
        functools.partial(local_kernel, by_head, features, first),
        grid=(count,),
        in_specs=specs + [HBM] * len(done),
        input_output_aliases=aliases,
        out_specs=[
            pl.BlockSpec((BLOCK, width + LANES), lambda k: (first + k, 0)),
            pl.BlockSpec((BLOCK, width), lambda k: (first + k, 0)),
        ],
        out_shape=[
            jax.ShapeDtypeStruct((length, width + LANES), OWN_TYPE),
            jax.ShapeDtypeStruct((length, width), FACTOR_TYPE),
        ],
        scratch_shapes=[pltpu.VMEM((head_count, LANES), F32)],
        compiler_params=params(),
        cost_estimate=pl.CostEstimate(
            flops=3_000_000_000, bytes_accessed=10_000_000, transcendentals=3_000_000
        ),
        name="local",
    )(*operands, *done)


def gated_kernel(first_layer, own_hbm, factor_hbm, prior_ref, *refs):
    if first_layer:
        out_hbm, own, factor, side, out_in, total, sent, got, staged, extra = refs
        cols = out_hbm.shape[0]
    else:
        out_ref, squares_ref, own, factor, side, total, got = refs
    groups, length, width = own.shape
    heads = width // LANES
    state_size = LANES // 2

    def lanes(group):
        return pl.ds(pl.multiple_of(group * width, width), width)

    def in_copies(group):
        own_copy = pltpu.make_async_copy(own_hbm.at[:, lanes(group)], own.at[group], got.at[group])
        at = groups + group
        return own_copy, pltpu.make_async_copy(factor_hbm.at[:, lanes(group)], factor.at[group], got.at[at])

    beside = pl.ds(groups * width, LANES)
    side_copy = pltpu.make_async_copy(own_hbm.at[:, beside], side, got.at[2 * groups])

    def out_copy(group):
        rows = out_in.shape[2]
        place = out_hbm.at[:, pl.ds(pl.multiple_of(group * rows, rows), rows), :]
        return pltpu.make_async_copy(out_in.at[group], place, sent.at[group])

    side_copy.start()
    for group in range(groups):
        for copy in in_copies(group):
            copy.start()
    total[...] = jnp.zeros_like(total)
    side_copy.wait()

    def advance(group, carry):
        depth = heads * state_size
        state = prior_ref[pl.ds(pl.multiple_of(group * depth, depth), depth), :]
        states = [state[head * state_size : (head + 1) * state_size, :] for head in range(heads)]
        parts = jnp.concatenate(split_two(jnp.concatenate(states, axis=1)), axis=0)
        for copy in in_copies(group):
            copy.wait()
        for start in range(0, length, CHUNK):
            chunk = slice(start, start + CHUNK)
            from_state = jnp.dot(side[chunk, :].astype(BF16), parts, preferred_element_type=F32)
            squares = total[chunk, :]
            for head in range(heads):
                place = slice(head * LANES, (head + 1) * LANES)
                gated = own[group, chunk, place].astype(F32)
                gated = gated + factor[group, chunk, place].astype(F32) * from_state[:, place]
                squares = squares + gated * gated
                if first_layer:
                    for row in range(CHUNK // cols):
                        pitched = pl.ds((start // cols + row) * PITCH, cols)
                        staged[head, pitched, :] = gated[row * cols : (row + 1) * cols, :]
                else:
                    out_ref[group, chunk, place] = gated.astype(out_ref.dtype)
            total[chunk, :] = squares
        if first_layer:
            rows = length // cols
            for head in range(heads):
                for col in range(cols):
                    picked = staged[head, pl.ds(col, rows, stride=PITCH), :]
                    out_in[group, col, head * rows : (head + 1) * rows, :] = picked.astype(BF16)
            out_copy(group).start()
        return carry

    lax.fori_loop(0, groups, advance, 0)
    ordered = total[...]
    if first_layer:
        rows = length // cols
        ordered = jnp.concatenate([total[pl.ds(col, rows, stride=cols), :] for col in range(cols)], axis=0)
    ones = jnp.ones((TILE, LANES), BF16)
    sums = jnp.zeros((TILE, length), F32)
    for part in split_three(ordered):
        sums = sums + lax.dot_general(ones, part, (((1,), (1,)), ((), ())), preferred_element_type=F32)
    if first_layer:
        high, middle, low = [part.astype(F32) for part in split_three(sums)]
        row = lax.broadcasted_iota(jnp.int32, (TILE, length), 0)
        parts = jnp.where(row == 0, high, jnp.where(row == 1, middle, low))
        parts = jnp.where(row < 3, parts, 0.0)
        empty = jnp.zeros((EXTRA - TILE, LANES), F32)
        for col in range(cols):
            start = col * rows
            inside = start % LANES
            tile = parts[:, start - inside : start - inside + LANES]
            if inside:
                tile = pltpu.roll(tile, LANES - inside, 1)
            extra[col, :, :] = jnp.concatenate([tile, empty], axis=0).astype(BF16)
        last = out_hbm.at[:, pl.ds(out_hbm.shape[1] - EXTRA, EXTRA), :]
        extra_copy = pltpu.make_async_copy(extra, last, sent.at[groups])
        extra_copy.start()
        extra_copy.wait()
        for group in range(groups):
            out_copy(group).wait()
    else:
        squares_ref[...] = sums[:1]


def gated_outputs(first_layer, own, factor, prior, cols):
    length, width = factor.shape
    heads = HEADS_PER_STEP
    part = heads * LANES
    groups = width // part
    scratch = [
        pltpu.VMEM((groups, length, part), own.dtype),
        pltpu.VMEM((groups, length, part), factor.dtype),
        pltpu.VMEM((length, LANES), own.dtype),
    ]
    total = pltpu.VMEM((length, LANES), F32)
    got = pltpu.SemaphoreType.DMA((2 * groups + 1,))
    if first_layer:
        rows = length // cols
        out_specs = HBM
        out_shape = jax.ShapeDtypeStruct((cols, width // LANES * rows + EXTRA, LANES), BF16)
        scratch += [
            pltpu.VMEM((groups, cols, heads * rows, LANES), BF16),
            total,
            pltpu.SemaphoreType.DMA((groups + 1,)),
            got,
            pltpu.VMEM((heads, rows * PITCH, LANES), F32),
            pltpu.VMEM((cols, EXTRA, LANES), BF16),
        ]
    else:
        out_specs = [VMEM, VMEM]
        out_shape = [
            jax.ShapeDtypeStruct((groups, length, part), LAST_TYPE),
            jax.ShapeDtypeStruct((1, length), F32),
        ]
        scratch += [total, got]
    return pl.pallas_call(
        functools.partial(gated_kernel, first_layer),
        in_specs=[HBM, HBM, VMEM],
        out_specs=out_specs,
        out_shape=out_shape,
        scratch_shapes=scratch,
        compiler_params=params(GATED_MB[first_layer]),
        cost_estimate=pl.CostEstimate(
            flops=1_200_000_000, bytes_accessed=13_000_000, transcendentals=2_000_000
        ),
        name="gated",
    )(own, factor, prior)


def scaled_kernel(features, gated_ref, squares_ref, gain_ref, out_hbm, out_in, sent):
    parts, rows, width = out_in.shape
    part_lanes = gated_ref.shape[2]

    def out_copy(part):
        place = pl.ds(pl.multiple_of(part * rows, rows), rows)
        return pltpu.make_async_copy(out_in.at[part], out_hbm.at[place], sent.at[part])

    def advance(part, carry):
        at = pl.ds(pl.multiple_of(part * rows, rows), rows)
        scale = norm_scale(squares_ref[:, at], features)
        column = jnp.transpose(jnp.broadcast_to(scale, (LANES, rows)))
        for head in range(width // LANES):
            place = slice(head * LANES, (head + 1) * LANES)
            group, inside = divmod(head * LANES, part_lanes)
            gated = gated_ref[group, at, inside : inside + LANES].astype(F32) * column
            out_in[part, :, place] = (gated * gain_ref[:, place]).astype(BF16)
        out_copy(part).start()
        return carry

    lax.fori_loop(0, parts, advance, 0)
    for part in range(parts):
        out_copy(part).wait()


def scaled_outputs(gated, squares, gain, features):
    groups, length, part_lanes = gated.shape
    width = groups * part_lanes
    parts = length // SCALED_ROWS
    return pl.pallas_call(
        functools.partial(scaled_kernel, features),
        in_specs=[VMEM, VMEM, VMEM],
        out_specs=HBM,
        out_shape=jax.ShapeDtypeStruct((length, width), BF16),
        scratch_shapes=[
            pltpu.VMEM((parts, SCALED_ROWS, width), BF16),
            pltpu.SemaphoreType.DMA((parts,)),
        ],
        compiler_params=params(48),
        name="scaled",
    )(gated, squares, gain)


def body(
    tokens_in,
    gate_rows,
    gate_cols,
    write_rows,
    read_rows,
    step_rows,
    decay_rows,
    skip_rows,
    norm_rows,
    write_cols,
    read_cols,
    step_cols,
    decay_cols,
    skip_cols,
    norm_cols,
):
    grid_rows, grid_cols, width = tokens_in.shape
    devices = lax.axis_size(SEQ)
    features = float(width * lax.axis_size("head"))
    tokens = grid_rows * grid_cols
    column_len = gate_cols.shape[0]

    x = tokens_in.reshape(tokens, width)
    payload, before = device_states(x, write_rows, step_rows, decay_rows, None, None, features, devices)
    half = tokens // BLOCK // 2
    gate = gate_rows.reshape(tokens, width)
    local = lambda first, decay, done: local_factors(
        first, half, x, write_rows, read_rows, step_rows, decay, gate, None, None, before, skip_rows, features, done
    )
    prior, done, decay = prior_states(payload, local(0, decay_rows, ()), decay_rows)
    hidden = gated_outputs(True, *local(half, decay, done), prior, grid_cols)
    hidden = lax.all_to_all(hidden, SEQ, split_axis=0, concat_axis=0, tiled=True)
    squares = hidden[:, -EXTRA : 3 - EXTRA, :grid_rows].astype(F32)
    squares = (squares[:, 0] + squares[:, 1] + squares[:, 2]).reshape(-1, LANES)
    squares = lax.psum(squares, "head")

    gain = norm_rows[None]
    payload, before = device_states(
        hidden, write_cols, step_cols, decay_cols, squares, gain, features, devices
    )
    half = column_len // BLOCK // 2
    gate = gate_cols.reshape(column_len, width)
    local = lambda first, decay, done: local_factors(
        first, half, hidden, write_cols, read_cols, step_cols, decay, gate, squares, gain, before, skip_cols, features, done
    )
    prior, done, decay = prior_states(payload, local(0, decay_cols, ()), decay_cols)
    gated, last_squares = gated_outputs(False, *local(half, decay, done), prior, 1)
    last_squares = lax.psum(last_squares, "head")
    out = scaled_outputs(gated, last_squares, norm_cols[None], features)
    return out.reshape(column_len, 1, width)


def solution(mesh):
    torus = Mesh(
        mesh.devices.reshape(4, 4, 2, mesh.shape["head"]), ("seq_0", "seq_1", "seq_2", "head")
    )
    return jax.shard_map(
        body,
        mesh=torus,
        in_specs=(
            P(SEQ, None, "head"),
            P(SEQ, None, "head"),
            P(None, SEQ, "head"),
            P(None, SEQ),
            P(None, SEQ),
            P("head", SEQ),
            P("head", SEQ),
            P("head"),
            P("head"),
            P(None, SEQ),
            P(None, SEQ),
            P("head", SEQ),
            P("head", SEQ),
            P("head"),
            P("head"),
        ),
        out_specs=P(None, SEQ, "head"),
        check_vma=False,
    )
```

time: 178 us -> 157 us (0.88)
  Pallas kernels: 64.4 us -> 52.1 us
  waiting for transfers between devices: 43 us -> 51.3 us
  starting transfers between devices: 37.2 us -> 30.5 us
  blocking collectives: 27.6 us -> 21.4 us
  local copies, waits for them, and re-layouts: 3.88 us -> 0.69 us
    pallas_call x5, Pallas kernels: 40.2 us -> 29.7 us  [the longest x4 27.4 us: local_factors(): pl.pallas_call(functools.partial(local_kernel, by_head, features, first),...]
    all_to_all x2, waiting for transfers between devices: 1.45 us -> 6.88 us  [prior_states(): ends = lax.all_to_all(payload, SEQ, split_axis=0, concat_axis=0, tiled=True)]
    all_to_all x2, starting transfers between devices: 13.9 us -> 8.85 us  [prior_states(): prior = lax.all_to_all(prior, SEQ, split_axis=0, concat_axis=0, tiled=True)]
    psum x1, blocking collectives: 15.5 us -> 10.8 us  [body(): last_squares = lax.psum(last_squares, 'head')]
    all_to_all x2, waiting for transfers between devices: 0.86 us -> 3.8 us  [prior_states(): prior = lax.all_to_all(prior, SEQ, split_axis=0, concat_axis=0, tiled=True)]
    unnamed x20 -> x6, local copies, waits for them, and re-layouts: 2.67 us -> 0.02 us
    pallas_call x2, Pallas kernels: 13.5 us -> 11.2 us  [gated_outputs(): pl.pallas_call(functools.partial(gated_kernel, first_layer), in_specs=[HB...]
  transfers between devices with their start and end apart: 5 -> 5, of which waited for: 4 -> 5; matrix products, arithmetic and copies ran while one was open for 1% -> 0% of each run, Pallas kernels for 20% -> 18%
where the time goes in v4:
time: 157 us; the launch traced here: 156 us
  Pallas kernels  52.1 us (33%)
  waiting for transfers between devices  51.3 us (33%)
  starting transfers between devices  30.5 us (19%)
  blocking collectives  21.4 us (14%)
    all_to_all x1, waiting for transfers between devices, body(): lax.all_to_all(hidden, SEQ, split_axis=0, concat_axis=0, tiled=True)  40.6 us
    pallas_call x4, Pallas kernels, local_factors(): pl.pallas_call(functools.partial(local_kernel, by_head, features, first),...  27.4 us
    all_to_all x2, starting transfers between devices, prior_states(): ends = lax.all_to_all(payload, SEQ, split_axis=0, concat_axis=0, tiled=True)  16 us
    pallas_call x2, Pallas kernels, gated_outputs(): pl.pallas_call(functools.partial(gated_kernel, first_layer), in_specs=[HB...  11.2 us
    psum x1, blocking collectives, body(): last_squares = lax.psum(last_squares, 'head')  10.8 us
    psum x1, blocking collectives, body(): squares = lax.psum(squares, 'head')  10.7 us
    pallas_call x2, Pallas kernels, device_states(): pl.pallas_call(functools.partial(states_kernel, by_head, features), in_sp...  9.51 us
    all_to_all x2, starting transfers between devices, prior_states(): prior = lax.all_to_all(prior, SEQ, split_axis=0, concat_axis=0, tiled=True)  8.85 us
  transfers between devices with their start and end apart: 5, of which 5 were waited for; matrix products, arithmetic and copies ran while one was open for 0% of the time, Pallas kernels for 18%

profile of v4, /device:TPU:1, one launch (start us, length us, event | category | flops | bytes accessed | tf_op | source)
XLA Modules:
  0.0 156.4 jit_solution(11501017673534530997)
XLA Ops:
  0.0 4.4 %states.2 = (f32[32,32,128]{2,1,0:T(8,128)}, f32[4,768,128]{2,1,0:T(8,128)}) custom-call(bf16[1024,1536]{1,0:T(8,128)(2,1)} %bitcast.8, bf16[64,1024]{1,0:T(8,128)(2,1)} %refs_1_.5, f32[12,1024]{1,0:T(8,128)} %refs_3_.5, f32[12,1024]{1,0:T(8,128)} %refs_4_.3), custom_call_target="tpu_custom_call" | custom-call | flops 500000000 | bytes 6000000 | tf_op jit(solution)/shard_map/states/pallas_call | solution.py:167
  4.4 9.7 %all-to-all-start = ((f32[32,32,128]{2,1,0:T(8,128)}), f32[32,32,128]{2,1,0:T(8,128)S(1)}, u32[]{:S(2)}, u32[]{:S(2)}) async-start(f32[32,32,128]{2,1,0:T(8,128)} %get-tuple-element.27), calls=%async_computation | async-start | bytes 1048576 | tf_op jit(solution)/shard_map/all_to_all | solution.py:206
  14.2 6.8 %local.4 = (f32[1024,1664]{1,0:T(8,128)}, bf16[1024,1536]{1,0:T(8,128)(2,1)}) custom-call(bf16[1024,1536]{1,0:T(8,128)(2,1)} %bitcast.9, bf16[64,1024]{1,0:T(8,128)(2,1)} %refs_1_.5, bf16[64,1024]{1,0:T(8,128)(2,1)} %refs_2_.5, f32[12,1024]{1,0:T(8,128)} %refs_3_.5, f32[12,1024]{1,0:T(8,128)} %refs_4_.3, bf16[1024,1536]{1,0:T(8,128)(2,1)} %bitcast.11, ...), custom_call_target="tpu_custom_call" | custom-call | flops 3000000000 | bytes 10000000 | tf_op jit(solution)/shard_map/local/pallas_call | solution.py:319
  20.9 3.9 %all-to-all-done.ends_ref = f32[32,32,128]{2,1,0:T(8,128)S(1)} async-done(((f32[32,32,128]{2,1,0:T(8,128)}), f32[32,32,128]{2,1,0:T(8,128)S(1)}, u32[]{:S(2)}, u32[]{:S(2)}) %all-to-all-start) | async-done | bytes 524320 | tf_op jit(solution)/shard_map/all_to_all | solution.py:206
  24.9 0.8 prefix.2
  25.7 3.9 %all-to-all-start.1 = ((f32[32,24,128]{2,1,0:T(8,128)}), f32[32,24,128]{2,1,0:T(8,128)S(1)}, u32[]{:S(2)}, u32[]{:S(2)}) async-start(f32[32,24,128]{2,1,0:T(8,128)} %prefix.2), calls=%async_computation.1 | async-start | bytes 786432 | tf_op jit(solution)/shard_map/all_to_all | solution.py:214
  29.6 6.9 %local.5 = (f32[1024,1664]{1,0:T(8,128)}, bf16[1024,1536]{1,0:T(8,128)(2,1)}) custom-call(bf16[1024,1536]{1,0:T(8,128)(2,1)} %bitcast.10, bf16[64,1024]{1,0:T(8,128)(2,1)} %refs_1_.5, bf16[64,1024]{1,0:T(8,128)(2,1)} %refs_2_.5, f32[12,1024]{1,0:T(8,128)} %refs_3_.5, f32[12,1024]{1,0:T(8,128)} %refs_4_.3, ...), custom_call_target="tpu_custom_call", output_to_operand_aliasing={{0}: (8, {}), {1}: (9, {})} | custom-call | flops 3000000000 | bytes 10000000 | tf_op jit(solution)/shard_map/local/pallas_call | solution.py:319
  36.5 2.1 %all-to-all-done.1 = f32[32,24,128]{2,1,0:T(8,128)S(1)} async-done(((f32[32,24,128]{2,1,0:T(8,128)}), f32[32,24,128]{2,1,0:T(8,128)S(1)}, u32[]{:S(2)}, u32[]{:S(2)}) %all-to-all-start.1) | async-done | bytes 393248 | tf_op jit(solution)/shard_map/all_to_all | solution.py:214
  38.6 6.5 %gated.2 = bf16[32,400,128]{2,1,0:T(8,128)(2,1)} custom-call(f32[1024,1664]{1,0:T(8,128)} %get-tuple-element.34.own_hbm, bf16[1024,1536]{1,0:T(8,128)(2,1)} %get-tuple-element.35.factor_hbm, f32[768,128]{1,0:T(8,128)S(1)} %bitcast.7), custom_call_target="tpu_custom_call" | custom-call | flops 1200000000 | bytes 13000000 | tf_op jit(solution)/shard_map/gated/pallas_call | solution.py:469
  45.1 0.0 copy-start.1
  45.1 5.6 %all-to-all-start.2 = ((bf16[32,400,128]{2,1,0:T(8,128)(2,1)}), bf16[32,400,128]{2,1,0:T(8,128)(2,1)S(1)}, u32[]{:S(2)}, u32[]{:S(2)}) async-start(bf16[32,400,128]{2,1,0:T(8,128)(2,1)} %gated.2), calls=%async_computation.2 | async-start | bytes 6553600 | tf_op jit(solution)/shard_map/all_to_all | solution.py:558
  50.8 0.0 copy-done.1
  50.8 0.6 broadcast_in_dim.6.refs_1_.refs_9_
  51.4 40.6 %all-to-all-done.2.x_ref.refs_0_ = bf16[32,400,128]{2,1,0:T(8,128)(2,1)S(1)} async-done(((bf16[32,400,128]{2,1,0:T(8,128)(2,1)}), bf16[32,400,128]{2,1,0:T(8,128)(2,1)S(1)}, u32[]{:S(2)}, u32[]{:S(2)}) %all-to-all-start.2) | async-done | bytes 3276832 | tf_op jit(solution)/shard_map/all_to_all | solution.py:558
  92.0 0.0 copy-start
  92.0 0.1 fusion
  92.1 0.1 add.18
  92.1 10.7 %psum.14.refs_0_.refs_8_ = f32[8,128]{1,0:T(8,128)} all-reduce(f32[8,128]{1,0:T(8,128)S(1)} %add.18), channel_id=1, replica_groups=mesh['seq_0'=4,'seq_1'=4,'seq_2'=2,'head'=4] {'head'}, use_global_device_ids=true, to_apply=%region_0.0 | all-reduce | flops 1024 | bytes 8192 | tf_op jit(solution)/shard_map/psum | solution.py:561
  102.8 0.0 copy-done
  102.8 5.1 %states.3 = (f32[32,32,128]{2,1,0:T(8,128)}, f32[4,768,128]{2,1,0:T(8,128)}) custom-call(bf16[32,400,128]{2,1,0:T(8,128)(2,1)} %copy-done, bf16[64,1024]{1,0:T(8,128)(2,1)} %refs_1_.7, f32[12,1024]{1,0:T(8,128)} %refs_3_.7, f32[12,1024]{1,0:T(8,128)} %refs_4_.5, f32[8,128]{1,0:T(8,128)} %psum.14.refs_0_.refs_8_, f32[1,1536]{1,0:T(1,128)} %broadcast_in_dim.6.refs_1_.refs_9_), custom_call_target="tpu_custom_call" | custom-call | flops 500000000 | bytes 6000000 | tf_op jit(solution)/shard_map/states/pallas_call | solution.py:167
  107.9 6.3 %all-to-all-start.3 = ((f32[32,32,128]{2,1,0:T(8,128)}), f32[32,32,128]{2,1,0:T(8,128)S(1)}, u32[]{:S(2)}, u32[]{:S(2)}) async-start(f32[32,32,128]{2,1,0:T(8,128)} %get-tuple-element.37), calls=%async_computation.3 | async-start | bytes 1048576 | tf_op jit(solution)/shard_map/all_to_all | solution.py:206
  114.2 0.0 copy-start.2
  114.2 6.8 %local.6 = (f32[1024,1664]{1,0:T(8,128)}, bf16[1024,1536]{1,0:T(8,128)(2,1)}) custom-call(bf16[32,400,128]{2,1,0:T(8,128)(2,1)} %copy-done, bf16[64,1024]{1,0:T(8,128)(2,1)} %refs_1_.7, bf16[64,1024]{1,0:T(8,128)(2,1)} %refs_2_.7, f32[12,1024]{1,0:T(8,128)} %refs_3_.7, f32[12,1024]{1,0:T(8,128)} %refs_4_.5, bf16[1024,1536]{1,0:T(8,128)(2,1)} %bitcast.13, ...), custom_call_target="tpu_custom_call" | custom-call | flops 3000000000 | bytes 10000000 | tf_op jit(solution)/shard_map/local/pallas_call | solution.py:319
  121.0 2.9 %all-to-all-done.3.ends_ref = f32[32,32,128]{2,1,0:T(8,128)S(1)} async-done(((f32[32,32,128]{2,1,0:T(8,128)}), f32[32,32,128]{2,1,0:T(8,128)S(1)}, u32[]{:S(2)}, u32[]{:S(2)}) %all-to-all-start.3) | async-done | bytes 524320 | tf_op jit(solution)/shard_map/all_to_all | solution.py:206
  124.0 0.8 prefix.3
  124.8 5.0 %all-to-all-start.4 = ((f32[32,24,128]{2,1,0:T(8,128)}), f32[32,24,128]{2,1,0:T(8,128)S(1)}, u32[]{:S(2)}, u32[]{:S(2)}) async-start(f32[32,24,128]{2,1,0:T(8,128)} %prefix.3), calls=%async_computation.4 | async-start | bytes 786432 | tf_op jit(solution)/shard_map/all_to_all | solution.py:214
  129.8 0.0 copy-done.2
  129.8 6.9 %local.7 = (f32[1024,1664]{1,0:T(8,128)}, bf16[1024,1536]{1,0:T(8,128)(2,1)}) custom-call(bf16[32,400,128]{2,1,0:T(8,128)(2,1)} %copy-done, bf16[64,1024]{1,0:T(8,128)(2,1)} %refs_1_.7, bf16[64,1024]{1,0:T(8,128)(2,1)} %refs_2_.7, f32[12,1024]{1,0:T(8,128)} %refs_3_.7, f32[12,1024]{1,0:T(8,128)} %refs_4_.5, ...), custom_call_target="tpu_custom_call", output_to_operand_aliasing={{0}: (10, {}), {1}: (11, {})} | custom-call | flops 3000000000 | bytes 10000000 | tf_op jit(solution)/shard_map/local/pallas_call | solution.py:319
  136.7 1.7 %all-to-all-done.4 = f32[32,24,128]{2,1,0:T(8,128)S(1)} async-done(((f32[32,24,128]{2,1,0:T(8,128)}), f32[32,24,128]{2,1,0:T(8,128)S(1)}, u32[]{:S(2)}, u32[]{:S(2)}) %all-to-all-start.4) | async-done | bytes 393248 | tf_op jit(solution)/shard_map/all_to_all | solution.py:214
  138.4 4.7 %gated.3 = (bf16[6,1024,256]{2,1,0:T(8,128)(2,1)S(1)}, f32[1,1024]{1,0:T(1,128)S(1)}) custom-call(f32[1024,1664]{1,0:T(8,128)} %get-tuple-element.44.own_hbm, bf16[1024,1536]{1,0:T(8,128)(2,1)} %get-tuple-element.45.factor_hbm, f32[768,128]{1,0:T(8,128)S(1)} %bitcast.6), custom_call_target="tpu_custom_call" | custom-call | flops 1200000000 | bytes 13000000 | tf_op jit(solution)/shard_map/gated/pallas_call | solution.py:469
  143.1 10.8 %psum.15.squares_ref = f32[1,1024]{1,0:T(1,128)S(1)} all-reduce(f32[1,1024]{1,0:T(1,128)S(1)} %get-tuple-element.48), channel_id=1, replica_groups=mesh['seq_0'=4,'seq_1'=4,'seq_2'=2,'head'=4] {'head'}, use_global_device_ids=true, to_apply=%region_1.0 | all-reduce | flops 1024 | bytes 8192 | tf_op jit(solution)/shard_map/psum | solution.py:574
  153.9 2.3 %scaled.1 = bf16[1024,1536]{1,0:T(8,128)(2,1)} custom-call(bf16[6,1024,256]{2,1,0:T(8,128)(2,1)S(1)} %get-tuple-element.47.gated_ref, f32[1,1024]{1,0:T(1,128)S(1)} %psum.15.squares_ref, f32[1,1536]{1,0:T(1,128)S(1)} %broadcast_in_dim.7.gain_ref), custom_call_target="tpu_custom_call" | custom-call | tf_op jit(solution)/shard_map/scaled/pallas_call | solution.py:512
  (2 shorter events, 0.0 us)
Async XLA Ops:
  4.4 20.4 %all-to-all-start = ((f32[32,32,128]{2,1,0:T(8,128)}), f32[32,32,128]{2,1,0:T(8,128)S(1)}, u32[]{:S(2)}, u32[]{:S(2)}) async-start(f32[32,32,128]{2,1,0:T(8,128)} %get-tuple-element.27), calls=%async_computation | async-start | bytes 1048576 | tf_op jit(solution)/shard_map/all_to_all | solution.py:206
  25.7 12.9 %all-to-all-start.1 = ((f32[32,24,128]{2,1,0:T(8,128)}), f32[32,24,128]{2,1,0:T(8,128)S(1)}, u32[]{:S(2)}, u32[]{:S(2)}) async-start(f32[32,24,128]{2,1,0:T(8,128)} %prefix.2), calls=%async_computation.1 | async-start | bytes 786432 | tf_op jit(solution)/shard_map/all_to_all | solution.py:214
  45.1 5.7 %copy-start.1 = (f32[1536]{0:T(1024)S(1)}, f32[1536]{0:T(1024)}, u32[]{:S(2)}) copy-start(f32[1536]{0:T(1024)} %param.23) | copy-start | bytes 18436
  45.1 46.8 %all-to-all-start.2 = ((bf16[32,400,128]{2,1,0:T(8,128)(2,1)}), bf16[32,400,128]{2,1,0:T(8,128)(2,1)S(1)}, u32[]{:S(2)}, u32[]{:S(2)}) async-start(bf16[32,400,128]{2,1,0:T(8,128)(2,1)} %gated.2), calls=%async_computation.2 | async-start | bytes 6553600 | tf_op jit(solution)/shard_map/all_to_all | solution.py:558
  92.0 10.8 %copy-start = (bf16[32,400,128]{2,1,0:T(8,128)(2,1)}, bf16[32,400,128]{2,1,0:T(8,128)(2,1)S(1)}, u32[]{:S(2)}) copy-start(bf16[32,400,128]{2,1,0:T(8,128)(2,1)S(1)} %all-to-all-done.2.x_ref.refs_0_) | copy-start | bytes 9830404
  107.9 16.0 %all-to-all-start.3 = ((f32[32,32,128]{2,1,0:T(8,128)}), f32[32,32,128]{2,1,0:T(8,128)S(1)}, u32[]{:S(2)}, u32[]{:S(2)}) async-start(f32[32,32,128]{2,1,0:T(8,128)} %get-tuple-element.37), calls=%async_computation.3 | async-start | bytes 1048576 | tf_op jit(solution)/shard_map/all_to_all | solution.py:206
  114.2 15.6 %copy-start.2 = (f32[1536]{0:T(1024)S(1)}, f32[1536]{0:T(1024)}, u32[]{:S(2)}) copy-start(f32[1536]{0:T(1024)} %param.29) | copy-start | bytes 18436
  124.8 13.6 %all-to-all-start.4 = ((f32[32,24,128]{2,1,0:T(8,128)}), f32[32,24,128]{2,1,0:T(8,128)S(1)}, u32[]{:S(2)}, u32[]{:S(2)}) async-start(f32[32,24,128]{2,1,0:T(8,128)} %prefix.3), calls=%async_computation.4 | async-start | bytes 786432 | tf_op jit(solution)/shard_map/all_to_all | solution.py:214

commit v5 on v4

--- a/solution.py
+++ b/solution.py
@@ -13,7 +13,7 @@
 EPSILON = 1e-05
 LANES = 128
 TILE = 8
-HEADS_PER_STEP = 2
+HEADS_PER_STEP = 3
 EXTRA = 16
 CHUNK = 128
 PITCH = 40
@@ -84,7 +84,7 @@
 
 def states_kernel(by_head, features, x_ref, write_hbm, step_hbm, decay_hbm, *refs):
     if by_head:
-        squares_ref, gain_hbm, payload_hbm, before_hbm, gain_ref, x_in, write_ref, step_ref, decay_ref, before, payload, total, sent, got = refs
+        squares_hbm, gain_hbm, payload_hbm, before_hbm, gain_ref, squares_ref, x_in, write_ref, step_ref, decay_ref, before, payload, total, sent, got = refs
     else:
         payload_hbm, before_hbm, x_in, write_ref, step_ref, decay_ref, before, payload, total, sent, got = refs
     head_count = step_ref.shape[0]
@@ -92,7 +92,7 @@
     blocks = before.shape[0] - 1
     pairs = ((decay_hbm, decay_ref), (step_hbm, step_ref), (write_hbm, write_ref))
     if by_head:
-        pairs += ((gain_hbm, gain_ref),)
+        pairs += ((squares_hbm, squares_ref), (gain_hbm, gain_ref))
     small = [pltpu.make_async_copy(*pair, got.at[at]) for at, pair in enumerate(pairs)]
 
     def x_copy(block):
@@ -160,9 +160,9 @@
     operands = [x, write, step, decay]
     scratch = []
     if by_head:
-        specs += [VMEM, HBM]
+        specs += [HBM, HBM]
         operands += [squares, gain]
-        scratch.append(pltpu.VMEM(gain.shape, F32))
+        scratch += [pltpu.VMEM(gain.shape, F32), pltpu.VMEM(squares.shape, F32)]
     scratch.append(pltpu.VMEM((blocks, x.shape[0] // blocks, *x.shape[1:]), BF16))
     return pl.pallas_call(
         functools.partial(states_kernel, by_head, features),
@@ -181,7 +181,7 @@
             pltpu.VMEM((devices, height + TILE, LANES), F32),
             pltpu.VMEM((head_count, LANES), F32),
             pltpu.SemaphoreType.DMA((blocks + 1,)),
-            pltpu.SemaphoreType.DMA((4 + blocks,)),
+            pltpu.SemaphoreType.DMA((5 + blocks,)),
         ],
         compiler_params=params(),
         cost_estimate=pl.CostEstimate(flops=500_000_000, bytes_accessed=6_000_000, transcendentals=20_000),
@@ -253,7 +253,7 @@
     read = read_ref[...]
     turned = jnp.transpose(read.astype(F32))
     reads = jnp.concatenate([turned, turned], axis=1)
-    own_ref[:, head_count * LANES :] = reads.astype(own_ref.dtype)
+    own_ref[own_ref.shape[0] - 1] = jnp.concatenate([reads] * HEADS_PER_STEP, axis=1).astype(own_ref.dtype)
     reads = reads.astype(BF16)
     scores = lax.dot_general(read, write_ref[...], (((0,), (0,)), ((), ())), preferred_element_type=F32)
     first_half, last_half = slice(0, half), slice(half, BLOCK)
@@ -285,8 +285,10 @@
         lift = jnp.broadcast_to(lifts[:, head : head + 1], (BLOCK, LANES))
         outputs = outputs + lift * read_state(reads, state)
         gate = silu(gate_ref[:, place].astype(F32))
-        own_ref[:, place] = (outputs * gate).astype(own_ref.dtype)
-        factor_ref[:, place] = (lift * kept[head : head + 1, :] * gate).astype(factor_ref.dtype)
+        group, inside = divmod(head, HEADS_PER_STEP)
+        inside = slice(inside * LANES, (inside + 1) * LANES)
+        own_ref[group, :, inside] = (outputs * gate).astype(own_ref.dtype)
+        factor_ref[group, :, inside] = (lift * kept[head : head + 1, :] * gate).astype(factor_ref.dtype)
 
 
 def local_factors(first, count, x, write, read, step, decay, gate, squares, gain, before, skip, features, done):
@@ -315,6 +317,8 @@
         specs.append(pl.BlockSpec(squares.shape, lambda k: (0, 0)))
         specs.append(pl.BlockSpec((1, width), lambda k: (0, 0)))
         operands += [squares, gain]
+    part = HEADS_PER_STEP * LANES
+    groups = width // part
     aliases = {len(operands) + at: at for at in range(len(done))}
     return pl.pallas_call(
         functools.partial(local_kernel, by_head, features, first),
@@ -322,12 +326,12 @@
         in_specs=specs + [HBM] * len(done),
         input_output_aliases=aliases,
         out_specs=[
-            pl.BlockSpec((BLOCK, width + LANES), lambda k: (first + k, 0)),
-            pl.BlockSpec((BLOCK, width), lambda k: (first + k, 0)),
+            pl.BlockSpec((groups + 1, BLOCK, part), lambda k: (0, first + k, 0)),
+            pl.BlockSpec((groups, BLOCK, part), lambda k: (0, first + k, 0)),
         ],
         out_shape=[
-            jax.ShapeDtypeStruct((length, width + LANES), OWN_TYPE),
-            jax.ShapeDtypeStruct((length, width), FACTOR_TYPE),
+            jax.ShapeDtypeStruct((groups + 1, length, part), OWN_TYPE),
+            jax.ShapeDtypeStruct((groups, length, part), FACTOR_TYPE),
         ],
         scratch_shapes=[pltpu.VMEM((head_count, LANES), F32)],
         compiler_params=params(),
@@ -348,16 +352,12 @@
     heads = width // LANES
     state_size = LANES // 2
 
-    def lanes(group):
-        return pl.ds(pl.multiple_of(group * width, width), width)
-
     def in_copies(group):
-        own_copy = pltpu.make_async_copy(own_hbm.at[:, lanes(group)], own.at[group], got.at[group])
+        own_copy = pltpu.make_async_copy(own_hbm.at[group], own.at[group], got.at[group])
         at = groups + group
-        return own_copy, pltpu.make_async_copy(factor_hbm.at[:, lanes(group)], factor.at[group], got.at[at])
-
-    beside = pl.ds(groups * width, LANES)
-    side_copy = pltpu.make_async_copy(own_hbm.at[:, beside], side, got.at[2 * groups])
+        return own_copy, pltpu.make_async_copy(factor_hbm.at[group], factor.at[group], got.at[at])
+
+    side_copy = pltpu.make_async_copy(own_hbm.at[groups, :, pl.ds(0, LANES)], side, got.at[2 * groups])
 
     def out_copy(group):
         rows = out_in.shape[2]
@@ -436,10 +436,9 @@
 
 
 def gated_outputs(first_layer, own, factor, prior, cols):
-    length, width = factor.shape
-    heads = HEADS_PER_STEP
-    part = heads * LANES
-    groups = width // part
+    groups, length, part = factor.shape
+    heads = part // LANES
+    width = groups * part
     scratch = [
         pltpu.VMEM((groups, length, part), own.dtype),
         pltpu.VMEM((groups, length, part), factor.dtype),
@@ -523,6 +522,14 @@
     )(gated, squares, gain)
 
 
+def sum_over_head(value):
+    devices = lax.axis_size("head")
+    total = value
+    for step in range(1, devices):
+        total = total + lax.ppermute(value, "head", [(at, at ^ step) for at in range(devices)])
+    return total
+
+
 def body(
     tokens_in,
     gate_rows,
@@ -558,7 +565,7 @@
     hidden = lax.all_to_all(hidden, SEQ, split_axis=0, concat_axis=0, tiled=True)
     squares = hidden[:, -EXTRA : 3 - EXTRA, :grid_rows].astype(F32)
     squares = (squares[:, 0] + squares[:, 1] + squares[:, 2]).reshape(-1, LANES)
-    squares = lax.psum(squares, "head")
+    squares = sum_over_head(squares)
 
     gain = norm_rows[None]
     payload, before = device_states(
@@ -571,7 +578,7 @@
     )
     prior, done, decay = prior_states(payload, local(0, decay_cols, ()), decay_cols)
     gated, last_squares = gated_outputs(False, *local(half, decay, done), prior, 1)
-    last_squares = lax.psum(last_squares, "head")
+    last_squares = sum_over_head(last_squares)
     out = scaled_outputs(gated, last_squares, norm_cols[None], features)
     return out.reshape(column_len, 1, width)
 

time: 157 us -> 150 us (0.955)
  waiting for transfers between devices: 51.3 us -> 17.2 us
  blocking collectives: 21.4 us -> 44.9 us
  starting transfers between devices: 30.5 us -> 34.2 us
    all_to_all x0 -> x1, blocking collectives: none -> 44.9 us  [body(): lax.all_to_all(hidden, SEQ, split_axis=0, concat_axis=0, tiled=True)]
    all_to_all x1 -> x0, waiting for transfers between devices: 40.6 us -> none  [body(): lax.all_to_all(hidden, SEQ, split_axis=0, concat_axis=0, tiled=True)]
    psum x2 -> x0, blocking collectives: 21.4 us -> none  [the longest x1 10.8 us: body(): last_squares = lax.psum(last_squares, 'head')]
    ppermute x0 -> x6, starting transfers between devices: none -> 12.6 us  [sum_over_head(): lax.ppermute(value, 'head', [(at, at ^ step) for at in range(devices)])]
    all_to_all x1 -> x0, starting transfers between devices: 5.64 us -> none  [body(): lax.all_to_all(hidden, SEQ, split_axis=0, concat_axis=0, tiled=True)]
    ppermute x0 -> x6, waiting for transfers between devices: none -> 5.31 us  [sum_over_head(): lax.ppermute(value, 'head', [(at, at ^ step) for at in range(devices)])]
    all_to_all x2, starting transfers between devices: 16 us -> 13.6 us  [prior_states(): ends = lax.all_to_all(payload, SEQ, split_axis=0, concat_axis=0, tiled=True)]
  transfers between devices with their start and end apart: 5 -> 10, of which waited for: 5 -> 8; matrix products, arithmetic and copies ran while one was open for 0% -> 0% of each run, Pallas kernels for 18% -> 19%
where the time goes in v5:
time: 150 us
  Pallas kernels  51.8 us (35%)
  blocking collectives  44.9 us (30%)
  starting transfers between devices  34.2 us (23%)
  waiting for transfers between devices  17.2 us (11%)
    all_to_all x1, blocking collectives, body(): lax.all_to_all(hidden, SEQ, split_axis=0, concat_axis=0, tiled=True)  44.9 us
    pallas_call x4, Pallas kernels, local_factors(): pl.pallas_call(functools.partial(local_kernel, by_head, features, first),...  27.8 us
    all_to_all x2, starting transfers between devices, prior_states(): ends = lax.all_to_all(payload, SEQ, split_axis=0, concat_axis=0, tiled=True)  13.6 us
    ppermute x6, starting transfers between devices, sum_over_head(): lax.ppermute(value, 'head', [(at, at ^ step) for at in range(devices)])  12.6 us
    pallas_call x2, Pallas kernels, gated_outputs(): pl.pallas_call(functools.partial(gated_kernel, first_layer), in_specs=[HB...  11.1 us
    pallas_call x2, Pallas kernels, device_states(): pl.pallas_call(functools.partial(states_kernel, by_head, features), in_sp...  8.87 us
    all_to_all x2, waiting for transfers between devices, prior_states(): ends = lax.all_to_all(payload, SEQ, split_axis=0, concat_axis=0, tiled=True)  8.01 us
    all_to_all x2, starting transfers between devices, prior_states(): prior = lax.all_to_all(prior, SEQ, split_axis=0, concat_axis=0, tiled=True)  7.99 us
  transfers between devices with their start and end apart: 10, of which 8 were waited for; matrix products, arithmetic and copies ran while one was open for 0% of the time, Pallas kernels for 19%

profile of v5, /device:TPU:1, one launch (start us, length us, event | category | flops | bytes accessed | tf_op | source)
XLA Modules:
  0.0 149.8 jit_solution(17355604387152194241)
XLA Ops:
  0.0 4.4 %states.2 = (f32[32,32,128]{2,1,0:T(8,128)}, f32[4,768,128]{2,1,0:T(8,128)}) custom-call(bf16[1024,1536]{1,0:T(8,128)(2,1)} %bitcast.8, bf16[64,1024]{1,0:T(8,128)(2,1)} %refs_1_.5, f32[12,1024]{1,0:T(8,128)} %refs_3_.5, f32[12,1024]{1,0:T(8,128)} %refs_4_.3), custom_call_target="tpu_custom_call" | custom-call | flops 500000000 | bytes 6000000 | tf_op jit(solution)/shard_map/states/pallas_call | solution.py:167
  4.4 9.7 %all-to-all-start = ((f32[32,32,128]{2,1,0:T(8,128)}), f32[32,32,128]{2,1,0:T(8,128)S(1)}, u32[]{:S(2)}, u32[]{:S(2)}) async-start(f32[32,32,128]{2,1,0:T(8,128)} %get-tuple-element.27), calls=%async_computation | async-start | bytes 1048576 | tf_op jit(solution)/shard_map/all_to_all | solution.py:206
  14.1 6.9 %local.4 = (f32[5,1024,384]{2,1,0:T(8,128)}, bf16[4,1024,384]{2,1,0:T(8,128)(2,1)}) custom-call(bf16[1024,1536]{1,0:T(8,128)(2,1)} %bitcast.9, bf16[64,1024]{1,0:T(8,128)(2,1)} %refs_1_.5, bf16[64,1024]{1,0:T(8,128)(2,1)} %refs_2_.5, f32[12,1024]{1,0:T(8,128)} %refs_3_.5, f32[12,1024]{1,0:T(8,128)} %refs_4_.3, bf16[1024,1536]{1,0:T(8,128)(2,1)} %bitcast.11, ...), custom_call_target="tpu_custom_call" | custom-call | flops 3000000000 | bytes 10000000 | tf_op jit(solution)/shard_map/local/pallas_call | solution.py:323
  21.0 3.8 %all-to-all-done.ends_ref = f32[32,32,128]{2,1,0:T(8,128)S(1)} async-done(((f32[32,32,128]{2,1,0:T(8,128)}), f32[32,32,128]{2,1,0:T(8,128)S(1)}, u32[]{:S(2)}, u32[]{:S(2)}) %all-to-all-start) | async-done | bytes 524320 | tf_op jit(solution)/shard_map/all_to_all | solution.py:206
  24.8 0.8 prefix.2
  25.7 3.9 %all-to-all-start.1 = ((f32[32,24,128]{2,1,0:T(8,128)}), f32[32,24,128]{2,1,0:T(8,128)S(1)}, u32[]{:S(2)}, u32[]{:S(2)}) async-start(f32[32,24,128]{2,1,0:T(8,128)} %prefix.2), calls=%async_computation.1 | async-start | bytes 786432 | tf_op jit(solution)/shard_map/all_to_all | solution.py:214
  29.6 7.0 %local.5 = (f32[5,1024,384]{2,1,0:T(8,128)}, bf16[4,1024,384]{2,1,0:T(8,128)(2,1)}) custom-call(bf16[1024,1536]{1,0:T(8,128)(2,1)} %bitcast.10, bf16[64,1024]{1,0:T(8,128)(2,1)} %refs_1_.5, bf16[64,1024]{1,0:T(8,128)(2,1)} %refs_2_.5, f32[12,1024]{1,0:T(8,128)} %refs_3_.5, f32[12,1024]{1,0:T(8,128)} %refs_4_.3, ...), custom_call_target="tpu_custom_call", output_to_operand_aliasing={{0}: (8, {}), {1}: (9, {})} | custom-call | flops 3000000000 | bytes 10000000 | tf_op jit(solution)/shard_map/local/pallas_call | solution.py:323
  36.6 2.0 %all-to-all-done.1 = f32[32,24,128]{2,1,0:T(8,128)S(1)} async-done(((f32[32,24,128]{2,1,0:T(8,128)}), f32[32,24,128]{2,1,0:T(8,128)S(1)}, u32[]{:S(2)}, u32[]{:S(2)}) %all-to-all-start.1) | async-done | bytes 393248 | tf_op jit(solution)/shard_map/all_to_all | solution.py:214
  38.6 6.4 %gated.2 = bf16[32,400,128]{2,1,0:T(8,128)(2,1)} custom-call(f32[5,1024,384]{2,1,0:T(8,128)} %get-tuple-element.34.own_hbm, bf16[4,1024,384]{2,1,0:T(8,128)(2,1)} %get-tuple-element.35.factor_hbm, f32[768,128]{1,0:T(8,128)S(1)} %bitcast.7), custom_call_target="tpu_custom_call" | custom-call | flops 1200000000 | bytes 13000000 | tf_op jit(solution)/shard_map/gated/pallas_call | solution.py:468
  45.0 0.0 copy-start.1
  45.1 44.9 %all_to_all.25.x_ref.refs_0_ = bf16[32,400,128]{2,1,0:T(8,128)(2,1)S(1)} all-to-all(bf16[32,400,128]{2,1,0:T(8,128)(2,1)} %gated.2), channel_id=1, replica_groups=mesh['seq_0'=4,'seq_1'=4,'seq_2'=2,'head'=4] {'seq_0','seq_1','seq_2'}, dimensions={0} | all-to-all | bytes 6553600 | tf_op jit(solution)/shard_map/all_to_all | solution.py:565
  90.0 0.0 copy-start
  90.0 0.1 fusion
  90.1 0.1 add.32
  90.2 3.2 %collective-permute-start = (f32[8,128]{1,0:T(8,128)S(1)}, f32[8,128]{1,0:T(8,128)S(1)}, u32[]{:S(2)}, u32[]{:S(2)}) collective-permute-start(f32[8,128]{1,0:T(8,128)S(1)} %add.32), channel_id=1, source_target_pairs={{0,1},{1,0},{2,3},{3,2},{4,5},{5,4},{6,7},{7,6},{8,9},{9,8},{10,11... | collective-permute-start | bytes 12296 | tf_op jit(solution)/shard_map/ppermute | solution.py:529
  93.4 2.6 %collective-permute-start.1 = (f32[8,128]{1,0:T(8,128)S(1)}, f32[8,128]{1,0:T(8,128)S(1)}, u32[]{:S(2)}, u32[]{:S(2)}) collective-permute-start(f32[8,128]{1,0:T(8,128)S(1)} %add.32), channel_id=1, source_target_pairs={{0,2},{1,3},{2,0},{3,1},{4,6},{5,7},{6,4},{7,5},{8,10},{9,11},{10,... | collective-permute-start | bytes 12296 | tf_op jit(solution)/shard_map/ppermute | solution.py:529
  96.0 0.6 collective-permute-start.2
  96.6 0.0 copy-done.1
  96.6 0.6 broadcast_in_dim.6.refs_1_.refs_9_
  97.2 0.0 collective-permute-done
  97.2 0.1 collective-permute-done.1
  97.3 3.2 %collective-permute-done.2 = f32[8,128]{1,0:T(8,128)S(1)} collective-permute-done((f32[8,128]{1,0:T(8,128)S(1)}, f32[8,128]{1,0:T(8,128)S(1)}, u32[]{:S(2)}, u32[]{:S(2)}) %collective-permute-start.2) | collective-permute-done | bytes 4128 | tf_op jit(solution)/shard_map/ppermute | solution.py:529
  100.5 0.6 add_add_fusion.1.refs_0_.refs_8_
  101.1 0.0 copy-done
  101.1 4.5 %states.3 = (f32[32,32,128]{2,1,0:T(8,128)}, f32[4,768,128]{2,1,0:T(8,128)}) custom-call(bf16[32,400,128]{2,1,0:T(8,128)(2,1)} %copy-done, bf16[64,1024]{1,0:T(8,128)(2,1)} %refs_1_.7, f32[12,1024]{1,0:T(8,128)} %refs_3_.7, f32[12,1024]{1,0:T(8,128)} %refs_4_.5, f32[8,128]{1,0:T(8,128)} %add_add_fusion.1.refs_0_.refs_8_, ...), custom_call_target="tpu_custom_call" | custom-call | flops 500000000 | bytes 6000000 | tf_op jit(solution)/shard_map/states/pallas_call | solution.py:167
  105.6 3.9 %all-to-all-start.3 = ((f32[32,32,128]{2,1,0:T(8,128)}), f32[32,32,128]{2,1,0:T(8,128)S(1)}, u32[]{:S(2)}, u32[]{:S(2)}) async-start(f32[32,32,128]{2,1,0:T(8,128)} %get-tuple-element.37), calls=%async_computation.3 | async-start | bytes 1048576 | tf_op jit(solution)/shard_map/all_to_all | solution.py:206
  109.5 6.9 %local.6 = (f32[5,1024,384]{2,1,0:T(8,128)}, bf16[4,1024,384]{2,1,0:T(8,128)(2,1)}) custom-call(bf16[32,400,128]{2,1,0:T(8,128)(2,1)} %copy-done, bf16[64,1024]{1,0:T(8,128)(2,1)} %refs_1_.7, bf16[64,1024]{1,0:T(8,128)(2,1)} %refs_2_.7, f32[12,1024]{1,0:T(8,128)} %refs_3_.7, f32[12,1024]{1,0:T(8,128)} %refs_4_.5, bf16[1024,1536]{1,0:T(8,128)(2,1)} %bitcast.13, ...), custom_call_target="tpu_custom_call" | custom-call | flops 3000000000 | bytes 10000000 | tf_op jit(solution)/shard_map/local/pallas_call | solution.py:323
  116.5 4.2 %all-to-all-done.3.ends_ref = f32[32,32,128]{2,1,0:T(8,128)S(1)} async-done(((f32[32,32,128]{2,1,0:T(8,128)}), f32[32,32,128]{2,1,0:T(8,128)S(1)}, u32[]{:S(2)}, u32[]{:S(2)}) %all-to-all-start.3) | async-done | bytes 524320 | tf_op jit(solution)/shard_map/all_to_all | solution.py:206
  120.7 0.9 prefix.3
  121.6 4.1 %all-to-all-start.4 = ((f32[32,24,128]{2,1,0:T(8,128)}), f32[32,24,128]{2,1,0:T(8,128)S(1)}, u32[]{:S(2)}, u32[]{:S(2)}) async-start(f32[32,24,128]{2,1,0:T(8,128)} %prefix.3), calls=%async_computation.4 | async-start | bytes 786432 | tf_op jit(solution)/shard_map/all_to_all | solution.py:214
  125.6 7.0 %local.7 = (f32[5,1024,384]{2,1,0:T(8,128)}, bf16[4,1024,384]{2,1,0:T(8,128)(2,1)}) custom-call(bf16[32,400,128]{2,1,0:T(8,128)(2,1)} %copy-done, bf16[64,1024]{1,0:T(8,128)(2,1)} %refs_1_.7, bf16[64,1024]{1,0:T(8,128)(2,1)} %refs_2_.7, f32[12,1024]{1,0:T(8,128)} %refs_3_.7, f32[12,1024]{1,0:T(8,128)} %refs_4_.5, ...), custom_call_target="tpu_custom_call", output_to_operand_aliasing={{0}: (10, {}), {1}: (11, {})} | custom-call | flops 3000000000 | bytes 10000000 | tf_op jit(solution)/shard_map/local/pallas_call | solution.py:323
  132.6 1.8 %all-to-all-done.4 = f32[32,24,128]{2,1,0:T(8,128)S(1)} async-done(((f32[32,24,128]{2,1,0:T(8,128)}), f32[32,24,128]{2,1,0:T(8,128)S(1)}, u32[]{:S(2)}, u32[]{:S(2)}) %all-to-all-start.4) | async-done | bytes 393248 | tf_op jit(solution)/shard_map/all_to_all | solution.py:214
  134.5 0.0 copy-start.2
  134.5 4.7 %gated.3 = (bf16[4,1024,384]{2,1,0:T(8,128)(2,1)S(1)}, f32[1,1024]{1,0:T(1,128)S(1)}) custom-call(f32[5,1024,384]{2,1,0:T(8,128)} %get-tuple-element.44.own_hbm, bf16[4,1024,384]{2,1,0:T(8,128)(2,1)} %get-tuple-element.45.factor_hbm, f32[768,128]{1,0:T(8,128)S(1)} %bitcast.6), custom_call_target="tpu_custom_call" | custom-call | flops 1200000000 | bytes 13000000 | tf_op jit(solution)/shard_map/gated/pallas_call | solution.py:468
  139.2 2.9 %collective-permute-start.3 = (f32[1,1024]{1,0:T(1,128)S(1)}, f32[1,1024]{1,0:T(1,128)S(1)}, u32[]{:S(2)}, u32[]{:S(2)}) collective-permute-start(f32[1,1024]{1,0:T(1,128)S(1)} %get-tuple-element.48), channel_id=1, source_target_pairs={{0,1},{1,0},{2,3},{3,2},{4,5},{5,4},{6,7},{7,6},{8,9},{9,8},{10,11... | collective-permute-start | bytes 12296 | tf_op jit(solution)/shard_map/ppermute | solution.py:529
  142.2 0.7 collective-permute-start.4
  142.8 2.5 %collective-permute-start.5 = (f32[1,1024]{1,0:T(1,128)S(1)}, f32[1,1024]{1,0:T(1,128)S(1)}, u32[]{:S(2)}, u32[]{:S(2)}) collective-permute-start(f32[1,1024]{1,0:T(1,128)S(1)} %get-tuple-element.48), channel_id=1, source_target_pairs={{0,3},{1,2},{2,1},{3,0},{4,7},{5,6},{6,5},{7,4},{8,11},{9,10},{10,... | collective-permute-start | bytes 12296 | tf_op jit(solution)/shard_map/ppermute | solution.py:529
  145.4 0.0 copy-done.2
  145.4 0.0 collective-permute-done.3
  145.4 0.7 collective-permute-done.4
  146.1 1.2 collective-permute-done.5
  147.4 2.3 %scaled.1 = bf16[1024,1536]{1,0:T(8,128)(2,1)} custom-call(bf16[4,1024,384]{2,1,0:T(8,128)(2,1)S(1)} %get-tuple-element.47.gated_ref, f32[1,1024]{1,0:T(1,128)S(1)} %add_add_fusion.squares_ref, f32[1,1536]{1,0:T(1,128)S(1)} %broadcast_in_dim.7.gain_ref), custom_call_target="tpu_custom_call" | custom-call | tf_op jit(solution)/shard_map/scaled/pallas_call | solution.py:511
  (3 shorter events, 0.0 us)
Async XLA Ops:
  4.4 20.4 %all-to-all-start = ((f32[32,32,128]{2,1,0:T(8,128)}), f32[32,32,128]{2,1,0:T(8,128)S(1)}, u32[]{:S(2)}, u32[]{:S(2)}) async-start(f32[32,32,128]{2,1,0:T(8,128)} %get-tuple-element.27), calls=%async_computation | async-start | bytes 1048576 | tf_op jit(solution)/shard_map/all_to_all | solution.py:206
  25.7 13.0 %all-to-all-start.1 = ((f32[32,24,128]{2,1,0:T(8,128)}), f32[32,24,128]{2,1,0:T(8,128)S(1)}, u32[]{:S(2)}, u32[]{:S(2)}) async-start(f32[32,24,128]{2,1,0:T(8,128)} %prefix.2), calls=%async_computation.1 | async-start | bytes 786432 | tf_op jit(solution)/shard_map/all_to_all | solution.py:214
  45.0 51.5 %copy-start.1 = (f32[1536]{0:T(1024)S(1)}, f32[1536]{0:T(1024)}, u32[]{:S(2)}) copy-start(f32[1536]{0:T(1024)} %param.23) | copy-start | bytes 18436
  90.0 11.1 %copy-start = (bf16[32,400,128]{2,1,0:T(8,128)(2,1)}, bf16[32,400,128]{2,1,0:T(8,128)(2,1)S(1)}, u32[]{:S(2)}) copy-start(bf16[32,400,128]{2,1,0:T(8,128)(2,1)S(1)} %all_to_all.25.x_ref.refs_0_) | copy-start | bytes 9830404
  90.2 7.0 %collective-permute-start = (f32[8,128]{1,0:T(8,128)S(1)}, f32[8,128]{1,0:T(8,128)S(1)}, u32[]{:S(2)}, u32[]{:S(2)}) collective-permute-start(f32[8,128]{1,0:T(8,128)S(1)} %add.32), channel_id=1, source_target_pairs={{0,1},{1,0},{2,3},{3,2},{4,5},{5,4},{6,7},{7,6},{8,9},{9,8},{10,11... | collective-permute-start | bytes 12296 | tf_op jit(solution)/shard_map/ppermute | solution.py:529
  93.4 4.0 %collective-permute-start.1 = (f32[8,128]{1,0:T(8,128)S(1)}, f32[8,128]{1,0:T(8,128)S(1)}, u32[]{:S(2)}, u32[]{:S(2)}) collective-permute-start(f32[8,128]{1,0:T(8,128)S(1)} %add.32), channel_id=1, source_target_pairs={{0,2},{1,3},{2,0},{3,1},{4,6},{5,7},{6,4},{7,5},{8,10},{9,11},{10,... | collective-permute-start | bytes 12296 | tf_op jit(solution)/shard_map/ppermute | solution.py:529
  96.0 4.5 %collective-permute-start.2 = (f32[8,128]{1,0:T(8,128)S(1)}, f32[8,128]{1,0:T(8,128)S(1)}, u32[]{:S(2)}, u32[]{:S(2)}) collective-permute-start(f32[8,128]{1,0:T(8,128)S(1)} %add.32), channel_id=1, source_target_pairs={{0,3},{1,2},{2,1},{3,0},{4,7},{5,6},{6,5},{7,4},{8,11},{9,10},{10,... | collective-permute-start | bytes 12296 | tf_op jit(solution)/shard_map/ppermute | solution.py:529
  105.6 15.1 %all-to-all-start.3 = ((f32[32,32,128]{2,1,0:T(8,128)}), f32[32,32,128]{2,1,0:T(8,128)S(1)}, u32[]{:S(2)}, u32[]{:S(2)}) async-start(f32[32,32,128]{2,1,0:T(8,128)} %get-tuple-element.37), calls=%async_computation.3 | async-start | bytes 1048576 | tf_op jit(solution)/shard_map/all_to_all | solution.py:206
  121.6 12.9 %all-to-all-start.4 = ((f32[32,24,128]{2,1,0:T(8,128)}), f32[32,24,128]{2,1,0:T(8,128)S(1)}, u32[]{:S(2)}, u32[]{:S(2)}) async-start(f32[32,24,128]{2,1,0:T(8,128)} %prefix.3), calls=%async_computation.4 | async-start | bytes 786432 | tf_op jit(solution)/shard_map/all_to_all | solution.py:214
  134.5 10.9 %copy-start.2 = (f32[1536]{0:T(1024)S(1)}, f32[1536]{0:T(1024)}, u32[]{:S(2)}) copy-start(f32[1536]{0:T(1024)} %param.29) | copy-start | bytes 18436
  139.2 6.2 %collective-permute-start.3 = (f32[1,1024]{1,0:T(1,128)S(1)}, f32[1,1024]{1,0:T(1,128)S(1)}, u32[]{:S(2)}, u32[]{:S(2)}) collective-permute-start(f32[1,1024]{1,0:T(1,128)S(1)} %get-tuple-element.48), channel_id=1, source_target_pairs={{0,1},{1,0},{2,3},{3,2},{4,5},{5,4},{6,7},{7,6},{8,9},{9,8},{10,11... | collective-permute-start | bytes 12296 | tf_op jit(solution)/shard_map/ppermute | solution.py:529
  142.2 4.0 %collective-permute-start.4 = (f32[1,1024]{1,0:T(1,128)S(1)}, f32[1,1024]{1,0:T(1,128)S(1)}, u32[]{:S(2)}, u32[]{:S(2)}) collective-permute-start(f32[1,1024]{1,0:T(1,128)S(1)} %get-tuple-element.48), channel_id=1, source_target_pairs={{0,2},{1,3},{2,0},{3,1},{4,6},{5,7},{6,4},{7,5},{8,10},{9,11},{10,... | collective-permute-start | bytes 12296 | tf_op jit(solution)/shard_map/ppermute | solution.py:529
  142.8 4.5 %collective-permute-start.5 = (f32[1,1024]{1,0:T(1,128)S(1)}, f32[1,1024]{1,0:T(1,128)S(1)}, u32[]{:S(2)}, u32[]{:S(2)}) collective-permute-start(f32[1,1024]{1,0:T(1,128)S(1)} %get-tuple-element.48), channel_id=1, source_target_pairs={{0,3},{1,2},{2,1},{3,0},{4,7},{5,6},{6,5},{7,4},{8,11},{9,10},{10,... | collective-permute-start | bytes 12296 | tf_op jit(solution)/shard_map/ppermute | solution.py:529

commit v6 on v5

--- a/solution.py
+++ b/solution.py
@@ -67,9 +67,9 @@
     return x_ref[:, head * LANES : (head + 1) * LANES]
 
 
-def block_scale(squares_ref, block, features):
+def block_scale(squares_refs, block, features):
     rows = BLOCK // LANES
-    squares = squares_ref[pl.ds(block * rows, rows), :]
+    squares = sum(ref[pl.ds(block * rows, rows), :] for ref in squares_refs)
     pieces = [squares[row : row + 1, :] for row in range(rows)]
     return norm_scale(jnp.concatenate(pieces, axis=1), features)
 
@@ -84,7 +84,7 @@
 
 def states_kernel(by_head, features, x_ref, write_hbm, step_hbm, decay_hbm, *refs):
     if by_head:
-        squares_hbm, gain_hbm, payload_hbm, before_hbm, gain_ref, squares_ref, x_in, write_ref, step_ref, decay_ref, before, payload, total, sent, got = refs
+        *squares_hbms, gain_hbm, payload_hbm, before_hbm, gain_ref, squares_ref, x_in, write_ref, step_ref, decay_ref, before, payload, total, sent, got = refs
     else:
         payload_hbm, before_hbm, x_in, write_ref, step_ref, decay_ref, before, payload, total, sent, got = refs
     head_count = step_ref.shape[0]
@@ -92,7 +92,8 @@
     blocks = before.shape[0] - 1
     pairs = ((decay_hbm, decay_ref), (step_hbm, step_ref), (write_hbm, write_ref))
     if by_head:
-        pairs += ((squares_hbm, squares_ref), (gain_hbm, gain_ref))
+        squares_refs = [squares_ref.at[at] for at in range(len(squares_hbms))]
+        pairs += ((gain_hbm, gain_ref), *zip(squares_hbms, squares_refs))
     small = [pltpu.make_async_copy(*pair, got.at[at]) for at, pair in enumerate(pairs)]
 
     def x_copy(block):
@@ -119,7 +120,7 @@
         final = cumulative[:, BLOCK - 1 :]
         weights = jnp.exp(final - cumulative) * step_ref[:, positions]
         if by_head:
-            weights = weights * block_scale(squares_ref, block, features)
+            weights = weights * block_scale(squares_refs, block, features)
         x_copy(block).wait()
         x_block = x_in.at[block]
         fading = jnp.broadcast_to(jnp.exp(final), (head_count, LANES))
@@ -160,9 +161,9 @@
     operands = [x, write, step, decay]
     scratch = []
     if by_head:
-        specs += [HBM, HBM]
-        operands += [squares, gain]
-        scratch += [pltpu.VMEM(gain.shape, F32), pltpu.VMEM(squares.shape, F32)]
+        specs += [HBM] * (len(squares) + 1)
+        operands += [*squares, gain]
+        scratch += [pltpu.VMEM(gain.shape, F32), pltpu.VMEM((len(squares), *squares[0].shape), F32)]
     scratch.append(pltpu.VMEM((blocks, x.shape[0] // blocks, *x.shape[1:]), BF16))
     return pl.pallas_call(
         functools.partial(states_kernel, by_head, features),
@@ -181,7 +182,7 @@
             pltpu.VMEM((devices, height + TILE, LANES), F32),
             pltpu.VMEM((head_count, LANES), F32),
             pltpu.SemaphoreType.DMA((blocks + 1,)),
-            pltpu.SemaphoreType.DMA((5 + blocks,)),
+            pltpu.SemaphoreType.DMA((len(operands) + blocks,)),
         ],
         compiler_params=params(),
         cost_estimate=pl.CostEstimate(flops=500_000_000, bytes_accessed=6_000_000, transcendentals=20_000),
@@ -220,10 +221,10 @@
     return jnp.dot(reads, parts, preferred_element_type=F32)
 
 
-def local_kernel(by_head, features, first, *refs):
+def local_kernel(by_head, features, first, parts, *refs):
     x_ref, write_ref, read_ref, step_ref, decay_ref, gate_ref, before_ref, skip_ref = refs[:8]
     if by_head:
-        squares_ref, gain_ref = refs[8:10]
+        *squares_refs, gain_ref = refs[8 : 9 + parts]
     own_ref, factor_ref, total = refs[-3:]
     head_count = step_ref.shape[0]
     state_size = write_ref.shape[0]
@@ -240,7 +241,7 @@
     cumulative = running_sums(decay_ref[:, pl.ds(pl.multiple_of(block * BLOCK, BLOCK), BLOCK)])
     step = step_ref[...]
     if by_head:
-        scale = block_scale(squares_ref, block, features)
+        scale = block_scale(squares_refs, block, features)
         step = step * scale
         scale_column = jnp.transpose(jnp.broadcast_to(scale, (LANES, BLOCK)))
     padding = jnp.zeros((LANES - head_count, BLOCK), F32)
@@ -314,14 +315,14 @@
     ]
     operands = [x, write, read, step, decay, gate, before, skip]
     if by_head:
-        specs.append(pl.BlockSpec(squares.shape, lambda k: (0, 0)))
+        specs += [pl.BlockSpec(part.shape, lambda k: (0, 0)) for part in squares]
         specs.append(pl.BlockSpec((1, width), lambda k: (0, 0)))
-        operands += [squares, gain]
+        operands += [*squares, gain]
     part = HEADS_PER_STEP * LANES
     groups = width // part
     aliases = {len(operands) + at: at for at in range(len(done))}
     return pl.pallas_call(
-        functools.partial(local_kernel, by_head, features, first),
+        functools.partial(local_kernel, by_head, features, first, len(squares) if by_head else 0),
         grid=(count,),
         in_specs=specs + [HBM] * len(done),
         input_output_aliases=aliases,
@@ -410,7 +411,7 @@
         ordered = jnp.concatenate([total[pl.ds(col, rows, stride=cols), :] for col in range(cols)], axis=0)
     ones = jnp.ones((TILE, LANES), BF16)
     sums = jnp.zeros((TILE, length), F32)
-    for part in split_three(ordered):
+    for part in split_two(ordered):
         sums = sums + lax.dot_general(ones, part, (((1,), (1,)), ((), ())), preferred_element_type=F32)
     if first_layer:
         high, middle, low = [part.astype(F32) for part in split_three(sums)]
@@ -479,7 +480,8 @@
     )(own, factor, prior)
 
 
-def scaled_kernel(features, gated_ref, squares_ref, gain_ref, out_hbm, out_in, sent):
+def scaled_kernel(features, gated_ref, gain_ref, *refs):
+    *squares_refs, out_hbm, out_in, sent = refs
     parts, rows, width = out_in.shape
     part_lanes = gated_ref.shape[2]
 
@@ -489,7 +491,7 @@
 
     def advance(part, carry):
         at = pl.ds(pl.multiple_of(part * rows, rows), rows)
-        scale = norm_scale(squares_ref[:, at], features)
+        scale = norm_scale(sum(ref[:, at] for ref in squares_refs), features)
         column = jnp.transpose(jnp.broadcast_to(scale, (LANES, rows)))
         for head in range(width // LANES):
             place = slice(head * LANES, (head + 1) * LANES)
@@ -510,7 +512,7 @@
     parts = length // SCALED_ROWS
     return pl.pallas_call(
         functools.partial(scaled_kernel, features),
-        in_specs=[VMEM, VMEM, VMEM],
+        in_specs=[VMEM] * (2 + len(squares)),
         out_specs=HBM,
         out_shape=jax.ShapeDtypeStruct((length, width), BF16),
         scratch_shapes=[
@@ -519,15 +521,15 @@
         ],
         compiler_params=params(48),
         name="scaled",
-    )(gated, squares, gain)
-
-
-def sum_over_head(value):
+    )(gated, gain, *squares)
+
+
+def over_head(value):
     devices = lax.axis_size("head")
-    total = value
-    for step in range(1, devices):
-        total = total + lax.ppermute(value, "head", [(at, at ^ step) for at in range(devices)])
-    return total
+    others = [
+        lax.ppermute(value, "head", [(at, at ^ step) for at in range(devices)]) for step in range(1, devices)
+    ]
+    return [value, *others]
 
 
 def body(
@@ -565,7 +567,7 @@
     hidden = lax.all_to_all(hidden, SEQ, split_axis=0, concat_axis=0, tiled=True)
     squares = hidden[:, -EXTRA : 3 - EXTRA, :grid_rows].astype(F32)
     squares = (squares[:, 0] + squares[:, 1] + squares[:, 2]).reshape(-1, LANES)
-    squares = sum_over_head(squares)
+    squares = [sum(over_head(squares))]
 
     gain = norm_rows[None]
     payload, before = device_states(
@@ -578,7 +580,7 @@
     )
     prior, done, decay = prior_states(payload, local(0, decay_cols, ()), decay_cols)
     gated, last_squares = gated_outputs(False, *local(half, decay, done), prior, 1)
-    last_squares = sum_over_head(last_squares)
+    last_squares = over_head(last_squares)
     out = scaled_outputs(gated, last_squares, norm_cols[None], features)
     return out.reshape(column_len, 1, width)
 

time: 150 us -> 150 us (level)
  no operation moved by 1% of the time
where the time goes in v6:
time: 150 us
  Pallas kernels  51.7 us (34%)
  blocking collectives  44.9 us (30%)
  starting transfers between devices  34.2 us (23%)
  waiting for transfers between devices  17.2 us (11%)
    all_to_all x1, blocking collectives, body(): lax.all_to_all(hidden, SEQ, split_axis=0, concat_axis=0, tiled=True)  44.9 us
    pallas_call x4, Pallas kernels, local_factors(): pl.pallas_call(functools.partial(local_kernel, by_head, features, first,...  27.8 us
    all_to_all x2, starting transfers between devices, prior_states(): ends = lax.all_to_all(payload, SEQ, split_axis=0, concat_axis=0, tiled=True)  13.6 us
    ppermute x6, starting transfers between devices, over_head(): lax.ppermute(value, 'head', [(at, at ^ step) for at in range(devices)])  12.6 us
    pallas_call x2, Pallas kernels, gated_outputs(): pl.pallas_call(functools.partial(gated_kernel, first_layer), in_specs=[HB...  11 us
    pallas_call x2, Pallas kernels, device_states(): pl.pallas_call(functools.partial(states_kernel, by_head, features), in_sp...  8.87 us
    all_to_all x2, waiting for transfers between devices, prior_states(): ends = lax.all_to_all(payload, SEQ, split_axis=0, concat_axis=0, tiled=True)  8.01 us
    all_to_all x2, starting transfers between devices, prior_states(): prior = lax.all_to_all(prior, SEQ, split_axis=0, concat_axis=0, tiled=True)  7.99 us
  transfers between devices with their start and end apart: 10, of which 8 were waited for; matrix products, arithmetic and copies ran while one was open for 0% of the time, Pallas kernels for 19%

profile of v6, /device:TPU:1, one launch (start us, length us, event | category | flops | bytes accessed | tf_op | source)
XLA Modules:
  0.0 149.7 jit_solution(15843966511320057572)
XLA Ops:
  0.0 4.4 %states.2 = (f32[32,32,128]{2,1,0:T(8,128)}, f32[4,768,128]{2,1,0:T(8,128)}) custom-call(bf16[1024,1536]{1,0:T(8,128)(2,1)} %bitcast.8, bf16[64,1024]{1,0:T(8,128)(2,1)} %refs_1_.5, f32[12,1024]{1,0:T(8,128)} %refs_3_.5, f32[12,1024]{1,0:T(8,128)} %refs_4_.3), custom_call_target="tpu_custom_call" | custom-call | flops 500000000 | bytes 6000000 | tf_op jit(solution)/shard_map/states/pallas_call | solution.py:168
  4.4 9.7 %all-to-all-start = ((f32[32,32,128]{2,1,0:T(8,128)}), f32[32,32,128]{2,1,0:T(8,128)S(1)}, u32[]{:S(2)}, u32[]{:S(2)}) async-start(f32[32,32,128]{2,1,0:T(8,128)} %get-tuple-element.27), calls=%async_computation | async-start | bytes 1048576 | tf_op jit(solution)/shard_map/all_to_all | solution.py:207
  14.1 6.9 %local.4 = (f32[5,1024,384]{2,1,0:T(8,128)}, bf16[4,1024,384]{2,1,0:T(8,128)(2,1)}) custom-call(bf16[1024,1536]{1,0:T(8,128)(2,1)} %bitcast.9, bf16[64,1024]{1,0:T(8,128)(2,1)} %refs_1_.5, bf16[64,1024]{1,0:T(8,128)(2,1)} %refs_2_.5, f32[12,1024]{1,0:T(8,128)} %refs_3_.5, f32[12,1024]{1,0:T(8,128)} %refs_4_.3, bf16[1024,1536]{1,0:T(8,128)(2,1)} %bitcast.11, ...), custom_call_target="tpu_custom_call" | custom-call | flops 3000000000 | bytes 10000000 | tf_op jit(solution)/shard_map/local/pallas_call | solution.py:324
  21.0 3.8 %all-to-all-done.ends_ref = f32[32,32,128]{2,1,0:T(8,128)S(1)} async-done(((f32[32,32,128]{2,1,0:T(8,128)}), f32[32,32,128]{2,1,0:T(8,128)S(1)}, u32[]{:S(2)}, u32[]{:S(2)}) %all-to-all-start) | async-done | bytes 524320 | tf_op jit(solution)/shard_map/all_to_all | solution.py:207
  24.8 0.8 prefix.2
  25.7 3.9 %all-to-all-start.1 = ((f32[32,24,128]{2,1,0:T(8,128)}), f32[32,24,128]{2,1,0:T(8,128)S(1)}, u32[]{:S(2)}, u32[]{:S(2)}) async-start(f32[32,24,128]{2,1,0:T(8,128)} %prefix.2), calls=%async_computation.1 | async-start | bytes 786432 | tf_op jit(solution)/shard_map/all_to_all | solution.py:215
  29.6 7.0 %local.5 = (f32[5,1024,384]{2,1,0:T(8,128)}, bf16[4,1024,384]{2,1,0:T(8,128)(2,1)}) custom-call(bf16[1024,1536]{1,0:T(8,128)(2,1)} %bitcast.10, bf16[64,1024]{1,0:T(8,128)(2,1)} %refs_1_.5, bf16[64,1024]{1,0:T(8,128)(2,1)} %refs_2_.5, f32[12,1024]{1,0:T(8,128)} %refs_3_.5, f32[12,1024]{1,0:T(8,128)} %refs_4_.3, ...), custom_call_target="tpu_custom_call", output_to_operand_aliasing={{0}: (8, {}), {1}: (9, {})} | custom-call | flops 3000000000 | bytes 10000000 | tf_op jit(solution)/shard_map/local/pallas_call | solution.py:324
  36.6 2.0 %all-to-all-done.1 = f32[32,24,128]{2,1,0:T(8,128)S(1)} async-done(((f32[32,24,128]{2,1,0:T(8,128)}), f32[32,24,128]{2,1,0:T(8,128)S(1)}, u32[]{:S(2)}, u32[]{:S(2)}) %all-to-all-start.1) | async-done | bytes 393248 | tf_op jit(solution)/shard_map/all_to_all | solution.py:215
  38.6 6.3 %gated.2 = bf16[32,400,128]{2,1,0:T(8,128)(2,1)} custom-call(f32[5,1024,384]{2,1,0:T(8,128)} %get-tuple-element.34.own_hbm, bf16[4,1024,384]{2,1,0:T(8,128)(2,1)} %get-tuple-element.35.factor_hbm, f32[768,128]{1,0:T(8,128)S(1)} %bitcast.7), custom_call_target="tpu_custom_call" | custom-call | flops 1200000000 | bytes 13000000 | tf_op jit(solution)/shard_map/gated/pallas_call | solution.py:469
  44.9 0.0 copy-start.1
  45.0 44.9 %all_to_all.25.x_ref.refs_0_ = bf16[32,400,128]{2,1,0:T(8,128)(2,1)S(1)} all-to-all(bf16[32,400,128]{2,1,0:T(8,128)(2,1)} %gated.2), channel_id=1, replica_groups=mesh['seq_0'=4,'seq_1'=4,'seq_2'=2,'head'=4] {'seq_0','seq_1','seq_2'}, dimensions={0} | all-to-all | bytes 6553600 | tf_op jit(solution)/shard_map/all_to_all | solution.py:567
  89.9 0.0 copy-start
  89.9 0.1 fusion
  90.0 0.1 add.23
  90.1 3.2 %collective-permute-start = (f32[8,128]{1,0:T(8,128)S(1)}, f32[8,128]{1,0:T(8,128)S(1)}, u32[]{:S(2)}, u32[]{:S(2)}) collective-permute-start(f32[8,128]{1,0:T(8,128)S(1)} %add.23), channel_id=1, source_target_pairs={{0,1},{1,0},{2,3},{3,2},{4,5},{5,4},{6,7},{7,6},{8,9},{9,8},{10,11... | collective-permute-start | bytes 12296 | tf_op jit(solution)/shard_map/ppermute | solution.py:530
  93.3 2.6 %collective-permute-start.1 = (f32[8,128]{1,0:T(8,128)S(1)}, f32[8,128]{1,0:T(8,128)S(1)}, u32[]{:S(2)}, u32[]{:S(2)}) collective-permute-start(f32[8,128]{1,0:T(8,128)S(1)} %add.23), channel_id=1, source_target_pairs={{0,2},{1,3},{2,0},{3,1},{4,6},{5,7},{6,4},{7,5},{8,10},{9,11},{10,... | collective-permute-start | bytes 12296 | tf_op jit(solution)/shard_map/ppermute | solution.py:530
  95.9 0.6 collective-permute-start.2
  96.5 0.0 copy-done.1
  96.5 0.6 broadcast_in_dim.6.refs_1_.refs_9_
  97.1 0.0 collective-permute-done
  97.1 0.1 collective-permute-done.1
  97.2 3.2 %collective-permute-done.2 = f32[8,128]{1,0:T(8,128)S(1)} collective-permute-done((f32[8,128]{1,0:T(8,128)S(1)}, f32[8,128]{1,0:T(8,128)S(1)}, u32[]{:S(2)}, u32[]{:S(2)}) %collective-permute-start.2) | collective-permute-done | bytes 4128 | tf_op jit(solution)/shard_map/ppermute | solution.py:530
  100.4 0.6 add_add_fusion.refs_0_.refs_8_
  101.0 0.0 copy-done
  101.0 4.5 %states.3 = (f32[32,32,128]{2,1,0:T(8,128)}, f32[4,768,128]{2,1,0:T(8,128)}) custom-call(bf16[32,400,128]{2,1,0:T(8,128)(2,1)} %copy-done, bf16[64,1024]{1,0:T(8,128)(2,1)} %refs_1_.7, f32[12,1024]{1,0:T(8,128)} %refs_3_.7, f32[12,1024]{1,0:T(8,128)} %refs_4_.5, f32[8,128]{1,0:T(8,128)} %add_add_fusion.refs_0_.refs_8_, f32[1,1536]{1,0:T(1,128)} %broadcast_in_dim.6.refs_1_.refs_9_), custom_call_target="tpu_custom_call" | custom-call | flops 500000000 | bytes 6000000 | tf_op jit(solution)/shard_map/states/pallas_call | solution.py:168
  105.5 3.9 %all-to-all-start.3 = ((f32[32,32,128]{2,1,0:T(8,128)}), f32[32,32,128]{2,1,0:T(8,128)S(1)}, u32[]{:S(2)}, u32[]{:S(2)}) async-start(f32[32,32,128]{2,1,0:T(8,128)} %get-tuple-element.37), calls=%async_computation.3 | async-start | bytes 1048576 | tf_op jit(solution)/shard_map/all_to_all | solution.py:207
  109.4 6.9 %local.6 = (f32[5,1024,384]{2,1,0:T(8,128)}, bf16[4,1024,384]{2,1,0:T(8,128)(2,1)}) custom-call(bf16[32,400,128]{2,1,0:T(8,128)(2,1)} %copy-done, bf16[64,1024]{1,0:T(8,128)(2,1)} %refs_1_.7, bf16[64,1024]{1,0:T(8,128)(2,1)} %refs_2_.7, f32[12,1024]{1,0:T(8,128)} %refs_3_.7, f32[12,1024]{1,0:T(8,128)} %refs_4_.5, bf16[1024,1536]{1,0:T(8,128)(2,1)} %bitcast.13, ...), custom_call_target="tpu_custom_call" | custom-call | flops 3000000000 | bytes 10000000 | tf_op jit(solution)/shard_map/local/pallas_call | solution.py:324
  116.4 4.2 %all-to-all-done.3.ends_ref = f32[32,32,128]{2,1,0:T(8,128)S(1)} async-done(((f32[32,32,128]{2,1,0:T(8,128)}), f32[32,32,128]{2,1,0:T(8,128)S(1)}, u32[]{:S(2)}, u32[]{:S(2)}) %all-to-all-start.3) | async-done | bytes 524320 | tf_op jit(solution)/shard_map/all_to_all | solution.py:207
  120.6 0.9 prefix.3
  121.5 4.1 %all-to-all-start.4 = ((f32[32,24,128]{2,1,0:T(8,128)}), f32[32,24,128]{2,1,0:T(8,128)S(1)}, u32[]{:S(2)}, u32[]{:S(2)}) async-start(f32[32,24,128]{2,1,0:T(8,128)} %prefix.3), calls=%async_computation.4 | async-start | bytes 786432 | tf_op jit(solution)/shard_map/all_to_all | solution.py:215
  125.5 7.0 %local.7 = (f32[5,1024,384]{2,1,0:T(8,128)}, bf16[4,1024,384]{2,1,0:T(8,128)(2,1)}) custom-call(bf16[32,400,128]{2,1,0:T(8,128)(2,1)} %copy-done, bf16[64,1024]{1,0:T(8,128)(2,1)} %refs_1_.7, bf16[64,1024]{1,0:T(8,128)(2,1)} %refs_2_.7, f32[12,1024]{1,0:T(8,128)} %refs_3_.7, f32[12,1024]{1,0:T(8,128)} %refs_4_.5, ...), custom_call_target="tpu_custom_call", output_to_operand_aliasing={{0}: (10, {}), {1}: (11, {})} | custom-call | flops 3000000000 | bytes 10000000 | tf_op jit(solution)/shard_map/local/pallas_call | solution.py:324
  132.6 1.8 %all-to-all-done.4 = f32[32,24,128]{2,1,0:T(8,128)S(1)} async-done(((f32[32,24,128]{2,1,0:T(8,128)}), f32[32,24,128]{2,1,0:T(8,128)S(1)}, u32[]{:S(2)}, u32[]{:S(2)}) %all-to-all-start.4) | async-done | bytes 393248 | tf_op jit(solution)/shard_map/all_to_all | solution.py:215
  134.4 0.0 copy-start.2
  134.4 4.7 %gated.3 = (bf16[4,1024,384]{2,1,0:T(8,128)(2,1)S(1)}, f32[1,1024]{1,0:T(1,128)S(1)}) custom-call(f32[5,1024,384]{2,1,0:T(8,128)} %get-tuple-element.44.own_hbm, bf16[4,1024,384]{2,1,0:T(8,128)(2,1)} %get-tuple-element.45.factor_hbm, f32[768,128]{1,0:T(8,128)S(1)} %bitcast.6), custom_call_target="tpu_custom_call" | custom-call | flops 1200000000 | bytes 13000000 | tf_op jit(solution)/shard_map/gated/pallas_call | solution.py:469
  139.0 2.9 %collective-permute-start.3 = (f32[1,1024]{1,0:T(1,128)S(1)}, f32[1,1024]{1,0:T(1,128)S(1)}, u32[]{:S(2)}, u32[]{:S(2)}) collective-permute-start(f32[1,1024]{1,0:T(1,128)S(1)} %get-tuple-element.48.refs_0_), channel_id=1, source_target_pairs={{0,1},{1,0},{2,3},{3,2},{4,5},{5,4},{6,7},{7,6},{8,9},{9,8},{10,11... | collective-permute-start | bytes 12296 | tf_op jit(solution)/shard_map/ppermute | solution.py:530
  142.0 0.7 collective-permute-start.4
  142.7 2.5 %collective-permute-start.5 = (f32[1,1024]{1,0:T(1,128)S(1)}, f32[1,1024]{1,0:T(1,128)S(1)}, u32[]{:S(2)}, u32[]{:S(2)}) collective-permute-start(f32[1,1024]{1,0:T(1,128)S(1)} %get-tuple-element.48.refs_0_), channel_id=1, source_target_pairs={{0,3},{1,2},{2,1},{3,0},{4,7},{5,6},{6,5},{7,4},{8,11},{9,10},{10,... | collective-permute-start | bytes 12296 | tf_op jit(solution)/shard_map/ppermute | solution.py:530
  145.2 0.0 copy-done.2
  145.2 0.0 collective-permute-done.3.refs_1_
  145.2 0.7 collective-permute-done.4.refs_2_
  146.0 1.2 collective-permute-done.5.refs_3_
  147.2 2.3 %scaled.1 = bf16[1024,1536]{1,0:T(8,128)(2,1)} custom-call(bf16[4,1024,384]{2,1,0:T(8,128)(2,1)S(1)} %get-tuple-element.47.gated_ref, f32[1,1536]{1,0:T(1,128)S(1)} %broadcast_in_dim.7.gain_ref, f32[1,1024]{1,0:T(1,128)S(1)} %get-tuple-element.48.refs_0_, f32[1,1024]{1,0:T(1,128)S(1)} %collective-permute-done.3.refs_1_, ...), custom_call_target="tpu_custom_call" | custom-call | tf_op jit(solution)/shard_map/scaled/pallas_call | solution.py:513
  (2 shorter events, 0.0 us)
Async XLA Ops:
  4.4 20.4 %all-to-all-start = ((f32[32,32,128]{2,1,0:T(8,128)}), f32[32,32,128]{2,1,0:T(8,128)S(1)}, u32[]{:S(2)}, u32[]{:S(2)}) async-start(f32[32,32,128]{2,1,0:T(8,128)} %get-tuple-element.27), calls=%async_computation | async-start | bytes 1048576 | tf_op jit(solution)/shard_map/all_to_all | solution.py:207
  25.7 13.0 %all-to-all-start.1 = ((f32[32,24,128]{2,1,0:T(8,128)}), f32[32,24,128]{2,1,0:T(8,128)S(1)}, u32[]{:S(2)}, u32[]{:S(2)}) async-start(f32[32,24,128]{2,1,0:T(8,128)} %prefix.2), calls=%async_computation.1 | async-start | bytes 786432 | tf_op jit(solution)/shard_map/all_to_all | solution.py:215
  44.9 51.5 %copy-start.1 = (f32[1536]{0:T(1024)S(1)}, f32[1536]{0:T(1024)}, u32[]{:S(2)}) copy-start(f32[1536]{0:T(1024)} %param.23) | copy-start | bytes 18436
  89.9 11.1 %copy-start = (bf16[32,400,128]{2,1,0:T(8,128)(2,1)}, bf16[32,400,128]{2,1,0:T(8,128)(2,1)S(1)}, u32[]{:S(2)}) copy-start(bf16[32,400,128]{2,1,0:T(8,128)(2,1)S(1)} %all_to_all.25.x_ref.refs_0_) | copy-start | bytes 9830404
  90.1 7.0 %collective-permute-start = (f32[8,128]{1,0:T(8,128)S(1)}, f32[8,128]{1,0:T(8,128)S(1)}, u32[]{:S(2)}, u32[]{:S(2)}) collective-permute-start(f32[8,128]{1,0:T(8,128)S(1)} %add.23), channel_id=1, source_target_pairs={{0,1},{1,0},{2,3},{3,2},{4,5},{5,4},{6,7},{7,6},{8,9},{9,8},{10,11... | collective-permute-start | bytes 12296 | tf_op jit(solution)/shard_map/ppermute | solution.py:530
  93.3 4.0 %collective-permute-start.1 = (f32[8,128]{1,0:T(8,128)S(1)}, f32[8,128]{1,0:T(8,128)S(1)}, u32[]{:S(2)}, u32[]{:S(2)}) collective-permute-start(f32[8,128]{1,0:T(8,128)S(1)} %add.23), channel_id=1, source_target_pairs={{0,2},{1,3},{2,0},{3,1},{4,6},{5,7},{6,4},{7,5},{8,10},{9,11},{10,... | collective-permute-start | bytes 12296 | tf_op jit(solution)/shard_map/ppermute | solution.py:530
  95.9 4.5 %collective-permute-start.2 = (f32[8,128]{1,0:T(8,128)S(1)}, f32[8,128]{1,0:T(8,128)S(1)}, u32[]{:S(2)}, u32[]{:S(2)}) collective-permute-start(f32[8,128]{1,0:T(8,128)S(1)} %add.23), channel_id=1, source_target_pairs={{0,3},{1,2},{2,1},{3,0},{4,7},{5,6},{6,5},{7,4},{8,11},{9,10},{10,... | collective-permute-start | bytes 12296 | tf_op jit(solution)/shard_map/ppermute | solution.py:530
  105.5 15.1 %all-to-all-start.3 = ((f32[32,32,128]{2,1,0:T(8,128)}), f32[32,32,128]{2,1,0:T(8,128)S(1)}, u32[]{:S(2)}, u32[]{:S(2)}) async-start(f32[32,32,128]{2,1,0:T(8,128)} %get-tuple-element.37), calls=%async_computation.3 | async-start | bytes 1048576 | tf_op jit(solution)/shard_map/all_to_all | solution.py:207
  121.5 12.9 %all-to-all-start.4 = ((f32[32,24,128]{2,1,0:T(8,128)}), f32[32,24,128]{2,1,0:T(8,128)S(1)}, u32[]{:S(2)}, u32[]{:S(2)}) async-start(f32[32,24,128]{2,1,0:T(8,128)} %prefix.3), calls=%async_computation.4 | async-start | bytes 786432 | tf_op jit(solution)/shard_map/all_to_all | solution.py:215
  134.4 10.8 %copy-start.2 = (f32[1536]{0:T(1024)S(1)}, f32[1536]{0:T(1024)}, u32[]{:S(2)}) copy-start(f32[1536]{0:T(1024)} %param.29) | copy-start | bytes 18436
  139.0 6.2 %collective-permute-start.3 = (f32[1,1024]{1,0:T(1,128)S(1)}, f32[1,1024]{1,0:T(1,128)S(1)}, u32[]{:S(2)}, u32[]{:S(2)}) collective-permute-start(f32[1,1024]{1,0:T(1,128)S(1)} %get-tuple-element.48.refs_0_), channel_id=1, source_target_pairs={{0,1},{1,0},{2,3},{3,2},{4,5},{5,4},{6,7},{7,6},{8,9},{9,8},{10,11... | collective-permute-start | bytes 12296 | tf_op jit(solution)/shard_map/ppermute | solution.py:530
  142.0 4.0 %collective-permute-start.4 = (f32[1,1024]{1,0:T(1,128)S(1)}, f32[1,1024]{1,0:T(1,128)S(1)}, u32[]{:S(2)}, u32[]{:S(2)}) collective-permute-start(f32[1,1024]{1,0:T(1,128)S(1)} %get-tuple-element.48.refs_0_), channel_id=1, source_target_pairs={{0,2},{1,3},{2,0},{3,1},{4,6},{5,7},{6,4},{7,5},{8,10},{9,11},{10,... | collective-permute-start | bytes 12296 | tf_op jit(solution)/shard_map/ppermute | solution.py:530
  142.7 4.5 %collective-permute-start.5 = (f32[1,1024]{1,0:T(1,128)S(1)}, f32[1,1024]{1,0:T(1,128)S(1)}, u32[]{:S(2)}, u32[]{:S(2)}) collective-permute-start(f32[1,1024]{1,0:T(1,128)S(1)} %get-tuple-element.48.refs_0_), channel_id=1, source_target_pairs={{0,3},{1,2},{2,1},{3,0},{4,7},{5,6},{6,5},{7,4},{8,11},{9,10},{10,... | collective-permute-start | bytes 12296 | tf_op jit(solution)/shard_map/ppermute | solution.py:530

commit v7 on v6

--- a/solution.py
+++ b/solution.py
@@ -17,6 +17,7 @@
 EXTRA = 16
 CHUNK = 128
 PITCH = 40
+STATES_MB = 53
 LOG2E = 1.4426950408889634
 OWN_TYPE = jnp.float32
 FACTOR_TYPE = jnp.bfloat16
@@ -84,7 +85,7 @@
 
 def states_kernel(by_head, features, x_ref, write_hbm, step_hbm, decay_hbm, *refs):
     if by_head:
-        *squares_hbms, gain_hbm, payload_hbm, before_hbm, gain_ref, squares_ref, x_in, write_ref, step_ref, decay_ref, before, payload, total, sent, got = refs
+        *squares_hbms, gain_hbm, payload_hbm, before_hbm, gain_ref, squares_ref, write_ref, step_ref, decay_ref, before, payload, total, sent, got = refs
     else:
         payload_hbm, before_hbm, x_in, write_ref, step_ref, decay_ref, before, payload, total, sent, got = refs
     head_count = step_ref.shape[0]
@@ -106,8 +107,9 @@
 
     for copy in small:
         copy.start()
-    for block in range(blocks):
-        x_copy(block).start()
+    if not by_head:
+        for block in range(blocks):
+            x_copy(block).start()
     before[0] = jnp.zeros(before.shape[1:], F32)
     total[...] = jnp.zeros_like(total)
     for copy in small:
@@ -121,8 +123,12 @@
         weights = jnp.exp(final - cumulative) * step_ref[:, positions]
         if by_head:
             weights = weights * block_scale(squares_refs, block, features)
-        x_copy(block).wait()
-        x_block = x_in.at[block]
+        if by_head:
+            devices = x_ref.shape[0] // blocks
+            x_block = x_ref.at[pl.ds(pl.multiple_of(block * devices, devices), devices)]
+        else:
+            x_copy(block).wait()
+            x_block = x_in.at[block]
         fading = jnp.broadcast_to(jnp.exp(final), (head_count, LANES))
         write = write_ref[:, positions].astype(F32)
         for head in range(head_count):
@@ -157,14 +163,15 @@
     blocks = length // BLOCK
     height = head_count * state_size // devices
     by_head = squares is not None
-    specs = [HBM] * 4
+    specs = [VMEM if by_head else HBM] + [HBM] * 3
     operands = [x, write, step, decay]
     scratch = []
     if by_head:
         specs += [HBM] * (len(squares) + 1)
         operands += [*squares, gain]
         scratch += [pltpu.VMEM(gain.shape, F32), pltpu.VMEM((len(squares), *squares[0].shape), F32)]
-    scratch.append(pltpu.VMEM((blocks, x.shape[0] // blocks, *x.shape[1:]), BF16))
+    else:
+        scratch.append(pltpu.VMEM((blocks, x.shape[0] // blocks, *x.shape[1:]), BF16))
     return pl.pallas_call(
         functools.partial(states_kernel, by_head, features),
         in_specs=specs,
@@ -184,7 +191,7 @@
             pltpu.SemaphoreType.DMA((blocks + 1,)),
             pltpu.SemaphoreType.DMA((len(operands) + blocks,)),
         ],
-        compiler_params=params(),
+        compiler_params=params(STATES_MB if by_head else 56),
         cost_estimate=pl.CostEstimate(flops=500_000_000, bytes_accessed=6_000_000, transcendentals=20_000),
         name="states",
     )(*operands)

time: 150 us -> 153 us (1.020)
    unnamed x6 -> x16, local copies, waits for them, and re-layouts: 0.01 us -> 1.85 us
  transfers between devices with their start and end apart: 10 -> 10, of which waited for: 8 -> 8; matrix products, arithmetic and copies ran while one was open for 0% -> 0% of each run, Pallas kernels for 19% -> 18%
where the time goes in v7:
time: 153 us; the launch traced here: 152 us
  Pallas kernels  52.8 us (35%)
  blocking collectives  45.1 us (29%)
  starting transfers between devices  34.2 us (22%)
  waiting for transfers between devices  17.7 us (12%)
  local copies, waits for them, and re-layouts  1.93 us (1%)
    all_to_all x1, blocking collectives, body(): lax.all_to_all(hidden, SEQ, split_axis=0, concat_axis=0, tiled=True)  45.1 us
    pallas_call x4, Pallas kernels, local_factors(): pl.pallas_call(functools.partial(local_kernel, by_head, features, first,...  27.9 us
    all_to_all x2, starting transfers between devices, prior_states(): ends = lax.all_to_all(payload, SEQ, split_axis=0, concat_axis=0, tiled=True)  13.6 us
    ppermute x6, starting transfers between devices, over_head(): lax.ppermute(value, 'head', [(at, at ^ step) for at in range(devices)])  12.6 us
    pallas_call x2, Pallas kernels, gated_outputs(): pl.pallas_call(functools.partial(gated_kernel, first_layer), in_specs=[HB...  10.9 us
    pallas_call x2, Pallas kernels, device_states(): pl.pallas_call(functools.partial(states_kernel, by_head, features), in_sp...  10 us
    all_to_all x2, starting transfers between devices, prior_states(): prior = lax.all_to_all(prior, SEQ, split_axis=0, concat_axis=0, tiled=True)  7.99 us
    all_to_all x2, waiting for transfers between devices, prior_states(): ends = lax.all_to_all(payload, SEQ, split_axis=0, concat_axis=0, tiled=True)  7.99 us
  transfers between devices with their start and end apart: 10, of which 8 were waited for; matrix products, arithmetic and copies ran while one was open for 0% of the time, Pallas kernels for 18%

profile of v7, /device:TPU:1, one launch (start us, length us, event | category | flops | bytes accessed | tf_op | source)
XLA Modules:
  0.0 152.1 jit_solution(11233073117275409441)
XLA Ops:
  0.0 4.4 %states.2 = (f32[32,32,128]{2,1,0:T(8,128)}, f32[4,768,128]{2,1,0:T(8,128)}) custom-call(bf16[1024,1536]{1,0:T(8,128)(2,1)} %bitcast.8, bf16[64,1024]{1,0:T(8,128)(2,1)} %refs_1_.5, f32[12,1024]{1,0:T(8,128)} %refs_3_.5, f32[12,1024]{1,0:T(8,128)} %refs_4_.3), custom_call_target="tpu_custom_call" | custom-call | flops 500000000 | bytes 6000000 | tf_op jit(solution)/shard_map/states/pallas_call | solution.py:175
  4.4 9.7 %all-to-all-start = ((f32[32,32,128]{2,1,0:T(8,128)}), f32[32,32,128]{2,1,0:T(8,128)S(1)}, u32[]{:S(2)}, u32[]{:S(2)}) async-start(f32[32,32,128]{2,1,0:T(8,128)} %get-tuple-element.27), calls=%async_computation | async-start | bytes 1048576 | tf_op jit(solution)/shard_map/all_to_all | solution.py:214
  14.1 6.9 %local.4 = (f32[5,1024,384]{2,1,0:T(8,128)}, bf16[4,1024,384]{2,1,0:T(8,128)(2,1)}) custom-call(bf16[1024,1536]{1,0:T(8,128)(2,1)} %bitcast.9, bf16[64,1024]{1,0:T(8,128)(2,1)} %refs_1_.5, bf16[64,1024]{1,0:T(8,128)(2,1)} %refs_2_.5, f32[12,1024]{1,0:T(8,128)} %refs_3_.5, f32[12,1024]{1,0:T(8,128)} %refs_4_.3, bf16[1024,1536]{1,0:T(8,128)(2,1)} %bitcast.11, ...), custom_call_target="tpu_custom_call" | custom-call | flops 3000000000 | bytes 10000000 | tf_op jit(solution)/shard_map/local/pallas_call | solution.py:331
  21.0 3.8 %all-to-all-done.ends_ref = f32[32,32,128]{2,1,0:T(8,128)S(1)} async-done(((f32[32,32,128]{2,1,0:T(8,128)}), f32[32,32,128]{2,1,0:T(8,128)S(1)}, u32[]{:S(2)}, u32[]{:S(2)}) %all-to-all-start) | async-done | bytes 524320 | tf_op jit(solution)/shard_map/all_to_all | solution.py:214
  24.8 0.8 prefix.2
  25.7 3.9 %all-to-all-start.1 = ((f32[32,24,128]{2,1,0:T(8,128)}), f32[32,24,128]{2,1,0:T(8,128)S(1)}, u32[]{:S(2)}, u32[]{:S(2)}) async-start(f32[32,24,128]{2,1,0:T(8,128)} %prefix.2), calls=%async_computation.1 | async-start | bytes 786432 | tf_op jit(solution)/shard_map/all_to_all | solution.py:222
  29.6 7.0 %local.5 = (f32[5,1024,384]{2,1,0:T(8,128)}, bf16[4,1024,384]{2,1,0:T(8,128)(2,1)}) custom-call(bf16[1024,1536]{1,0:T(8,128)(2,1)} %bitcast.10, bf16[64,1024]{1,0:T(8,128)(2,1)} %refs_1_.5, bf16[64,1024]{1,0:T(8,128)(2,1)} %refs_2_.5, f32[12,1024]{1,0:T(8,128)} %refs_3_.5, f32[12,1024]{1,0:T(8,128)} %refs_4_.3, ...), custom_call_target="tpu_custom_call", output_to_operand_aliasing={{0}: (8, {}), {1}: (9, {})} | custom-call | flops 3000000000 | bytes 10000000 | tf_op jit(solution)/shard_map/local/pallas_call | solution.py:331
  36.6 2.0 %all-to-all-done.1 = f32[32,24,128]{2,1,0:T(8,128)S(1)} async-done(((f32[32,24,128]{2,1,0:T(8,128)}), f32[32,24,128]{2,1,0:T(8,128)S(1)}, u32[]{:S(2)}, u32[]{:S(2)}) %all-to-all-start.1) | async-done | bytes 393248 | tf_op jit(solution)/shard_map/all_to_all | solution.py:222
  38.6 6.2 %gated.2 = bf16[32,400,128]{2,1,0:T(8,128)(2,1)} custom-call(f32[5,1024,384]{2,1,0:T(8,128)} %get-tuple-element.34.own_hbm, bf16[4,1024,384]{2,1,0:T(8,128)(2,1)} %get-tuple-element.35.factor_hbm, f32[768,128]{1,0:T(8,128)S(1)} %bitcast.7), custom_call_target="tpu_custom_call" | custom-call | flops 1200000000 | bytes 13000000 | tf_op jit(solution)/shard_map/gated/pallas_call | solution.py:476
  44.9 0.0 copy-start.6
  44.9 0.0 copy-start
  44.9 0.0 copy-start.1
  44.9 0.0 copy-start.2
  44.9 45.1 %all_to_all.25.x_ref.refs_0_ = bf16[32,400,128]{2,1,0:T(8,128)(2,1)S(1)} all-to-all(bf16[32,400,128]{2,1,0:T(8,128)(2,1)} %gated.2), channel_id=1, replica_groups=mesh['seq_0'=4,'seq_1'=4,'seq_2'=2,'head'=4] {'seq_0','seq_1','seq_2'}, dimensions={0} | all-to-all | bytes 6553600 | tf_op jit(solution)/shard_map/all_to_all | solution.py:574
  90.0 0.0 copy-start.5
  90.0 1.8 %copy-done.5 = bf16[32,400,128]{2,1,0:T(8,128)(2,1)} copy-done((bf16[32,400,128]{2,1,0:T(8,128)(2,1)}, bf16[32,400,128]{2,1,0:T(8,128)(2,1)S(1)}, u32[]{:S(2)}) %copy-start.5) | copy-done | bytes 3276824
  91.8 0.1 fusion
  91.9 0.1 add.23
  92.0 3.2 %collective-permute-start = (f32[8,128]{1,0:T(8,128)S(1)}, f32[8,128]{1,0:T(8,128)S(1)}, u32[]{:S(2)}, u32[]{:S(2)}) collective-permute-start(f32[8,128]{1,0:T(8,128)S(1)} %add.23), channel_id=1, source_target_pairs={{0,1},{1,0},{2,3},{3,2},{4,5},{5,4},{6,7},{7,6},{8,9},{9,8},{10,11... | collective-permute-start | bytes 12296 | tf_op jit(solution)/shard_map/ppermute | solution.py:537
  95.2 2.6 %collective-permute-start.1 = (f32[8,128]{1,0:T(8,128)S(1)}, f32[8,128]{1,0:T(8,128)S(1)}, u32[]{:S(2)}, u32[]{:S(2)}) collective-permute-start(f32[8,128]{1,0:T(8,128)S(1)} %add.23), channel_id=1, source_target_pairs={{0,2},{1,3},{2,0},{3,1},{4,6},{5,7},{6,4},{7,5},{8,10},{9,11},{10,... | collective-permute-start | bytes 12296 | tf_op jit(solution)/shard_map/ppermute | solution.py:537
  97.8 0.6 collective-permute-start.2
  98.4 0.0 copy-done.6
  98.4 0.0 copy-start.3
  98.4 0.0 collective-permute-done
  98.4 0.7 collective-permute-done.1
  99.1 3.2 %collective-permute-done.2 = f32[8,128]{1,0:T(8,128)S(1)} collective-permute-done((f32[8,128]{1,0:T(8,128)S(1)}, f32[8,128]{1,0:T(8,128)S(1)}, u32[]{:S(2)}, u32[]{:S(2)}) %collective-permute-start.2) | collective-permute-done | bytes 4128 | tf_op jit(solution)/shard_map/ppermute | solution.py:537
  102.3 0.0 copy-done
  102.3 0.0 copy-done.1
  102.3 0.0 copy-done.2
  102.4 0.0 copy-start.4
  102.4 5.7 %states.3 = (f32[32,32,128]{2,1,0:T(8,128)}, f32[4,768,128]{2,1,0:T(8,128)}) custom-call(bf16[32,400,128]{2,1,0:T(8,128)(2,1)} %copy-done.5, bf16[64,1024]{1,0:T(8,128)(2,1)S(1)} %copy-done, f32[12,1024]{1,0:T(8,128)S(1)} %copy-done.1, f32[12,1024]{1,0:T(8,128)S(1)} %copy-done.2, f32[8,128]{1,0:T(8,128)S(1)} %add_add_fusion.refs_0_.refs_8_, ...), custom_call_target="tpu_custom_call" | custom-call | flops 500000000 | bytes 6000000 | tf_op jit(solution)/shard_map/states/pallas_call | solution.py:175
  108.0 3.9 %all-to-all-start.3 = ((f32[32,32,128]{2,1,0:T(8,128)}), f32[32,32,128]{2,1,0:T(8,128)S(1)}, u32[]{:S(2)}, u32[]{:S(2)}) async-start(f32[32,32,128]{2,1,0:T(8,128)} %get-tuple-element.37), calls=%async_computation.3 | async-start | bytes 1048576 | tf_op jit(solution)/shard_map/all_to_all | solution.py:214
  111.9 0.0 copy-done.3
  111.9 0.0 copy-done.4
  112.0 6.9 %local.6 = (f32[5,1024,384]{2,1,0:T(8,128)}, bf16[4,1024,384]{2,1,0:T(8,128)(2,1)}) custom-call(bf16[32,400,128]{2,1,0:T(8,128)(2,1)} %copy-done.5, bf16[64,1024]{1,0:T(8,128)(2,1)} %refs_1_.7, bf16[64,1024]{1,0:T(8,128)(2,1)} %refs_2_.7, f32[12,1024]{1,0:T(8,128)} %refs_3_.7, f32[12,1024]{1,0:T(8,128)} %refs_4_.5, bf16[1024,1536]{1,0:T(8,128)(2,1)} %bitcast.13, ...), custom_call_target="tpu_custom_call" | custom-call | flops 3000000000 | bytes 10000000 | tf_op jit(solution)/shard_map/local/pallas_call | solution.py:331
  118.9 4.2 %all-to-all-done.3.ends_ref = f32[32,32,128]{2,1,0:T(8,128)S(1)} async-done(((f32[32,32,128]{2,1,0:T(8,128)}), f32[32,32,128]{2,1,0:T(8,128)S(1)}, u32[]{:S(2)}, u32[]{:S(2)}) %all-to-all-start.3) | async-done | bytes 524320 | tf_op jit(solution)/shard_map/all_to_all | solution.py:214
  123.1 0.9 prefix.3
  123.9 4.1 %all-to-all-start.4 = ((f32[32,24,128]{2,1,0:T(8,128)}), f32[32,24,128]{2,1,0:T(8,128)S(1)}, u32[]{:S(2)}, u32[]{:S(2)}) async-start(f32[32,24,128]{2,1,0:T(8,128)} %prefix.3), calls=%async_computation.4 | async-start | bytes 786432 | tf_op jit(solution)/shard_map/all_to_all | solution.py:222
  128.0 7.0 %local.7 = (f32[5,1024,384]{2,1,0:T(8,128)}, bf16[4,1024,384]{2,1,0:T(8,128)(2,1)}) custom-call(bf16[32,400,128]{2,1,0:T(8,128)(2,1)} %copy-done.5, bf16[64,1024]{1,0:T(8,128)(2,1)} %refs_1_.7, bf16[64,1024]{1,0:T(8,128)(2,1)} %refs_2_.7, f32[12,1024]{1,0:T(8,128)} %refs_3_.7, f32[12,1024]{1,0:T(8,128)} %refs_4_.5, ...), custom_call_target="tpu_custom_call", output_to_operand_aliasing={{0}: (10, {}), {1}: (11, {})} | custom-call | flops 3000000000 | bytes 10000000 | tf_op jit(solution)/shard_map/local/pallas_call | solution.py:331
  135.0 1.8 %all-to-all-done.4 = f32[32,24,128]{2,1,0:T(8,128)S(1)} async-done(((f32[32,24,128]{2,1,0:T(8,128)}), f32[32,24,128]{2,1,0:T(8,128)S(1)}, u32[]{:S(2)}, u32[]{:S(2)}) %all-to-all-start.4) | async-done | bytes 393248 | tf_op jit(solution)/shard_map/all_to_all | solution.py:222
  136.9 0.0 copy-start.7
  136.9 4.7 %gated.3 = (bf16[4,1024,384]{2,1,0:T(8,128)(2,1)S(1)}, f32[1,1024]{1,0:T(1,128)S(1)}) custom-call(f32[5,1024,384]{2,1,0:T(8,128)} %get-tuple-element.44.own_hbm, bf16[4,1024,384]{2,1,0:T(8,128)(2,1)} %get-tuple-element.45.factor_hbm, f32[768,128]{1,0:T(8,128)S(1)} %bitcast.6), custom_call_target="tpu_custom_call" | custom-call | flops 1200000000 | bytes 13000000 | tf_op jit(solution)/shard_map/gated/pallas_call | solution.py:476
  141.5 2.9 %collective-permute-start.3 = (f32[1,1024]{1,0:T(1,128)S(1)}, f32[1,1024]{1,0:T(1,128)S(1)}, u32[]{:S(2)}, u32[]{:S(2)}) collective-permute-start(f32[1,1024]{1,0:T(1,128)S(1)} %get-tuple-element.48.refs_0_), channel_id=1, source_target_pairs={{0,1},{1,0},{2,3},{3,2},{4,5},{5,4},{6,7},{7,6},{8,9},{9,8},{10,11... | collective-permute-start | bytes 12296 | tf_op jit(solution)/shard_map/ppermute | solution.py:537
  144.5 0.7 collective-permute-start.4
  145.1 2.5 %collective-permute-start.5 = (f32[1,1024]{1,0:T(1,128)S(1)}, f32[1,1024]{1,0:T(1,128)S(1)}, u32[]{:S(2)}, u32[]{:S(2)}) collective-permute-start(f32[1,1024]{1,0:T(1,128)S(1)} %get-tuple-element.48.refs_0_), channel_id=1, source_target_pairs={{0,3},{1,2},{2,1},{3,0},{4,7},{5,6},{6,5},{7,4},{8,11},{9,10},{10,... | collective-permute-start | bytes 12296 | tf_op jit(solution)/shard_map/ppermute | solution.py:537
  147.7 0.0 copy-done.7
  147.7 0.0 collective-permute-done.3.refs_1_
  147.7 0.7 collective-permute-done.4.refs_2_
  148.4 1.2 collective-permute-done.5.refs_3_
  149.7 2.3 %scaled.1 = bf16[1024,1536]{1,0:T(8,128)(2,1)} custom-call(bf16[4,1024,384]{2,1,0:T(8,128)(2,1)S(1)} %get-tuple-element.47.gated_ref, f32[1,1536]{1,0:T(1,128)S(1)} %broadcast_in_dim.7.gain_ref, f32[1,1024]{1,0:T(1,128)S(1)} %get-tuple-element.48.refs_0_, f32[1,1024]{1,0:T(1,128)S(1)} %collective-permute-done.3.refs_1_, ...), custom_call_target="tpu_custom_call" | custom-call | tf_op jit(solution)/shard_map/scaled/pallas_call | solution.py:520
  (4 shorter events, 0.0 us)
Async XLA Ops:
  4.4 20.4 %all-to-all-start = ((f32[32,32,128]{2,1,0:T(8,128)}), f32[32,32,128]{2,1,0:T(8,128)S(1)}, u32[]{:S(2)}, u32[]{:S(2)}) async-start(f32[32,32,128]{2,1,0:T(8,128)} %get-tuple-element.27), calls=%async_computation | async-start | bytes 1048576 | tf_op jit(solution)/shard_map/all_to_all | solution.py:214
  25.7 13.0 %all-to-all-start.1 = ((f32[32,24,128]{2,1,0:T(8,128)}), f32[32,24,128]{2,1,0:T(8,128)S(1)}, u32[]{:S(2)}, u32[]{:S(2)}) async-start(f32[32,24,128]{2,1,0:T(8,128)} %prefix.2), calls=%async_computation.1 | async-start | bytes 786432 | tf_op jit(solution)/shard_map/all_to_all | solution.py:222
  44.9 53.5 %copy-start.6 = (f32[1536]{0:T(1024)S(1)}, f32[1536]{0:T(1024)}, u32[]{:S(2)}) copy-start(f32[1536]{0:T(1024)} %param.23) | copy-start | bytes 18436
  44.9 57.5 %copy-start = (bf16[64,1024]{1,0:T(8,128)(2,1)S(1)}, bf16[64,1024]{1,0:T(8,128)(2,1)}, u32[]{:S(2)}) copy-start(bf16[64,1024]{1,0:T(8,128)(2,1)} %refs_1_.7) | copy-start | bytes 393220
  44.9 57.5 %copy-start.1 = (f32[12,1024]{1,0:T(8,128)S(1)}, f32[12,1024]{1,0:T(8,128)}, u32[]{:S(2)}) copy-start(f32[12,1024]{1,0:T(8,128)} %refs_3_.7) | copy-start | bytes 147460
  44.9 57.4 %copy-start.2 = (f32[12,1024]{1,0:T(8,128)S(1)}, f32[12,1024]{1,0:T(8,128)}, u32[]{:S(2)}) copy-start(f32[12,1024]{1,0:T(8,128)} %refs_4_.5) | copy-start | bytes 147460
  90.0 1.8 %copy-start.5 = (bf16[32,400,128]{2,1,0:T(8,128)(2,1)}, bf16[32,400,128]{2,1,0:T(8,128)(2,1)S(1)}, u32[]{:S(2)}) copy-start(bf16[32,400,128]{2,1,0:T(8,128)(2,1)S(1)} %all_to_all.25.x_ref.refs_0_) | copy-start | bytes 9830404
  92.0 6.5 %collective-permute-start = (f32[8,128]{1,0:T(8,128)S(1)}, f32[8,128]{1,0:T(8,128)S(1)}, u32[]{:S(2)}, u32[]{:S(2)}) collective-permute-start(f32[8,128]{1,0:T(8,128)S(1)} %add.23), channel_id=1, source_target_pairs={{0,1},{1,0},{2,3},{3,2},{4,5},{5,4},{6,7},{7,6},{8,9},{9,8},{10,11... | collective-permute-start | bytes 12296 | tf_op jit(solution)/shard_map/ppermute | solution.py:537
  95.2 4.0 %collective-permute-start.1 = (f32[8,128]{1,0:T(8,128)S(1)}, f32[8,128]{1,0:T(8,128)S(1)}, u32[]{:S(2)}, u32[]{:S(2)}) collective-permute-start(f32[8,128]{1,0:T(8,128)S(1)} %add.23), channel_id=1, source_target_pairs={{0,2},{1,3},{2,0},{3,1},{4,6},{5,7},{6,4},{7,5},{8,10},{9,11},{10,... | collective-permute-start | bytes 12296 | tf_op jit(solution)/shard_map/ppermute | solution.py:537
  97.8 4.5 %collective-permute-start.2 = (f32[8,128]{1,0:T(8,128)S(1)}, f32[8,128]{1,0:T(8,128)S(1)}, u32[]{:S(2)}, u32[]{:S(2)}) collective-permute-start(f32[8,128]{1,0:T(8,128)S(1)} %add.23), channel_id=1, source_target_pairs={{0,3},{1,2},{2,1},{3,0},{4,7},{5,6},{6,5},{7,4},{8,11},{9,10},{10,... | collective-permute-start | bytes 12296 | tf_op jit(solution)/shard_map/ppermute | solution.py:537
  98.4 13.5 %copy-start.3 = (f32[1,1536]{1,0:T(1,128)}, f32[1,1536]{1,0:T(1,128)S(1)}, u32[]{:S(2)}) copy-start(f32[1,1536]{1,0:T(1,128)S(1)} %broadcast_in_dim.6.refs_1_.refs_9_) | copy-start | bytes 18436
  102.4 9.6 %copy-start.4 = (f32[8,128]{1,0:T(8,128)}, f32[8,128]{1,0:T(8,128)S(1)}, u32[]{:S(2)}) copy-start(f32[8,128]{1,0:T(8,128)S(1)} %add_add_fusion.refs_0_.refs_8_) | copy-start | bytes 12292
  108.0 15.1 %all-to-all-start.3 = ((f32[32,32,128]{2,1,0:T(8,128)}), f32[32,32,128]{2,1,0:T(8,128)S(1)}, u32[]{:S(2)}, u32[]{:S(2)}) async-start(f32[32,32,128]{2,1,0:T(8,128)} %get-tuple-element.37), calls=%async_computation.3 | async-start | bytes 1048576 | tf_op jit(solution)/shard_map/all_to_all | solution.py:214
  123.9 12.9 %all-to-all-start.4 = ((f32[32,24,128]{2,1,0:T(8,128)}), f32[32,24,128]{2,1,0:T(8,128)S(1)}, u32[]{:S(2)}, u32[]{:S(2)}) async-start(f32[32,24,128]{2,1,0:T(8,128)} %prefix.3), calls=%async_computation.4 | async-start | bytes 786432 | tf_op jit(solution)/shard_map/all_to_all | solution.py:222
  136.9 10.8 %copy-start.7 = (f32[1536]{0:T(1024)S(1)}, f32[1536]{0:T(1024)}, u32[]{:S(2)}) copy-start(f32[1536]{0:T(1024)} %param.29) | copy-start | bytes 18436
  141.5 6.2 %collective-permute-start.3 = (f32[1,1024]{1,0:T(1,128)S(1)}, f32[1,1024]{1,0:T(1,128)S(1)}, u32[]{:S(2)}, u32[]{:S(2)}) collective-permute-start(f32[1,1024]{1,0:T(1,128)S(1)} %get-tuple-element.48.refs_0_), channel_id=1, source_target_pairs={{0,1},{1,0},{2,3},{3,2},{4,5},{5,4},{6,7},{7,6},{8,9},{9,8},{10,11... | collective-permute-start | bytes 12296 | tf_op jit(solution)/shard_map/ppermute | solution.py:537
  144.5 4.0 %collective-permute-start.4 = (f32[1,1024]{1,0:T(1,128)S(1)}, f32[1,1024]{1,0:T(1,128)S(1)}, u32[]{:S(2)}, u32[]{:S(2)}) collective-permute-start(f32[1,1024]{1,0:T(1,128)S(1)} %get-tuple-element.48.refs_0_), channel_id=1, source_target_pairs={{0,2},{1,3},{2,0},{3,1},{4,6},{5,7},{6,4},{7,5},{8,10},{9,11},{10,... | collective-permute-start | bytes 12296 | tf_op jit(solution)/shard_map/ppermute | solution.py:537
  145.1 4.5 %collective-permute-start.5 = (f32[1,1024]{1,0:T(1,128)S(1)}, f32[1,1024]{1,0:T(1,128)S(1)}, u32[]{:S(2)}, u32[]{:S(2)}) collective-permute-start(f32[1,1024]{1,0:T(1,128)S(1)} %get-tuple-element.48.refs_0_), channel_id=1, source_target_pairs={{0,3},{1,2},{2,1},{3,0},{4,7},{5,6},{6,5},{7,4},{8,11},{9,10},{10,... | collective-permute-start | bytes 12296 | tf_op jit(solution)/shard_map/ppermute | solution.py:537
